TPU v7x, 32 devices: a whole 2x2x4 slice. The times are simulated.
32 devices in a mesh: ctx: 4 (over x, core), fsdp: 8 (over z, y).
Axes of the slice: x: 2, y: 2, z: 4, core: 2. Of those that a mesh axis runs over, the one named last changes fastest.
Arguments:
- tokens: bfloat16 [64, 512, 1024], P('fsdp', 'ctx'), may hold values from -8 to 8
- cotangent: bfloat16 [64, 512, 1024], P('fsdp', 'ctx'), may hold values from -8 to 8
- input_weight: bfloat16 [1024, 3072], P('fsdp'), may hold values from -0.25 to 0.25
- output_weight: bfloat16 [1024, 1024], P('fsdp'), may hold values from -1.5 to 1.5
- up_weight: bfloat16 [1024, 4096], P('fsdp'), may hold values from -0.1875 to 0.1875
- down_weight: bfloat16 [4096, 1024], P('fsdp'), may hold values from -0.125 to 0.125
- query_bias: bfloat16 [1024], P('fsdp'), may hold values from -3 to 3
- value_bias: bfloat16 [1024], P('fsdp'), may hold values from -3 to 3
- output_bias: bfloat16 [1024], P('fsdp'), may hold values from -3 to 3
- norm_gain: bfloat16 [1024], P('fsdp'), may hold values from 0.25 to 1.75
- norm_shift: bfloat16 [1024], P('fsdp'), may hold values from -1.75 to 1.75
- up_bias: bfloat16 [4096], P('fsdp'), may hold values from -3 to 3
- down_bias: bfloat16 [1024], P('fsdp'), may hold values from -1.75 to 1.75
- final_gain: bfloat16 [1024], P('fsdp'), may hold values from 0.25 to 1.75
- final_shift: bfloat16 [1024], P('fsdp'), may hold values from -1.75 to 1.75
Outputs:
- layer_out: bfloat16 [64, 512, 1024], P('fsdp', 'ctx')
- tokens_grad: bfloat16 [64, 512, 1024], P('fsdp', 'ctx')
- input_weight_grad: float32 [1024, 3072], P('fsdp')
- output_weight_grad: float32 [1024, 1024], P('fsdp')
- up_weight_grad: float32 [1024, 4096], P('fsdp')
- down_weight_grad: float32 [4096, 1024], P('fsdp')
- query_bias_grad: float32 [1024], P('fsdp')
- value_bias_grad: float32 [1024], P('fsdp')
- output_bias_grad: float32 [1024], P('fsdp')
- norm_gain_grad: float32 [1024], P('fsdp')
- norm_shift_grad: float32 [1024], P('fsdp')
- up_bias_grad: float32 [4096], P('fsdp')
- down_bias_grad: float32 [1024], P('fsdp')
- final_gain_grad: float32 [1024], P('fsdp')
- final_shift_grad: float32 [1024], P('fsdp')
All inputs are finite; a program needn't handle non-finite values.
Results may differ from a plain program's by a relative error of at most 0.019.
The roundings to bfloat16 on the way count: a program that leaves them out, or rounds other values in their place, can miss the bound.
Values may be sent and summed in bfloat16 or wider, within the bound.
No kernel may reach another device: no remote copies, remote signals or barrier semaphores. Data moves between devices by JAX's collectives and lax.ppermute only.
A program may use at most 256 MiB of HBM per device.

v0:
```python
import math

import jax
import jax.numpy as jnp
from jax import lax
from jax.sharding import PartitionSpec as P

H = 16


epsilon = 1e-05


def for_sending(value):
    return jax.tree.map(lambda a: a.astype(jnp.bfloat16) if a.dtype == jnp.float32 else a, value)


def norm_forward(values):
    centre = values - jnp.mean(values, axis=-1, keepdims=True)
    inverse = lax.rsqrt(jnp.mean(centre * centre, axis=-1, keepdims=True) + epsilon)
    return (centre * inverse, inverse)


def norm_backward(upstream, normed, inverse, gain):
    scaled = upstream * gain
    return inverse * (
        scaled
        - jnp.mean(scaled, axis=-1, keepdims=True)
        - normed * jnp.mean(scaled * normed, axis=-1, keepdims=True)
    )


def gelu_exact(values):
    return jax.nn.gelu(values, approximate=False)


def attend_forward(blocks):
    query, key_rows, value_rows = blocks
    factor = 1.0 / math.sqrt(query.shape[-1])
    scores = (
        jnp.einsum("sqhd,skhd->shqk", query, key_rows, preferred_element_type=jnp.float32) * factor
    )
    row_max = jnp.max(scores, axis=-1, keepdims=True)
    exponent = jnp.exp(scores - row_max)
    totals = jnp.sum(exponent, axis=-1, keepdims=True)
    probs = (exponent / totals).astype(jnp.bfloat16)
    context = jnp.einsum("shqk,skhd->sqhd", probs, value_rows, preferred_element_type=jnp.float32)
    return (context.astype(jnp.bfloat16), row_max + jnp.log(totals))


def attend_backward(blocks):
    query, key_rows, value_rows, d_context, log_total = blocks
    factor = 1.0 / math.sqrt(query.shape[-1])
    scores = (
        jnp.einsum("sqhd,skhd->shqk", query, key_rows, preferred_element_type=jnp.float32) * factor
    )
    probs = jnp.exp(scores - log_total)
    d_probs = jnp.einsum(
        "sqhd,skhd->shqk", d_context, value_rows, preferred_element_type=jnp.float32
    )
    centre = jnp.sum(probs * d_probs, axis=-1, keepdims=True)
    d_scores = (probs * (d_probs - centre)).astype(jnp.bfloat16)
    d_query = (
        jnp.einsum("shqk,skhd->sqhd", d_scores, key_rows, preferred_element_type=jnp.float32)
        * factor
    ).astype(jnp.bfloat16)
    d_keys = (
        jnp.einsum("shqk,sqhd->skhd", d_scores, query, preferred_element_type=jnp.float32) * factor
    )
    d_values = jnp.einsum(
        "shqk,sqhd->skhd", probs.astype(jnp.bfloat16), d_context, preferred_element_type=jnp.float32
    )
    return (d_query, d_keys, d_values)


def in_blocks(array, group):
    return array.reshape((array.shape[0] // group, group) + array.shape[1:])


def local(
    tokens,
    cotangent,
    input_weight,
    output_weight,
    up_weight,
    down_weight,
    query_bias,
    value_bias,
    output_bias,
    norm_gain,
    norm_shift,
    up_bias,
    down_bias,
    final_gain,
    final_shift,
):
    shards = (
        input_weight,
        output_weight,
        up_weight,
        down_weight,
        query_bias,
        value_bias,
        output_bias,
        norm_gain,
        norm_shift,
        up_bias,
        down_bias,
        final_gain,
        final_shift,
    )
    whole = (
        lax.all_gather(shards[0], "fsdp", axis=0, tiled=True),
        lax.all_gather(shards[1], "fsdp", axis=0, tiled=True),
        lax.all_gather(shards[2], "fsdp", axis=0, tiled=True),
        lax.all_gather(shards[3], "fsdp", axis=0, tiled=True),
        lax.all_gather(shards[4], "fsdp", axis=0, tiled=True),
        lax.all_gather(shards[5], "fsdp", axis=0, tiled=True),
        lax.all_gather(shards[6], "fsdp", axis=0, tiled=True),
        lax.all_gather(shards[7], "fsdp", axis=0, tiled=True),
        lax.all_gather(shards[8], "fsdp", axis=0, tiled=True),
        lax.all_gather(shards[9], "fsdp", axis=0, tiled=True),
        lax.all_gather(shards[10], "fsdp", axis=0, tiled=True),
        lax.all_gather(shards[11], "fsdp", axis=0, tiled=True),
        lax.all_gather(shards[12], "fsdp", axis=0, tiled=True),
    )
    wide_input, wide_output, wide_up, wide_down = (whole[0], whole[1], whole[2], whole[3])
    vectors = [member.astype(jnp.float32) for member in whole[4:]]
    (
        full_qbias,
        full_vbias,
        full_obias,
        full_ngain,
        full_nshift,
        full_ubias,
        full_dbias,
        full_fgain,
        full_fshift,
    ) = vectors
    seqs, local_len, width = tokens.shape
    length = local_len * lax.axis_size("ctx")
    rows_all = seqs * local_len
    head_size = width // H
    group = math.gcd(seqs, max(1, 512 // local_len))
    tok_rows = tokens.reshape(rows_all, width)
    merged = jnp.dot(tok_rows, wide_input, preferred_element_type=jnp.float32)
    query = (merged[:, :width] + full_qbias).astype(jnp.bfloat16)
    key_rows = merged[:, width : 2 * width].astype(jnp.bfloat16)
    value_rows = (merged[:, 2 * width :] + full_vbias).astype(jnp.bfloat16)
    all_keys, all_values = (
        lax.all_gather(key_rows.reshape(seqs, local_len, width), "ctx", axis=1, tiled=True),
        lax.all_gather(value_rows.reshape(seqs, local_len, width), "ctx", axis=1, tiled=True),
    )
    head_query = in_blocks(query.reshape(seqs, local_len, H, head_size), group)
    head_keys = in_blocks(all_keys.reshape(seqs, length, H, head_size), group)
    head_values = in_blocks(all_values.reshape(seqs, length, H, head_size), group)
    context, log_total = lax.map(attend_forward, (head_query, head_keys, head_values))
    context_rows = context.reshape(rows_all, width)
    pre_one = (
        tok_rows.astype(jnp.float32)
        + jnp.dot(context_rows, wide_output, preferred_element_type=jnp.float32)
        + full_obias
    )
    normed_one, inverse_one = norm_forward(pre_one)
    hidden = normed_one * full_ngain + full_nshift
    hidden_low = hidden.astype(jnp.bfloat16)
    inner = jnp.dot(hidden_low, wide_up, preferred_element_type=jnp.float32) + full_ubias
    active_full, gelu_pull = jax.vjp(gelu_exact, inner)
    active = active_full.astype(jnp.bfloat16)
    pre_two = hidden + jnp.dot(active, wide_down, preferred_element_type=jnp.float32) + full_dbias
    normed_two, inverse_two = norm_forward(pre_two)
    layer_out = (normed_two * full_fgain + full_fshift).astype(jnp.bfloat16).reshape(tokens.shape)
    again = (
        lax.all_gather(shards[0], "fsdp", axis=0, tiled=True),
        lax.all_gather(shards[1], "fsdp", axis=0, tiled=True),
        lax.all_gather(shards[2], "fsdp", axis=0, tiled=True),
        lax.all_gather(shards[3], "fsdp", axis=0, tiled=True),
        lax.all_gather(shards[4], "fsdp", axis=0, tiled=True),
        lax.all_gather(shards[5], "fsdp", axis=0, tiled=True),
        lax.all_gather(shards[6], "fsdp", axis=0, tiled=True),
        lax.all_gather(shards[7], "fsdp", axis=0, tiled=True),
        lax.all_gather(shards[8], "fsdp", axis=0, tiled=True),
        lax.all_gather(shards[9], "fsdp", axis=0, tiled=True),
        lax.all_gather(shards[10], "fsdp", axis=0, tiled=True),
        lax.all_gather(shards[11], "fsdp", axis=0, tiled=True),
        lax.all_gather(shards[12], "fsdp", axis=0, tiled=True),
    )
    back_input, back_output, back_up, back_down = (again[0], again[1], again[2], again[3])
    back_ngain = again[7].astype(jnp.float32)
    back_fgain = again[11].astype(jnp.float32)
    upstream = cotangent.reshape(rows_all, width).astype(jnp.float32)
    final_gain_grad = jnp.sum(upstream * normed_two, axis=0)
    final_shift_grad = jnp.sum(upstream, axis=0)
    d_pre_two = norm_backward(upstream, normed_two, inverse_two, back_fgain)
    d_branch = d_pre_two.astype(jnp.bfloat16)
    down_bias_grad = jnp.sum(d_pre_two, axis=0)
    down_weight_grad = jnp.einsum("nf,nd->fd", active, d_branch, preferred_element_type=jnp.float32)
    d_active = jnp.einsum("nd,fd->nf", d_branch, back_down, preferred_element_type=jnp.float32)
    d_inner = gelu_pull(d_active)[0].astype(jnp.bfloat16)
    up_bias_grad = jnp.sum(d_inner.astype(jnp.float32), axis=0)
    up_weight_grad = jnp.einsum(
        "nd,nf->df", hidden_low, d_inner, preferred_element_type=jnp.float32
    )
    d_hidden = d_pre_two + jnp.einsum(
        "nf,df->nd", d_inner, back_up, preferred_element_type=jnp.float32
    )
    norm_gain_grad = jnp.sum(d_hidden * normed_one, axis=0)
    norm_shift_grad = jnp.sum(d_hidden, axis=0)
    d_pre_one = norm_backward(d_hidden, normed_one, inverse_one, back_ngain)
    d_attn = d_pre_one.astype(jnp.bfloat16)
    output_bias_grad = jnp.sum(d_pre_one, axis=0)
    output_weight_grad = jnp.einsum(
        "nc,nd->cd", context_rows, d_attn, preferred_element_type=jnp.float32
    )
    d_context = jnp.einsum(
        "nd,cd->nc", d_attn, back_output, preferred_element_type=jnp.float32
    ).astype(jnp.bfloat16)
    head_dctx = in_blocks(d_context.reshape(seqs, local_len, H, head_size), group)
    d_query, d_keys, d_values = lax.map(
        attend_backward, (head_query, head_keys, head_values, head_dctx, log_total)
    )
    own_keys, own_values = (
        lax.psum_scatter(
            d_keys.reshape(seqs, length, width).astype(jnp.bfloat16),
            "ctx",
            scatter_dimension=1,
            tiled=True,
        ).astype(jnp.float32),
        lax.psum_scatter(
            d_values.reshape(seqs, length, width).astype(jnp.bfloat16),
            "ctx",
            scatter_dimension=1,
            tiled=True,
        ).astype(jnp.float32),
    )
    query_grad_rows = d_query.reshape(rows_all, width)
    value_grad_rows = own_values.reshape(rows_all, width).astype(jnp.bfloat16)
    d_merged = jnp.concatenate(
        [query_grad_rows, own_keys.reshape(rows_all, width).astype(jnp.bfloat16), value_grad_rows],
        axis=1,
    )
    query_bias_grad = jnp.sum(query_grad_rows.astype(jnp.float32), axis=0)
    value_bias_grad = jnp.sum(value_grad_rows.astype(jnp.float32), axis=0)
    input_weight_grad = jnp.einsum(
        "nd,ne->de", tok_rows, d_merged, preferred_element_type=jnp.float32
    )
    tokens_grad = (
        d_pre_one
        + jnp.einsum("ne,de->nd", d_merged, back_input, preferred_element_type=jnp.float32)
    ).astype(jnp.bfloat16)
    tokens_grad = tokens_grad.reshape(tokens.shape)
    grads = (
        lax.psum_scatter(input_weight_grad, "fsdp", scatter_dimension=0, tiled=True),
        lax.psum_scatter(output_weight_grad, "fsdp", scatter_dimension=0, tiled=True),
        lax.psum_scatter(up_weight_grad, "fsdp", scatter_dimension=0, tiled=True),
        lax.psum_scatter(down_weight_grad, "fsdp", scatter_dimension=0, tiled=True),
        lax.psum_scatter(query_bias_grad, "fsdp", scatter_dimension=0, tiled=True),
        lax.psum_scatter(value_bias_grad, "fsdp", scatter_dimension=0, tiled=True),
        lax.psum_scatter(output_bias_grad, "fsdp", scatter_dimension=0, tiled=True),
        lax.psum_scatter(norm_gain_grad, "fsdp", scatter_dimension=0, tiled=True),
        lax.psum_scatter(norm_shift_grad, "fsdp", scatter_dimension=0, tiled=True),
        lax.psum_scatter(up_bias_grad, "fsdp", scatter_dimension=0, tiled=True),
        lax.psum_scatter(down_bias_grad, "fsdp", scatter_dimension=0, tiled=True),
        lax.psum_scatter(final_gain_grad, "fsdp", scatter_dimension=0, tiled=True),
        lax.psum_scatter(final_shift_grad, "fsdp", scatter_dimension=0, tiled=True),
    )
    grads = tuple(
        jax.tree.map(
            lambda part: part.astype(jnp.float32), lax.psum(for_sending(tuple(grads)), "ctx")
        )
    )
    return (layer_out, tokens_grad) + tuple(grads)


def solution(mesh):
    return jax.shard_map(
        local,
        mesh=mesh,
        in_specs=(
            P("fsdp", "ctx", None),
            P("fsdp", "ctx", None),
            P("fsdp", None),
            P("fsdp", None),
            P("fsdp", None),
            P("fsdp", None),
            P("fsdp"),
            P("fsdp"),
            P("fsdp"),
            P("fsdp"),
            P("fsdp"),
            P("fsdp"),
            P("fsdp"),
            P("fsdp"),
            P("fsdp"),
        ),
        out_specs=(
            P("fsdp", "ctx", None),
            P("fsdp", "ctx", None),
            P("fsdp", None),
            P("fsdp", None),
            P("fsdp", None),
            P("fsdp", None),
            P("fsdp"),
            P("fsdp"),
            P("fsdp"),
            P("fsdp"),
            P("fsdp"),
            P("fsdp"),
            P("fsdp"),
            P("fsdp"),
            P("fsdp"),
        ),
        check_vma=False,
    )
```

profile of v0, /device:TPU:0, one launch (start us, length us, event | category | flops | bytes accessed | tf_op | source)
XLA Modules:
  0.0 1874.8 jit_solution(1731667253623744546)
XLA Ops:
  8.0 22.5 %all-gather = bf16[8,1,128]{2,1,0:T(2,128)(2,1)S(1)} all-gather(bf16[1,1,128]{2,1,0:T(2,128)(2,1)} %bitcast.226), channel_id=1, replica_groups=mesh['ctx'=4,'fsdp'=8] {'fsdp'}, dimensions={0}, use_global_device_ids=true | all-gather | bytes 2304 | tf_op jit(solution)/shard_map/all_gather | solution.py:118
  30.5 16.7 all-gather.1
  47.2 64.8 %all-gather.16.cloned.1.call-done = bf16[1024,3072]{1,0:T(8,128)(2,1)} async-done(((bf16[128,3072]{1,0:T(8,128)(2,1)}), bf16[1024,3072]{1,0:T(8,128)(2,1)}) %all-gather.16.cloned.1.call-update) | async-done | bytes 6291472 | tf_op jit(solution)/shard_map/all_gather | solution.py:113
  112.0 9.4 fusion.94
  127.8 4.0 slice.23
  133.7 17.6 all-gather.2
  151.9 16.7 all-gather.3
  169.2 17.6 all-gather.4
  187.4 26.0 %all-gather.5 = bf16[8,1,512]{2,1,0:T(2,128)(2,1)S(1)} all-gather(bf16[1,1,512]{2,1,0:T(2,128)(2,1)S(1)} %reshape.164), channel_id=1, replica_groups=mesh['ctx'=4,'fsdp'=8] {'fsdp'}, dimensions={0}, use_global_device_ids=true | all-gather | bytes 9216 | tf_op jit(solution)/shard_map/all_gather | solution.py:122
  214.0 16.1 all-gather.6
  230.7 18.2 all-gather.7
  250.9 16.4 all-gather.8
  267.9 6.5 reshape.195
  274.4 4.9 copy.67
  279.3 11.4 copy.64
  290.7 11.4 copy.66
  302.2 38.9 %while.26 = (s32[]{:T(128)}, bf16[2,4,128,16,64]{2,1,0,4,3:T(4,128)(2,1)}, f32[2,4,16,128,1]{3,2,1,4,0:T(8,128)S(1)}, bf16[2,4,512,16,64]{2,4,3,1,0:T(8,128)(2,1...) while((s32[]{:T(128)}, ...), condition=%wide.region_3.4_spmd, body=%wide.region_0.3_spmd.sunk | while | flops 1112006656 | bytes 63178832 | solution.py:157
  302.2 5.0 multiply_reduce_fusion.9
  307.2 4.1 fusion.127
  311.3 7.3 fusion.128
  321.7 4.8 multiply_reduce_fusion.9
  326.5 4.1 fusion.127
  330.7 7.3 fusion.128
  341.0 4.8 reshape.149
  345.8 6.2 fusion.92
  354.6 67.0 %all-gather.24.cloned.1.call-done = bf16[1024,4096]{1,0:T(8,128)(2,1)} async-done(((bf16[128,4096]{1,0:T(8,128)(2,1)}), bf16[1024,4096]{1,0:T(8,128)(2,1)}) %all-gather.24.cloned.1.call-update) | async-done | bytes 8388624 | tf_op jit(solution)/shard_map/all_gather | solution.py:115
  421.7 51.3 %multiply_convert_fusion.2 = (bf16[1024,4096]{1,0:T(8,128)(2,1)}, f32[1024,4096]{1,0:T(8,128)}, f32[1024,4096]{1,0:T(8,128)}) fusion(f32[4096]{0:T(1024)S(1)} %bitcast.219, bf16[1024,4096]{1,0:T(8,128)(2,1)} %all-gather.24.cloned.1.call-done, f32[1024,1024]{1,0:T(8,128)} %copy-done.5, f32[1024]{0:T(1024)S(1)} %bitcast.221, f32[1024]{0:T(1024)S(1)} %bitcast.212, ...), kind=kOutput, calls=%fused_computation.59 | convolution fusion | flops 8872001536 | bytes 54558720 | tf_op jit(solution)/shard_map/dot_general | solution.py:167
  472.9 73.8 %all-gather.26.cloned.1.call-done = bf16[4096,1024]{1,0:T(8,128)(2,1)} async-done(((bf16[512,1024]{1,0:T(8,128)(2,1)}), bf16[4096,1024]{1,0:T(8,128)(2,1)}) %all-gather.26.cloned.1.call-update) | async-done | bytes 8388624 | tf_op jit(solution)/shard_map/all_gather | solution.py:116
  546.8 14.9 fusion.93
  564.9 4.3 fusion.88
  569.2 24.8 %convert_reduce_fusion = (f32[4096]{0:T(1024)}, bf16[1024,4096]{1,0:T(8,128)(2,1)}) fusion(f32[1024,4096]{1,0:T(8,128)} %get-tuple-element.287, bf16[4096,1024]{1,0:T(8,128)(2,1)} %all-gather.26.cloned.1.call-done, f32[1024,1024]{1,0:T(8,128)} %get-tuple-element.283, f32[1024,4096]{1,0:T(8,128)} %get-tuple-element.297, f32[4096]{0:T(1024)S(1)} %bitcast.220), kind=kOutput, calls=%fused_computation.57 | convolution fusion | flops 8662282240 | bytes 54558720 | tf_op jit(solution)/shard_map/nd,fd->nf/dot_general | solution.py:198
  594.0 17.5 multiply_reduce_fusion.2
  619.2 6.6 reshape.181
  625.8 5.8 copy.71
  631.6 108.6 %while.27 = (s32[]{:T(128)}, bf16[2,4,128,16,64]{2,4,3,1,0:T(8,128)(2,1)}, bf16[2,4,512,16,64]{2,4,3,1,0:T(8,128)(2,1)}, bf16[2,4,512,16,64]{2,4,3,1,0:T(8,128)(...) while((s32[]{:T(128)}, ...), condition=%wide.region_14.15_spmd, body=%wide.region_12.14_spmd.sunk | while | flops 2737823744 | bytes 185832640 | solution.py:219
  631.6 10.5 fusion.137
  642.0 12.8 multiply_reduce_fusion.10
  654.9 11.9 multiply_convert_fusion.4
  670.1 5.5 fusion.138
  677.0 9.0 bitcast_dynamic-update-slice_fusion.8
  685.9 10.5 fusion.137
  696.4 12.8 multiply_reduce_fusion.10
  709.2 11.9 multiply_convert_fusion.4
  724.4 5.5 fusion.138
  731.3 8.9 bitcast_dynamic-update-slice_fusion.8
  740.2 12.7 copy.82
  752.9 16.3 copy.92
  769.3 13.6 copy.80
  782.9 16.4 copy.90
  801.2 6.5 fusion.73
  807.8 16.8 fusion.84
  824.7 16.5 fusion.76
  845.8 4.4 reshape.151
  853.8 60.1 %reduce-scatter.19.cloned.1.call-done = bf16[128,8192]{1,0:T(8,128)(2,1)} async-done(((bf16[512,8192]{1,0:T(8,128)(2,1)}), bf16[128,8192]{1,0:T(8,128)(2,1)}) %reduce-scatter.19.cloned.1.call-update) | async-done | bytes 2097168
  925.8 4.1 copy.76
  929.9 14.7 convolution_bitcast_fusion
  949.2 56.4 %reduce-scatter.13.cloned.1.call-done = f32[128,1024]{1,0:T(8,128)} async-done(((f32[1024,1024]{1,0:T(8,128)}), f32[128,1024]{1,0:T(8,128)}) %reduce-scatter.13.cloned.1.call-update) | async-done | bytes 524304 | tf_op jit(solution)/shard_map/reduce_scatter | solution.py:254
  1012.2 38.9 %all-reduce.9 = (bf16[1024]{0:T(1024)(128)(2,1)S(1)}, bf16[1024]{0:T(1024)(128)(2,1)S(1)}, bf16[1024]{0:T(1024)(128)(2,1)S(1)}, bf16[1024]{0:T(1024)(128)(2,1)S(...) all-reduce(f32[1024]{0:T(1024)S(1)} %reduce_sum.182, ...), channel_id=8, replica_groups=mesh['ctx'=4,'fsdp'=8] {'fsdp'}, use_global_device_ids=true, to_apply=%region_26.27.clone | all-reduce | flops 12288 | bytes 73728
  1051.7 6.4 all-reduce.10
  1062.8 230.0 %reduce-scatter.15.cloned.1.call-done = f32[128,4096]{1,0:T(8,128)} async-done(((f32[1024,4096]{1,0:T(8,128)}), f32[128,4096]{1,0:T(8,128)}) %reduce-scatter.15.cloned.1.call-update) | async-done | bytes 2097168 | tf_op jit(solution)/shard_map/reduce_scatter | solution.py:255
  1295.5 282.5 %reduce-scatter.17.cloned.1.call-done = f32[512,1024]{1,0:T(8,128)} async-done(((f32[4096,1024]{1,0:T(8,128)}), f32[512,1024]{1,0:T(8,128)}) %reduce-scatter.17.cloned.1.call-update) | async-done | bytes 2097168 | tf_op jit(solution)/shard_map/reduce_scatter | solution.py:256
  1580.6 208.0 %reduce-scatter.11.cloned.1.call-done = f32[128,3072]{0,1:T(8,128)} async-done(((f32[1024,3072]{0,1:T(8,128)}), f32[128,3072]{0,1:T(8,128)}) %reduce-scatter.11.cloned.1.call-update) | async-done | bytes 1572880 | tf_op jit(solution)/shard_map/reduce_scatter | solution.py:253
  1791.0 12.1 add_convert_fusion.1
  1803.1 57.0 %all-reduce.14.cloned.1.call-done = (bf16[128,3072]{0,1:T(8,128)(2,1)}, bf16[128,1024]{1,0:T(8,128)(2,1)}, bf16[128,4096]{1,0:T(8,128)(2,1)}, bf16[512,1024]{1,0:T(8,128)(2,1)}) async-done(((bf16[128,3072]{0,1:T(8,128)(2,1)}, bf16[128,1024]{1,0:T(8,128)(2,1)}, bf16[128,4096]{1,0:T(8,128)(2,1)}, bf16[512,1024]{1,0:T(8,128)(2,1)}), (bf16[128,3072]{0,1:T(8,128)(2,1)}, bf16[128,1024]{1,0:T(8,128)(2,1)}, ...) | async-done | bytes 3145744 | tf_op jit(solution)/shard_map/psum | solution.py:269
  (208 shorter events, 96.2 us)
Async XLA Ops:
  7.2 104.8 %all-gather.16.cloned.1.call-start = ((), (), s32[]{:S(2)}) async-start(), calls=%async_computation.6 | async-start | bytes 7077888 | tf_op jit(solution)/shard_map/all_gather | solution.py:113
  7.9 271.4 %all-gather.18.cloned.1.call-start = ((), (), s32[]{:S(2)}) async-start(), calls=%async_computation.7 | async-start | bytes 10485760 | tf_op jit(solution)/shard_map/all_gather | solution.py:152
  121.4 6.3 copy-start.7
  127.7 6.0 copy-start.41
  127.7 24.2 %copy-start.42 = (bf16[128]{0:T(256)(128)(2,1)S(1)}, bf16[128]{0:T(256)(128)(2,1)}, u32[]{:S(2)}) copy-start(bf16[128]{0:T(256)(128)(2,1)} %param.28) | copy-start | bytes 772
  127.7 41.5 %copy-start.43 = (bf16[128]{0:T(256)(128)(2,1)S(1)}, bf16[128]{0:T(256)(128)(2,1)}, u32[]{:S(2)}) copy-start(bf16[128]{0:T(256)(128)(2,1)} %param.29) | copy-start | bytes 772
  127.7 59.7 %copy-start.40 = (bf16[512]{0:T(512)(128)(2,1)S(1)}, bf16[512]{0:T(512)(128)(2,1)}, u32[]{:S(2)}) copy-start(bf16[512]{0:T(512)(128)(2,1)} %param.30) | copy-start | bytes 3076
  127.7 86.3 %copy-start.44 = (bf16[128]{0:T(256)(128)(2,1)S(1)}, bf16[128]{0:T(256)(128)(2,1)}, u32[]{:S(2)}) copy-start(bf16[128]{0:T(256)(128)(2,1)} %param.31) | copy-start | bytes 772
  127.7 103.0 %copy-start.45 = (bf16[128]{0:T(256)(128)(2,1)S(1)}, bf16[128]{0:T(256)(128)(2,1)}, u32[]{:S(2)}) copy-start(bf16[128]{0:T(256)(128)(2,1)} %param.32) | copy-start | bytes 772
  127.7 121.2 %copy-start.3 = (bf16[8,128,1024]{2,1,0:T(8,128)(2,1)S(1)}, bf16[8,128,1024]{2,1,0:T(8,128)(2,1)}, u32[]{:S(2)}) copy-start(bf16[8,128,1024]{2,1,0:T(8,128)(2,1)} %param.20) | copy-start | bytes 6291460
  127.8 123.2 %copy-start.46 = (bf16[128]{0:T(256)(128)(2,1)S(1)}, bf16[128]{0:T(256)(128)(2,1)}, u32[]{:S(2)}) copy-start(bf16[128]{0:T(256)(128)(2,1)} %param.33) | copy-start | bytes 772
  127.8 162.9 %all-gather.20.cloned.1.call-start = ((), (), s32[]{:S(2)}) async-start(), calls=%async_computation.8 | async-start | bytes 10485760 | tf_op jit(solution)/shard_map/all_gather | solution.py:151
  131.8 214.0 %all-gather.22.cloned.1.call-start = ((), (), s32[]{:S(2)}) async-start(), calls=%async_computation.9 | async-start | bytes 2359296 | tf_op jit(solution)/shard_map/all_gather | solution.py:114
  132.4 289.2 %all-gather.24.cloned.1.call-start = ((), (), s32[]{:S(2)}) async-start(), calls=%async_computation.10 | async-start | bytes 9437184 | tf_op jit(solution)/shard_map/all_gather | solution.py:115
  133.0 413.8 %all-gather.26.cloned.1.call-start = ((), (), s32[]{:S(2)}) async-start(), calls=%async_computation.11 | async-start | bytes 9437184 | tf_op jit(solution)/shard_map/all_gather | solution.py:116
  133.6 716.7 %reduce-scatter.21.cloned.1.call-start = ((), (), s32[]{:S(2)}) async-start(), calls=%async_computation.17 | async-start | bytes 10485760
  248.9 19.0 %copy-start.18 = (f32[8,1,128]{2,1,0:T(1,128)}, f32[8,1,128]{2,1,0:T(1,128)S(1)}, u32[]{:S(2)}) copy-start(f32[8,1,128]{2,1,0:T(1,128)S(1)} %convert_element_type.272) | copy-start | bytes 12292
  302.2 43.6 %copy-start.39 = (f32[8,1,128]{2,1,0:T(1,128)S(1)}, f32[8,1,128]{2,1,0:T(1,128)}, u32[]{:S(2)}) copy-start(f32[8,1,128]{2,1,0:T(1,128)} %convert_element_type.267) | copy-start | bytes 12292
  341.0 11.0 copy-start
  341.0 11.1 copy-start.15
  345.8 75.8 %copy-start.27 = (f32[8,1,128]{2,1,0:T(1,128)S(1)}, f32[8,1,128]{2,1,0:T(1,128)}, u32[]{:S(2)}) copy-start(f32[8,1,128]{2,1,0:T(1,128)} %convert_element_type.268) | copy-start | bytes 12292
  345.8 75.8 %copy-start.32 = (f32[8,1,512]{2,1,0:T(1,128)S(1)}, f32[8,1,512]{2,1,0:T(1,128)}, u32[]{:S(2)}) copy-start(f32[8,1,512]{2,1,0:T(1,128)} %convert_element_type.270) | copy-start | bytes 49156
  345.8 75.8 %copy-start.36 = (f32[8,1,128]{2,1,0:T(1,128)S(1)}, f32[8,1,128]{2,1,0:T(1,128)}, u32[]{:S(2)}) copy-start(f32[8,1,128]{2,1,0:T(1,128)} %convert_element_type.269) | copy-start | bytes 12292
  352.1 2.0 copy-start.5
  352.1 259.4 %copy-start.20 = (f32[1024]{0:T(1024)}, f32[1024]{0:T(1024)S(1)}, u32[]{:S(2)}) copy-start(f32[1024]{0:T(1024)S(1)} %broadcast_multiply_fusion.4) | copy-start | bytes 12292
  354.6 256.8 %copy-start.29 = (f32[1024]{0:T(1024)}, f32[1024]{0:T(1024)S(1)}, u32[]{:S(2)}) copy-start(f32[1024]{0:T(1024)S(1)} %add_rsqrt_fusion.1) | copy-start | bytes 12292
  421.6 125.1 %copy-start.38 = (f32[8,1,128]{2,1,0:T(1,128)S(1)}, f32[8,1,128]{2,1,0:T(1,128)}, u32[]{:S(2)}) copy-start(f32[8,1,128]{2,1,0:T(1,128)} %convert_element_type.271) | copy-start | bytes 12292
  546.8 15.5 copy-start.4
  546.8 15.5 copy-start.19
  561.7 3.3 copy-start.23
  561.7 3.2 copy-start.24
  594.0 17.5 copy-start.6
  611.5 4.0 copy-start.47
  613.5 2.0 copy-start.11
  619.2 12.4 copy-start.1
  619.2 12.4 copy-start.16
  631.6 10.5 copy-start.2
  666.8 3.3 copy-start.8
  675.6 1.3 copy-start.9
  685.9 10.5 copy-start.2
  721.1 3.3 copy-start.8
  730.0 1.3 copy-start.9
  769.3 144.6 %reduce-scatter.19.cloned.1.call-start = ((), (), s32[]{:S(2)}) async-start(), calls=%async_computation.16 | async-start | bytes 10485760
  799.4 1.8 copy-start.12
  799.4 8.3 copy-start.21
  799.4 8.3 copy-start.28
  799.4 8.3 copy-start.30
  799.4 8.3 copy-start.37
  799.4 206.1 %reduce-scatter.13.cloned.1.call-start = ((), (), s32[]{:S(2)}) async-start(), calls=%async_computation.13 | async-start | bytes 4718592 | tf_op jit(solution)/shard_map/reduce_scatter | solution.py:254
  807.7 485.1 %reduce-scatter.15.cloned.1.call-start = ((), (), s32[]{:S(2)}) async-start(), calls=%async_computation.14 | async-start | bytes 18874368 | tf_op jit(solution)/shard_map/reduce_scatter | solution.py:255
  824.6 753.3 %reduce-scatter.17.cloned.1.call-start = ((), (), s32[]{:S(2)}) async-start(), calls=%async_computation.15 | async-start | bytes 18874368 | tf_op jit(solution)/shard_map/reduce_scatter | solution.py:256
  841.2 1.6 copy-start.10
  841.2 947.4 %reduce-scatter.11.cloned.1.call-start = ((), (), s32[]{:S(2)}) async-start(), calls=%async_computation.12 | async-start | bytes 14155776 | tf_op jit(solution)/shard_map/reduce_scatter | solution.py:253
  944.7 67.5 %copy-start.22 = (f32[1024]{0:T(1024)S(1)}, f32[1024]{0:T(1024)}, u32[]{:S(2)}) copy-start(f32[1024]{0:T(1024)} %get-tuple-element.282) | copy-start | bytes 12292
  944.7 67.5 %copy-start.25 = (f32[1024]{0:T(1024)S(1)}, f32[1024]{0:T(1024)}, u32[]{:S(2)}) copy-start(f32[1024]{0:T(1024)} %get-tuple-element.228) | copy-start | bytes 12292
  944.7 67.5 %copy-start.26 = (f32[1024]{0:T(1024)S(1)}, f32[1024]{0:T(1024)}, u32[]{:S(2)}) copy-start(f32[1024]{0:T(1024)} %get-tuple-element.284) | copy-start | bytes 12292
  944.7 67.5 %copy-start.31 = (f32[4096]{0:T(1024)S(1)}, f32[4096]{0:T(1024)}, u32[]{:S(2)}) copy-start(f32[4096]{0:T(1024)} %get-tuple-element.301) | copy-start | bytes 49156
  944.7 67.4 %copy-start.33 = (f32[1024]{0:T(1024)S(1)}, f32[1024]{0:T(1024)}, u32[]{:S(2)}) copy-start(f32[1024]{0:T(1024)} %get-tuple-element.224) | copy-start | bytes 12292
  944.7 67.4 %copy-start.34 = (f32[1024]{0:T(1024)S(1)}, f32[1024]{0:T(1024)}, u32[]{:S(2)}) copy-start(f32[1024]{0:T(1024)} %get-tuple-element.222) | copy-start | bytes 12292
  944.7 67.4 %copy-start.35 = (f32[1024]{0:T(1024)S(1)}, f32[1024]{0:T(1024)}, u32[]{:S(2)}) copy-start(f32[1024]{0:T(1024)} %get-tuple-element.227) | copy-start | bytes 12292
  944.7 915.3 %all-reduce.14.cloned.1.call-start = ((), (), s32[]{:S(2)}) async-start(), calls=%async_computation.18 | async-start | bytes 6291456 | tf_op jit(solution)/shard_map/psum | solution.py:269
  1012.1 778.9 %copy-start.13 = (bf16[1024,1024]{0,1:T(8,128)(2,1)S(1)}, bf16[1024,1024]{0,1:T(8,128)(2,1)}, u32[]{:S(2)}) copy-start(bf16[1024,1024]{0,1:T(8,128)(2,1)} %reshape.151) | copy-start | bytes 6291460
  1860.1 5.6 copy-start.14
  1860.1 7.1 copy-start.17
  (1 other events, 0.7 us)
Sparse Core Ops, SparseCore 0:
  10.2 101.7 all-gather.15
  127.9 56.4 all-gather.17
  186.6 58.2 all-gather.19
  246.9 49.2 all-gather.21
  298.2 123.4 all-gather.23
  423.6 123.1 all-gather.25
  769.4 69.8 reduce-scatter.20
  842.1 71.7 reduce-scatter.18
  917.5 88.0 reduce-scatter.12
  1009.7 283.0 reduce-scatter.14
  1296.5 281.3 reduce-scatter.16
  1581.8 206.7 reduce-scatter.10
  1791.9 68.0 all-reduce.13
where the time goes:
time: 1880 us; the launch traced here: 1870 us
  waiting for transfers between devices  1100 us (59%)
  matrix products  301 us (16%)
  blocking collectives  213 us (11%)
  local copies, waits for them, and re-layouts  166 us (9%)
  other arithmetic  76 us (4%)
    reduce_scatter x1, waiting for transfers between devices, local(): lax.psum_scatter(down_weight_grad, 'fsdp', scatter_dimension=0, tiled=True)  282 us
    reduce_scatter x1, waiting for transfers between devices, local(): lax.psum_scatter(up_weight_grad, 'fsdp', scatter_dimension=0, tiled=True)  230 us
    reduce_scatter x1, waiting for transfers between devices, local(): lax.psum_scatter(input_weight_grad, 'fsdp', scatter_dimension=0, tiled=True)  208 us
    unnamed x111, local copies, waits for them, and re-layouts  80.9 us
    all_gather x1, waiting for transfers between devices, local(): lax.all_gather(shards[3], 'fsdp', axis=0, tiled=True)  73.8 us
    all_gather x1, waiting for transfers between devices, local(): lax.all_gather(shards[2], 'fsdp', axis=0, tiled=True)  67 us
    all_gather x1, waiting for transfers between devices, local(): lax.all_gather(shards[0], 'fsdp', axis=0, tiled=True)  64.8 us
    unnamed x15, waiting for transfers between devices  62.5 us
  transfers between devices with their start and end apart: 13, of which 9 were waited for; matrix products, arithmetic and copies ran while one was open for 15% of the time, Pallas kernels for 0%

commit v1 on v0

v1 whole, which is shorter than its diff:
```python
import math

import jax
import jax.numpy as jnp
from jax import lax
from jax.sharding import PartitionSpec as P

H = 16


epsilon = 1e-05


def norm_forward(values):
    centre = values - jnp.mean(values, axis=-1, keepdims=True)
    inverse = lax.rsqrt(jnp.mean(centre * centre, axis=-1, keepdims=True) + epsilon)
    return (centre * inverse, inverse)


def norm_backward(upstream, normed, inverse, gain):
    scaled = upstream * gain
    return inverse * (
        scaled
        - jnp.mean(scaled, axis=-1, keepdims=True)
        - normed * jnp.mean(scaled * normed, axis=-1, keepdims=True)
    )


def gelu_exact(values):
    return jax.nn.gelu(values, approximate=False)


def attend_forward(blocks):
    query, key_rows, value_rows = blocks
    factor = 1.0 / math.sqrt(query.shape[-1])
    scores = (
        jnp.einsum("sqhd,skhd->shqk", query, key_rows, preferred_element_type=jnp.float32) * factor
    )
    row_max = jnp.max(scores, axis=-1, keepdims=True)
    exponent = jnp.exp(scores - row_max)
    totals = jnp.sum(exponent, axis=-1, keepdims=True)
    probs = (exponent / totals).astype(jnp.bfloat16)
    context = jnp.einsum("shqk,skhd->sqhd", probs, value_rows, preferred_element_type=jnp.float32)
    return (context.astype(jnp.bfloat16), row_max + jnp.log(totals))


def attend_backward(blocks):
    query, key_rows, value_rows, d_context, log_total = blocks
    factor = 1.0 / math.sqrt(query.shape[-1])
    scores = (
        jnp.einsum("sqhd,skhd->shqk", query, key_rows, preferred_element_type=jnp.float32) * factor
    )
    probs = jnp.exp(scores - log_total)
    d_probs = jnp.einsum(
        "sqhd,skhd->shqk", d_context, value_rows, preferred_element_type=jnp.float32
    )
    centre = jnp.sum(probs * d_probs, axis=-1, keepdims=True)
    d_scores = (probs * (d_probs - centre)).astype(jnp.bfloat16)
    d_query = (
        jnp.einsum("shqk,skhd->sqhd", d_scores, key_rows, preferred_element_type=jnp.float32)
        * factor
    ).astype(jnp.bfloat16)
    d_keys = (
        jnp.einsum("shqk,sqhd->skhd", d_scores, query, preferred_element_type=jnp.float32) * factor
    ).astype(jnp.bfloat16)
    d_values = jnp.einsum(
        "shqk,sqhd->skhd", probs.astype(jnp.bfloat16), d_context, preferred_element_type=jnp.float32
    ).astype(jnp.bfloat16)
    return (d_query, d_keys, d_values)


def quarter(shard):
    rows = shard.shape[0] // lax.axis_size("ctx")
    return lax.dynamic_slice_in_dim(shard, lax.axis_index("ctx") * rows, rows, 0)


def gathered(shard):
    return lax.all_gather(quarter(shard), ("fsdp", "ctx"), axis=0, tiled=True)


def reduced(grad):
    part = lax.psum_scatter(
        grad.astype(jnp.bfloat16), ("fsdp", "ctx"), scatter_dimension=0, tiled=True
    )
    return lax.all_gather(part, "ctx", axis=0, tiled=True).astype(jnp.float32)


def local(
    tokens,
    cotangent,
    input_weight,
    output_weight,
    up_weight,
    down_weight,
    query_bias,
    value_bias,
    output_bias,
    norm_gain,
    norm_shift,
    up_bias,
    down_bias,
    final_gain,
    final_shift,
):
    small = (
        query_bias,
        value_bias,
        output_bias,
        norm_gain,
        norm_shift,
        up_bias,
        down_bias,
        final_gain,
        final_shift,
    )
    sizes = [member.shape[0] for member in small]
    ends = [sum(sizes[: i + 1]) for i in range(len(sizes))]
    all_small = lax.all_gather(jnp.concatenate(small), "fsdp", axis=0, tiled=False)
    (
        full_qbias,
        full_vbias,
        full_obias,
        full_ngain,
        full_nshift,
        full_ubias,
        full_dbias,
        full_fgain,
        full_fshift,
    ) = [
        all_small[:, end - size : end].reshape(-1).astype(jnp.float32)
        for size, end in zip(sizes, ends)
    ]
    mine = lax.all_to_all(tokens, "ctx", split_axis=0, concat_axis=1, tiled=True)
    mine_cot = lax.all_to_all(cotangent, "ctx", split_axis=0, concat_axis=1, tiled=True)
    wide_input = gathered(input_weight)
    wide_output = gathered(output_weight)
    wide_up = gathered(up_weight)
    wide_down = gathered(down_weight)
    seqs, length, width = mine.shape
    rows_all = seqs * length
    head_size = width // H
    tok_rows = mine.reshape(rows_all, width)
    merged = jnp.dot(tok_rows, wide_input, preferred_element_type=jnp.float32)
    query = (merged[:, :width] + full_qbias).astype(jnp.bfloat16)
    key_rows = merged[:, width : 2 * width].astype(jnp.bfloat16)
    value_rows = (merged[:, 2 * width :] + full_vbias).astype(jnp.bfloat16)
    shape = (seqs, 1, length, H, head_size)
    head_query = query.reshape(shape)
    head_keys = key_rows.reshape(shape)
    head_values = value_rows.reshape(shape)
    context, log_total = lax.map(attend_forward, (head_query, head_keys, head_values))
    context_rows = context.reshape(rows_all, width)
    pre_one = (
        tok_rows.astype(jnp.float32)
        + jnp.dot(context_rows, wide_output, preferred_element_type=jnp.float32)
        + full_obias
    )
    normed_one, inverse_one = norm_forward(pre_one)
    hidden = normed_one * full_ngain + full_nshift
    hidden_low = hidden.astype(jnp.bfloat16)
    inner = jnp.dot(hidden_low, wide_up, preferred_element_type=jnp.float32) + full_ubias
    active_full, gelu_pull = jax.vjp(gelu_exact, inner)
    active = active_full.astype(jnp.bfloat16)
    pre_two = hidden + jnp.dot(active, wide_down, preferred_element_type=jnp.float32) + full_dbias
    normed_two, inverse_two = norm_forward(pre_two)
    layer_out = (normed_two * full_fgain + full_fshift).astype(jnp.bfloat16).reshape(mine.shape)
    upstream = mine_cot.reshape(rows_all, width).astype(jnp.float32)
    final_gain_grad = jnp.sum(upstream * normed_two, axis=0)
    final_shift_grad = jnp.sum(upstream, axis=0)
    d_pre_two = norm_backward(upstream, normed_two, inverse_two, full_fgain)
    d_branch = d_pre_two.astype(jnp.bfloat16)
    down_bias_grad = jnp.sum(d_pre_two, axis=0)
    down_weight_grad = jnp.einsum("nf,nd->fd", active, d_branch, preferred_element_type=jnp.float32)
    d_active = jnp.einsum("nd,fd->nf", d_branch, wide_down, preferred_element_type=jnp.float32)
    d_inner = gelu_pull(d_active)[0].astype(jnp.bfloat16)
    up_bias_grad = jnp.sum(d_inner.astype(jnp.float32), axis=0)
    up_weight_grad = jnp.einsum(
        "nd,nf->df", hidden_low, d_inner, preferred_element_type=jnp.float32
    )
    d_hidden = d_pre_two + jnp.einsum(
        "nf,df->nd", d_inner, wide_up, preferred_element_type=jnp.float32
    )
    norm_gain_grad = jnp.sum(d_hidden * normed_one, axis=0)
    norm_shift_grad = jnp.sum(d_hidden, axis=0)
    d_pre_one = norm_backward(d_hidden, normed_one, inverse_one, full_ngain)
    d_attn = d_pre_one.astype(jnp.bfloat16)
    output_bias_grad = jnp.sum(d_pre_one, axis=0)
    output_weight_grad = jnp.einsum(
        "nc,nd->cd", context_rows, d_attn, preferred_element_type=jnp.float32
    )
    d_context = jnp.einsum(
        "nd,cd->nc", d_attn, wide_output, preferred_element_type=jnp.float32
    ).astype(jnp.bfloat16)
    head_dctx = d_context.reshape(shape)
    d_query, d_keys, d_values = lax.map(
        attend_backward, (head_query, head_keys, head_values, head_dctx, log_total)
    )
    d_query = d_query.reshape(rows_all, width)
    d_values = d_values.reshape(rows_all, width)
    d_merged = jnp.concatenate([d_query, d_keys.reshape(rows_all, width), d_values], axis=1)
    query_bias_grad = jnp.sum(d_query.astype(jnp.float32), axis=0)
    value_bias_grad = jnp.sum(d_values.astype(jnp.float32), axis=0)
    input_weight_grad = jnp.einsum(
        "nd,ne->de", tok_rows, d_merged, preferred_element_type=jnp.float32
    )
    tokens_grad = (
        d_pre_one
        + jnp.einsum("ne,de->nd", d_merged, wide_input, preferred_element_type=jnp.float32)
    ).astype(jnp.bfloat16)
    tokens_grad = tokens_grad.reshape(mine.shape)
    layer_out, tokens_grad = [
        lax.all_to_all(member, "ctx", split_axis=1, concat_axis=0, tiled=True)
        for member in (layer_out, tokens_grad)
    ]
    matrices = tuple(
        reduced(member)
        for member in (input_weight_grad, output_weight_grad, up_weight_grad, down_weight_grad)
    )
    vectors = (
        query_bias_grad,
        value_bias_grad,
        output_bias_grad,
        norm_gain_grad,
        norm_shift_grad,
        up_bias_grad,
        down_bias_grad,
        final_gain_grad,
        final_shift_grad,
    )
    parts = lax.axis_size("fsdp")
    joined = jnp.concatenate([member.reshape(parts, -1) for member in vectors], axis=1)
    summed = lax.psum(joined, ("fsdp", "ctx"))
    own = lax.dynamic_index_in_dim(summed, lax.axis_index("fsdp"), 0, keepdims=False)
    small_grads = tuple(own[end - size : end] for size, end in zip(sizes, ends))
    return (layer_out, tokens_grad) + matrices + small_grads


def solution(mesh):
    rows = P("fsdp", "ctx", None)
    matrix = P("fsdp", None)
    vector = P("fsdp")
    return jax.shard_map(
        local,
        mesh=mesh,
        in_specs=(rows,) * 2 + (matrix,) * 4 + (vector,) * 9,
        out_specs=(rows,) * 2 + (matrix,) * 4 + (vector,) * 9,
        check_vma=False,
    )
```

time: 1880 us -> 994 us (0.53)
  waiting for transfers between devices: 1100 us -> 384 us
  blocking collectives: 213 us -> 120 us
  local copies, waits for them, and re-layouts: 166 us -> 102 us
    reduce_scatter x4, waiting for transfers between devices: 777 us -> 255 us  [reduced(): lax.psum_scatter(grad.astype(jnp.bfloat16), ('fsdp', 'ctx'), scatter_dime...]
    all_gather x9 -> x3, blocking collectives: 168 us -> 47.9 us  [the longest x1 33 us: local(): lax.all_gather(jnp.concatenate(small), 'fsdp', axis=0, tiled=False)]
    all_gather x6, waiting for transfers between devices: 206 us -> 90.4 us  [the longest x4 67.7 us: gathered(): return lax.all_gather(quarter(shard), ('fsdp', 'ctx'), axis=0, tiled=True)]
    unnamed x15 -> x10, waiting for transfers between devices: 62.5 us -> 0.8 us
    unnamed x111 -> x110, local copies, waits for them, and re-layouts: 80.9 us -> 23.5 us
    psum x1 -> x0, waiting for transfers between devices: 57 us -> none  [local(): lax.psum(for_sending(tuple(grads)), 'ctx')]
    unnamed x1 -> x0, blocking collectives: 38.9 us -> none
    all_to_all x0 -> x3, waiting for transfers between devices: none -> 37.6 us  [the longest x2 37.6 us: local(): lax.all_to_all(member, 'ctx', split_axis=1, concat_axis=0, tiled=True)]
  transfers between devices with their start and end apart: 13 -> 13, of which waited for: 9 -> 9; matrix products, arithmetic and copies ran while one was open for 15% -> 38% of each run, Pallas kernels for 0% -> 0%
where the time goes in v1:
time: 994 us; the launch traced here: 984 us
  waiting for transfers between devices  384 us (39%)
  matrix products  286 us (29%)
  blocking collectives  120 us (12%)
  local copies, waits for them, and re-layouts  102 us (10%)
  other arithmetic  64.5 us (6%)
  between operations  15.3 us (2%)
  starting transfers between devices  12.4 us (1%)
    reduce_scatter x4, waiting for transfers between devices, reduced(): lax.psum_scatter(grad.astype(jnp.bfloat16), ('fsdp', 'ctx'), scatter_dime...  255 us
    all_gather x4, waiting for transfers between devices, gathered(): return lax.all_gather(quarter(shard), ('fsdp', 'ctx'), axis=0, tiled=True)  67.7 us
    dot_general x1, matrix products, local(): jnp.dot(hidden_low, wide_up, preferred_element_type=jnp.float32)  51.7 us
    psum x1, blocking collectives, local(): summed = lax.psum(joined, ('fsdp', 'ctx'))  39 us
    all_to_all x2, waiting for transfers between devices, local(): lax.all_to_all(member, 'ctx', split_axis=1, concat_axis=0, tiled=True)  37.6 us
    all_gather x1, blocking collectives, local(): lax.all_gather(jnp.concatenate(small), 'fsdp', axis=0, tiled=False)  33 us
    all_to_all x1, blocking collectives, local(): lax.all_to_all(tokens, 'ctx', split_axis=0, concat_axis=1, tiled=True)  33 us
    dot_general x1, matrix products, local(): jnp.einsum('nd,fd->nf', d_branch, wide_down, preferred_element_type=jnp.f...  24.8 us
  transfers between devices with their start and end apart: 13, of which 9 were waited for; matrix products, arithmetic and copies ran while one was open for 38% of the time, Pallas kernels for 0%

profile of v1, /device:TPU:0, one launch (start us, length us, event | category | flops | bytes accessed | tf_op | source)
XLA Modules:
  0.0 983.9 jit_solution(5195755060029864727)
XLA Ops:
  11.4 33.0 %all_to_all.60 = bf16[8,128,1024]{2,1,0:T(8,128)(2,1)} all-to-all(bf16[8,128,1024]{2,1,0:T(8,128)(2,1)} %param.19), channel_id=1, replica_groups=mesh['ctx'=4,'fsdp'=8] {'ctx'}, dimensions={0} | all-to-all | bytes 4194304 | tf_op jit(solution)/shard_map/all_to_all | solution.py:133
  44.4 3.6 all-to-all-start.2
  51.9 33.0 %all-gather.1 = bf16[8,1,1536]{2,1,0:T(2,128)(2,1)S(1)} all-gather(bf16[1,1,1536]{2,1,0:T(2,128)(2,1)S(1)} %reshape.378), channel_id=2, replica_groups=mesh['ctx'=4,'fsdp'=8] {'fsdp'}, dimensions={0}, use_global_device_ids=true | all-gather | bytes 27648 | tf_op jit(solution)/shard_map/all_gather | solution.py:118
  86.1 3.1 copy.71
  93.0 4.6 all-gather.9.cloned.1.call-done
  97.6 8.9 convolution_bitcast_fusion
  109.2 4.5 reshape.347
  113.7 3.4 copy.72
  117.0 4.5 reshape.348
  121.5 3.4 copy.73
  124.9 2.7 reshape.349
  131.2 54.1 %while.26 = (s32[]{:T(128)}, bf16[2,1,512,16,64]{2,4,3,1,0:T(8,128)(2,1)}, f32[2,1,16,512,1]{3,2,4,1,0:T(8,128)S(1)}, bf16[2,1,512,16,64]{2,4,3,1,0:T(8,128)(2,1...) while((s32[]{:T(128)}, ...), condition=%wide.region_3.4_spmd, body=%wide.region_0.3_spmd.sunk | while | flops 1112006656 | bytes 54790224 | solution.py:151
  131.4 9.4 multiply_reduce_fusion.11
  140.9 8.6 fusion.125
  149.5 8.9 fusion.126
  158.4 9.4 multiply_reduce_fusion.11
  167.9 8.6 fusion.125
  176.5 8.8 fusion.126
  185.3 4.5 copy.75
  191.7 5.7 fusion.87
  200.0 35.4 %all-gather.13.cloned.1.call-done = bf16[1024,4096]{1,0:T(8,128)(2,1)} async-done(((bf16[32,4096]{1,0:T(8,128)(2,1)}), bf16[1024,4096]{1,0:T(8,128)(2,1)}) %all-gather.13.cloned.1.call-update) | async-done | bytes 8388624 | tf_op jit(solution)/shard_map/all_gather | solution.py:78
  235.4 51.7 %multiply_convert_fusion.3 = (bf16[1024,4096]{1,0:T(8,128)(2,1)}, f32[1024,4096]{1,0:T(8,128)}, f32[1024,4096]{1,0:T(8,128)}) fusion(f32[4096]{0:T(1024)S(1)} %bitcast.286, bf16[1024,4096]{1,0:T(8,128)(2,1)} %all-gather.13.cloned.1.call-done, f32[1024,1024]{1,0:T(8,128)} %copy-done.10, f32[1024]{0:T(1024)S(1)} %copy-done.31, f32[1024]{0:T(1024)S(1)} %copy-done.23, ...), kind=kOutput, calls=%fused_computation.62 | convolution fusion | flops 8872001536 | bytes 54558720 | tf_op jit(solution)/shard_map/dot_general | solution.py:161
  287.1 27.7 %all-gather.15.cloned.1.call-done = bf16[4096,1024]{1,0:T(8,128)(2,1)} async-done(((bf16[128,1024]{1,0:T(8,128)(2,1)}), bf16[4096,1024]{1,0:T(8,128)(2,1)}) %all-gather.15.cloned.1.call-update) | async-done | bytes 8388624 | tf_op jit(solution)/shard_map/all_gather | solution.py:78
  314.8 14.8 %fusion.88 = (f32[1024]{0:T(1024)S(1)}, f32[1024,1024]{1,0:T(8,128)S(1)}) fusion(f32[1024]{0:T(1024)S(1)} %copy-done.32, bf16[1024,4096]{1,0:T(8,128)(2,1)} %get-tuple-element.217, bf16[4096,1024]{1,0:T(8,128)(2,1)} %all-gather.15.cloned.1.call-done, f32[1024]{0:T(1024)S(1)} %copy-done.31, f32[1024]{0:T(1024)S(1)} %copy-done.23, ...), kind=kOutput, calls=%fused_computation.171 | convolution fusion | flops 8597273600 | bytes 25190400 | tf_op jit(solution)/shard_map/dot_general | solution.py:164
  334.5 4.4 fusion.84
  338.9 24.8 %convert_reduce_fusion = (f32[4096]{0:T(1024)}, bf16[1024,4096]{1,0:T(8,128)(2,1)}) fusion(f32[1024,4096]{1,0:T(8,128)} %get-tuple-element.218, bf16[4096,1024]{1,0:T(8,128)(2,1)} %all-gather.15.cloned.1.call-done, f32[1024,1024]{1,0:T(8,128)} %get-tuple-element.214, f32[1024,4096]{1,0:T(8,128)} %get-tuple-element.244, f32[4096]{0:T(1024)S(1)} %bitcast.287), kind=kOutput, calls=%fused_computation.60 | convolution fusion | flops 8662282240 | bytes 54558720 | tf_op jit(solution)/shard_map/nd,fd->nf/dot_general | solution.py:174
  363.7 15.5 %convolution_convert_fusion.1 = bf16[1024,4096]{1,0:T(8,128)(2,1)} fusion(bf16[1024,4096]{1,0:T(8,128)(2,1)} %get-tuple-element.249, f32[1024,1024]{1,0:T(8,128)} %copy-done.10, f32[1024]{0:T(1024)S(1)} %copy-done.31, f32[1024]{0:T(1024)S(1)} %copy-done.23, f32[1024]{0:T(1024)S(1)} %add_rsqrt_fusion.1, f32[1024]{0:T(1024)S(1)} %broadcast_multiply_fusion.4), kind=kOutput, calls=%fused_computation.77 | convolution fusion | flops 8599371776 | bytes 20987904 | tf_op jit(solution)/shard_map/nd,nf->df/dot_general | solution.py:177
  379.2 15.5 %convolution_convert_fusion = bf16[4096,1024]{1,0:T(8,128)(2,1)} fusion(bf16[1024,4096]{1,0:T(8,128)(2,1)} %get-tuple-element.217, f32[1024,1024]{1,0:T(8,128)} %get-tuple-element.214), kind=kOutput, calls=%fused_computation.76 | convolution fusion | flops 8595177472 | bytes 20971520 | tf_op jit(solution)/shard_map/nf,nd->fd/dot_general | solution.py:173
  394.8 17.5 %multiply_reduce_fusion.2 = (f32[1024]{0:T(1024)}, f32[1024]{0:T(1024)S(1)}, f32[1024]{0:T(1024)S(1)}, f32[1024]{0:T(1024)}, f32[1024,1024]{1,0:T(8,128)S(1)}) fusion(f32[1024,1024]{1,0:T(8,128)} %copy-done.10, f32[1024]{0:T(1024)S(1)} %add_rsqrt_fusion.1, f32[1024]{0:T(1024)S(1)} %broadcast_multiply_fusion.4, f32[1024]{0:T(1024)S(1)} %copy-done.23, ...), kind=kOutput, calls=%fused_computation.88 | convolution fusion | flops 8600416256 | bytes 29388800 | tf_op jit(solution)/shard_map/nf,df->nd/dot_general | solution.py:180
  418.7 4.0 reshape.381
  422.8 5.6 copy.83
  428.4 5.9 convolution_convert_fusion.2
  439.1 89.6 %while.27 = (s32[]{:T(128)}, bf16[2,1,512,16,64]{2,4,3,1,0:T(8,128)(2,1)}, bf16[2,1,512,16,64]{2,4,3,1,0:T(8,128)(2,1)}, bf16[2,1,512,16,64]{2,4,3,1,0:T(8,128)(...) while((s32[]{:T(128)}, ...), condition=%wide.region_14.15_spmd, body=%wide.region_12.14_spmd.sunk | while | flops 2737299456 | bytes 253990112 | solution.py:195
  439.6 3.9 fusion.135
  443.5 10.9 %multiply_reduce_fusion.12 = (f32[16,512]{1,0:T(8,128)S(1)}, f32[16,512,512]{1,2,0:T(8,128)}) fusion(f32[16,512,512]{1,2,0:T(8,128)S(1)} %fusion.135, f32[16,512]{1,0:T(8,128)S(1)} %dynamic-slice_bitcast_fusion.9, bf16[2,1,512,16,64]{2,4,3,1,0:T(8,128)(2,1)} %get-tuple-element.401, s32[]{:T(128)} %get-tuple-element.383, ...), kind=kOutput, calls=%fused_computation.20.clone.1 | convolution fusion | flops 553639936 | bytes 35718144 | tf_op jit(solution)/shard_map/while/body/eval_jaxpr/sqhd,skhd->shqk/dot_general | solution.py:54
  455.1 10.6 %multiply_convert_fusion.5 = bf16[16,512,512]{1,2,0:T(8,128)(2,1)} fusion(f32[16,512,512]{1,2,0:T(8,128)} %get-tuple-element.350, f32[16,512,512]{1,2,0:T(8,128)S(1)} %fusion.135, f32[16,512]{1,0:T(8,128)S(1)} %get-tuple-element.351, f32[16,512]{1,0:T(8,128)S(1)} %dynamic-slice_bitcast_fusion.9), kind=kLoop, calls=%fused_computation.19.clone.1 | loop fusion | flops 20971520 | bytes 42008576 | tf_op jit(solution)/shard_map/while/body/eval_jaxpr/convert_element_type | solution.py:58
  465.7 7.5 fusion.137
  475.6 8.4 fusion.138
  484.0 3.9 fusion.135
  488.0 10.9 %multiply_reduce_fusion.12 = (f32[16,512]{1,0:T(8,128)S(1)}, f32[16,512,512]{1,2,0:T(8,128)}) fusion(f32[16,512,512]{1,2,0:T(8,128)S(1)} %fusion.135, f32[16,512]{1,0:T(8,128)S(1)} %dynamic-slice_bitcast_fusion.9, bf16[2,1,512,16,64]{2,4,3,1,0:T(8,128)(2,1)} %get-tuple-element.401, s32[]{:T(128)} %get-tuple-element.383, ...), kind=kOutput, calls=%fused_computation.20.clone.1 | convolution fusion | flops 553639936 | bytes 35718144 | tf_op jit(solution)/shard_map/while/body/eval_jaxpr/sqhd,skhd->shqk/dot_general | solution.py:54
  499.6 10.6 %multiply_convert_fusion.5 = bf16[16,512,512]{1,2,0:T(8,128)(2,1)} fusion(f32[16,512,512]{1,2,0:T(8,128)} %get-tuple-element.350, f32[16,512,512]{1,2,0:T(8,128)S(1)} %fusion.135, f32[16,512]{1,0:T(8,128)S(1)} %get-tuple-element.351, f32[16,512]{1,0:T(8,128)S(1)} %dynamic-slice_bitcast_fusion.9), kind=kLoop, calls=%fused_computation.19.clone.1 | loop fusion | flops 20971520 | bytes 42008576 | tf_op jit(solution)/shard_map/while/body/eval_jaxpr/convert_element_type | solution.py:58
  510.1 7.5 fusion.137
  520.1 8.5 fusion.138
  528.7 3.9 copy.85
  535.9 3.8 copy.87
  543.4 8.6 convert_bitcast_fusion
  552.0 8.9 copy.97
  560.9 11.4 %add_convert_fusion.1 = bf16[1024,1024]{1,0:T(8,128)(2,1)S(1)} fusion(f32[1024,1024]{1,0:T(8,128)} %copy-done.14, bf16[1024,3072]{0,1:T(8,128)(2,1)} %copy-done.18, bf16[1024,3072]{1,0:T(8,128)(2,1)} %all-gather.9.cloned.1.call-done), kind=kOutput, calls=%fused_computation.91 | convolution fusion | flops 6444548096 | bytes 18874368 | tf_op jit(solution)/shard_map/ne,de->nd/dot_general | solution.py:208
  572.3 3.5 copy.88
  575.8 4.5 all-to-all-start.3
  585.7 3.5 copy.76
  589.1 37.6 %all-to-all-done.3 = bf16[2,512,1024]{2,0,1:T(2,128)(2,1)} async-done(((bf16[2,512,1024]{2,0,1:T(2,128)(2,1)}), bf16[2,512,1024]{2,0,1:T(2,128)(2,1)}, u32[]{:S(2)}, u32[]{:S(2)}) %all-to-all-start.3) | async-done | bytes 2097184 | tf_op jit(solution)/shard_map/all_to_all | solution.py:212
  626.8 3.9 all-to-all-start.1
  630.7 51.7 %reduce-scatter.11.cloned.1.call-done = bf16[128,1024]{1,0:T(8,128)(2,1)} async-done(((bf16[4096,1024]{1,0:T(8,128)(2,1)}), bf16[128,1024]{1,0:T(8,128)(2,1)}) %reduce-scatter.11.cloned.1.call-update) | async-done | bytes 262160 | tf_op jit(solution)/shard_map/reduce_scatter | solution.py:82
  682.6 39.0 %psum.7 = f32[8,1536]{1,0:T(8,128)S(1)} all-reduce(f32[8,1536]{1,0:T(8,128)S(1)} %constant_dynamic-update-slice_fusion.3), channel_id=1, replica_groups=mesh['ctx'=4,'fsdp'=8] {'fsdp','ctx'}, use_global_device_ids=true, to_apply=%region_28.29 | all-reduce | flops 12288 | bytes 98304 | tf_op jit(solution)/shard_map/psum | solution.py:232
  722.9 3.6 copy.89
  728.4 92.5 %reduce-scatter.7.cloned.1.call-done = bf16[32,1024]{1,0:T(8,128)(2,1)} async-done(((bf16[1024,1024]{1,0:T(8,128)(2,1)}), bf16[32,1024]{1,0:T(8,128)(2,1)}) %reduce-scatter.7.cloned.1.call-update) | async-done | bytes 65552 | tf_op jit(solution)/shard_map/reduce_scatter | solution.py:82
  820.9 6.0 all_gather.37
  827.7 110.5 %reduce-scatter.13.cloned.1.call-done = bf16[32,3072]{1,0:T(8,128)(2,1)} async-done(((bf16[1024,3072]{1,0:T(8,128)(2,1)}), bf16[32,3072]{1,0:T(8,128)(2,1)}) %reduce-scatter.13.cloned.1.call-update) | async-done | bytes 196624 | tf_op jit(solution)/shard_map/reduce_scatter | solution.py:82
  938.2 8.9 all_gather.36
  948.4 7.3 all-gather.17.cloned.1.call-done
  955.7 2.8 convert_element_type.271
  958.5 15.4 %all-gather.19.cloned.1.call-done = bf16[512,1024]{1,0:T(8,128)(2,1)} async-done(((bf16[128,1024]{1,0:T(8,128)(2,1)}), bf16[512,1024]{1,0:T(8,128)(2,1)}) %all-gather.19.cloned.1.call-update) | async-done | bytes 1048592 | tf_op jit(solution)/shard_map/all_gather | solution.py:85
  973.9 2.8 convert_element_type.273
  (201 shorter events, 63.5 us)
Async XLA Ops:
  7.2 3.4 copy-start
  7.2 90.4 %all-gather.9.cloned.1.call-start = ((), (), s32[]{:S(2)}) async-start(), calls=%async_computation.8 | async-start | bytes 6488064 | tf_op jit(solution)/shard_map/all_gather | solution.py:78
  9.0 182.8 %all-gather.11.cloned.1.call-start = ((), (), s32[]{:S(2)}) async-start(), calls=%async_computation.9 | async-start | bytes 2162688 | tf_op jit(solution)/shard_map/all_gather | solution.py:78
  10.5 224.9 %all-gather.13.cloned.1.call-start = ((), (), s32[]{:S(2)}) async-start(), calls=%async_computation.10 | async-start | bytes 8650752 | tf_op jit(solution)/shard_map/all_gather | solution.py:78
  11.3 38.5 %copy-start.37 = (bf16[128]{0:T(256)(128)(2,1)S(1)}, bf16[128]{0:T(256)(128)(2,1)}, u32[]{:S(2)}) copy-start(bf16[128]{0:T(256)(128)(2,1)} %param.25) | copy-start | bytes 772
  11.3 38.8 %copy-start.38 = (bf16[128]{0:T(256)(128)(2,1)S(1)}, bf16[128]{0:T(256)(128)(2,1)}, u32[]{:S(2)}) copy-start(bf16[128]{0:T(256)(128)(2,1)} %param.26) | copy-start | bytes 772
  11.3 39.0 %copy-start.39 = (bf16[128]{0:T(256)(128)(2,1)S(1)}, bf16[128]{0:T(256)(128)(2,1)}, u32[]{:S(2)}) copy-start(bf16[128]{0:T(256)(128)(2,1)} %param.27) | copy-start | bytes 772
  11.4 39.2 %copy-start.40 = (bf16[128]{0:T(256)(128)(2,1)S(1)}, bf16[128]{0:T(256)(128)(2,1)}, u32[]{:S(2)}) copy-start(bf16[128]{0:T(256)(128)(2,1)} %param.28) | copy-start | bytes 772
  11.4 39.4 %copy-start.41 = (bf16[128]{0:T(256)(128)(2,1)S(1)}, bf16[128]{0:T(256)(128)(2,1)}, u32[]{:S(2)}) copy-start(bf16[128]{0:T(256)(128)(2,1)} %param.29) | copy-start | bytes 772
  11.4 39.6 %copy-start.36 = (bf16[512]{0:T(512)(128)(2,1)S(1)}, bf16[512]{0:T(512)(128)(2,1)}, u32[]{:S(2)}) copy-start(bf16[512]{0:T(512)(128)(2,1)} %param.30) | copy-start | bytes 3076
  11.4 39.8 %copy-start.42 = (bf16[128]{0:T(256)(128)(2,1)S(1)}, bf16[128]{0:T(256)(128)(2,1)}, u32[]{:S(2)}) copy-start(bf16[128]{0:T(256)(128)(2,1)} %param.31) | copy-start | bytes 772
  11.4 40.0 %copy-start.43 = (bf16[128]{0:T(256)(128)(2,1)S(1)}, bf16[128]{0:T(256)(128)(2,1)}, u32[]{:S(2)}) copy-start(bf16[128]{0:T(256)(128)(2,1)} %param.32) | copy-start | bytes 772
  11.4 40.2 %copy-start.44 = (bf16[128]{0:T(256)(128)(2,1)S(1)}, bf16[128]{0:T(256)(128)(2,1)}, u32[]{:S(2)}) copy-start(bf16[128]{0:T(256)(128)(2,1)} %param.33) | copy-start | bytes 772
  44.4 44.9 %all-to-all-start.2 = ((bf16[8,128,1024]{2,1,0:T(8,128)(2,1)}), bf16[8,128,1024]{2,1,0:T(8,128)(2,1)S(1)}, u32[]{:S(2)}, u32[]{:S(2)}) async-start(bf16[8,128,1024]{2,1,0:T(8,128)(2,1)} %param.20), calls=%async_computation.2 | async-start | bytes 4194304 | tf_op jit(solution)/shard_map/all_to_all | solution.py:134
  48.0 266.8 %all-gather.15.cloned.1.call-start = ((), (), s32[]{:S(2)}) async-start(), calls=%async_computation.11 | async-start | bytes 8650752 | tf_op jit(solution)/shard_map/all_gather | solution.py:78
  49.8 530.6 %reduce-scatter.9.cloned.1.call-start = ((), (), s32[]{:S(2)}) async-start(), calls=%async_computation.13 | async-start | bytes 8650752 | tf_op jit(solution)/shard_map/reduce_scatter | solution.py:82
  86.1 5.9 copy-start.21
  89.3 2.7 copy-start.8
  92.0 5.5 copy-start.15
  185.3 6.4 copy-start.4
  185.3 6.4 copy-start.19
  185.3 6.5 copy-start.33
  197.4 2.0 copy-start.10
  197.5 38.0 %copy-start.23 = (f32[1024]{0:T(1024)S(1)}, f32[1024]{0:T(1024)}, u32[]{:S(2)}) copy-start(f32[1024]{0:T(1024)} %get-tuple-element.238) | copy-start | bytes 12292
  197.5 38.0 %copy-start.30 = (f32[1,4,8,128]{3,1,2,0:T(4,128)S(1)}, f32[1,4,8,128]{3,1,2,0:T(4,128)}, u32[]{:S(2)}) copy-start(f32[1,4,8,128]{3,1,2,0:T(4,128)} %copy.101) | copy-start | bytes 49156
  197.5 37.9 %copy-start.31 = (f32[1024]{0:T(1024)S(1)}, f32[1024]{0:T(1024)}, u32[]{:S(2)}) copy-start(f32[1024]{0:T(1024)} %get-tuple-element.237) | copy-start | bytes 12292
  235.4 79.4 %copy-start.32 = (f32[1024]{0:T(1024)S(1)}, f32[1024]{0:T(1024)}, u32[]{:S(2)}) copy-start(f32[1024]{0:T(1024)} %get-tuple-element.236) | copy-start | bytes 12292
  329.6 2.2 copy-start.7
  329.6 2.2 copy-start.22
  331.8 2.7 copy-start.24
  331.8 2.7 copy-start.28
  379.2 303.2 %reduce-scatter.11.cloned.1.call-start = ((), (), s32[]{:S(2)}) async-start(), calls=%async_computation.15 | async-start | bytes 8650752 | tf_op jit(solution)/shard_map/reduce_scatter | solution.py:82
  394.8 426.1 %reduce-scatter.7.cloned.1.call-start = ((), (), s32[]{:S(2)}) async-start(), calls=%async_computation.12 | async-start | bytes 2162688 | tf_op jit(solution)/shard_map/reduce_scatter | solution.py:82
  394.8 17.5 %copy-start.11 = (f32[1024,1024]{1,0:T(8,128)S(1)}, f32[1024,1024]{1,0:T(8,128)}, u32[]{:S(2)}) copy-start(f32[1024,1024]{1,0:T(8,128)} %copy-done.10) | copy-start | bytes 12582916
  412.3 4.0 copy-start.45
  414.3 2.1 copy-start.14
  422.8 5.6 copy-start.17
  434.3 4.8 copy-start.20
  434.4 503.8 %reduce-scatter.13.cloned.1.call-start = ((), (), s32[]{:S(2)}) async-start(), calls=%async_computation.17 | async-start | bytes 6488064 | tf_op jit(solution)/shard_map/reduce_scatter | solution.py:82
  443.5 11.6 %copy-start.2 = (f32[16,512,512]{1,2,0:T(8,128)}, f32[16,512,512]{1,2,0:T(8,128)S(1)}, u32[]{:S(2)}) copy-start(f32[16,512,512]{1,2,0:T(8,128)S(1)} %fusion.135) | copy-start | bytes 50331652 | tf_op jit(solution)/shard_map/while
  465.7 7.5 copy-start.3
  465.7 7.5 copy-start.5
  473.2 2.4 copy-start.6
  488.0 11.6 %copy-start.2 = (f32[16,512,512]{1,2,0:T(8,128)}, f32[16,512,512]{1,2,0:T(8,128)S(1)}, u32[]{:S(2)}) copy-start(f32[16,512,512]{1,2,0:T(8,128)S(1)} %fusion.135) | copy-start | bytes 50331652 | tf_op jit(solution)/shard_map/while
  510.1 7.5 copy-start.3
  510.1 7.5 copy-start.5
  517.6 2.4 copy-start.6
  528.7 4.5 copy-start.12
  540.5 2.9 copy-start.16
  540.8 2.6 copy-start.18
  572.3 8.7 copy-start.9
  575.8 51.0 %all-to-all-start.3 = ((bf16[2,512,1024]{2,0,1:T(2,128)(2,1)}), bf16[2,512,1024]{2,0,1:T(2,128)(2,1)}, u32[]{:S(2)}, u32[]{:S(2)}) async-start(bf16[2,512,1024]{2,0,1:T(2,128)(2,1)} %copy.88), calls=%async_computation.3 | async-start | bytes 4194304 | tf_op jit(solution)/shard_map/all_to_all | solution.py:212
  580.3 375.4 %all-gather.17.cloned.1.call-start = ((), (), s32[]{:S(2)}) async-start(), calls=%async_computation.14 | async-start | bytes 1310720 | tf_op jit(solution)/shard_map/all_gather | solution.py:85
  581.4 4.2 copy-start.13
  585.6 45.1 %copy-start.27 = (f32[1024]{0:T(1024)S(1)}, f32[1024]{0:T(1024)}, u32[]{:S(2)}) copy-start(f32[1024]{0:T(1024)} %get-tuple-element.215) | copy-start | bytes 12292
  585.6 96.8 %copy-start.35 = (f32[1024]{0:T(1024)S(1)}, f32[1024]{0:T(1024)}, u32[]{:S(2)}) copy-start(f32[1024]{0:T(1024)} %get-tuple-element.179) | copy-start | bytes 12292
  585.6 96.8 %copy-start.29 = (f32[4096]{0:T(1024)S(1)}, f32[4096]{0:T(1024)}, u32[]{:S(2)}) copy-start(f32[4096]{0:T(1024)} %get-tuple-element.248) | copy-start | bytes 49156
  585.6 96.9 %copy-start.34 = (f32[1024]{0:T(1024)S(1)}, f32[1024]{0:T(1024)}, u32[]{:S(2)}) copy-start(f32[1024]{0:T(1024)} %get-tuple-element.182) | copy-start | bytes 12292
  585.6 96.9 %copy-start.26 = (f32[1024]{0:T(1024)S(1)}, f32[1024]{0:T(1024)}, u32[]{:S(2)}) copy-start(f32[1024]{0:T(1024)} %get-tuple-element.213) | copy-start | bytes 12292
  585.6 96.9 %copy-start.25 = (f32[1024]{0:T(1024)S(1)}, f32[1024]{0:T(1024)}, u32[]{:S(2)}) copy-start(f32[1024]{0:T(1024)} %get-tuple-element.177) | copy-start | bytes 12292
  626.8 99.7 %all-to-all-start.1 = ((bf16[2,512,1024]{2,0,1:T(2,128)(2,1)}), bf16[2,512,1024]{2,0,1:T(2,128)(2,1)S(1)}, u32[]{:S(2)}, u32[]{:S(2)}) async-start(bf16[2,512,1024]{2,0,1:T(2,128)(2,1)} %copy.76), calls=%async_computation.1 | async-start | bytes 4194304 | tf_op jit(solution)/shard_map/all_to_all | solution.py:212
  630.7 343.2 %all-gather.19.cloned.1.call-start = ((), (), s32[]{:S(2)}) async-start(), calls=%async_computation.16 | async-start | bytes 1310720 | tf_op jit(solution)/shard_map/all_gather | solution.py:85
  938.2 38.5 %copy-start.1 = (bf16[128,4096]{1,0:T(8,128)(2,1)S(1)}, bf16[128,4096]{1,0:T(8,128)(2,1)}, u32[]{:S(2)}) copy-start(bf16[128,4096]{1,0:T(8,128)(2,1)} %param.23) | copy-start | bytes 3145732
Sparse Core Ops, SparseCore 0:
  11.5 86.0 all-gather.8
  100.4 55.1 all-gather.10
  159.1 76.3 all-gather.12
  238.7 76.0 all-gather.14
  379.3 147.3 reduce-scatter.8
  528.9 153.4 reduce-scatter.10
  684.7 136.1 reduce-scatter.6
  827.5 110.6 reduce-scatter.12
  939.8 15.8 all-gather.16
  957.1 16.7 all-gather.18

commit v2 on v1

v2 whole, which is shorter than its diff:
```python
import functools
import math

import jax
import jax.numpy as jnp
from jax import lax
from jax.experimental import pallas as pl
from jax.experimental.pallas import tpu as pltpu
from jax.sharding import PartitionSpec as P

HEAD = 64
EPSILON = 1e-05
LOW = jnp.bfloat16
WIDE = jnp.float32
NN = (((1,), (0,)), ((), ()))
NT = (((1,), (1,)), ((), ()))
TN = (((0,), (0,)), ((), ()))
PAD = 16


def dot(left, right, dims):
    return lax.dot_general(left, right, dims, preferred_element_type=WIDE)


def cost(flops, moved):
    scale = 16
    return pl.CostEstimate(
        flops=int(flops) // scale, bytes_accessed=int(moved) // scale, transcendentals=0
    )


def params(mib):
    return pltpu.CompilerParams(vmem_limit_bytes=mib << 20)


def struct(shape, dtype=LOW):
    return jax.ShapeDtypeStruct(tuple(shape), dtype)


def bits_of(size):
    return size.bit_length() - 1


ANYWHERE = pl.BlockSpec(memory_space=pl.ANY)


def placed(index, order):
    out = 0
    for bit in order:
        out = out * 2 + (index // 2**bit) % 2
    return out


def fetch(held_ref, parts, ranks, moves):
    for rank in range(ranks):

        def step(part, carry):
            for first, place, sem in moves:
                target = place(part, rank)
                source = held_ref.at[part * ranks + rank].at[:, pl.ds(first, target.shape[1])]
                pltpu.make_async_copy(source, target, sem).start()
            return carry

        lax.fori_loop(0, parts, step, 0)


def landed(target, sem):
    pltpu.make_async_copy(target, target, sem).wait()


def ds(index, size):
    return pl.ds(pl.multiple_of(index * size, size), size)


def fetch_input(held_ref, weight, sem, parts, ranks):
    width = weight.shape[0]
    rows, columns = width // parts, 3 * width // ranks

    def place(part, rank):
        return weight.at[ds(part, rows), pl.ds(rank * columns, columns)]

    fetch(held_ref, parts, ranks, [(0, place, sem)])
    landed(weight, sem)


def merge_kernel(tok_ref, bias_ref, held_ref, *refs, parts, ranks):
    q_ref, k_ref, v_ref, weight, sem = refs[-5:]
    width = tok_ref.shape[1]

    @pl.when(pl.program_id(0) == 0)
    def _():
        fetch_input(held_ref, weight, sem, parts, ranks)

    rows = tok_ref[...]
    for at, out in enumerate((q_ref, k_ref, v_ref)):
        value = dot(rows, weight[:, at * width : (at + 1) * width], NN)
        if at != 1:
            value = value + bias_ref[at : at + 1, :].astype(WIDE)
        out[...] = value.astype(LOW)


def merge(tok, held, bias, parts, ranks, after, tile=256):
    rows, width = tok.shape
    row = pl.BlockSpec((tile, width), lambda i: (i, 0))
    return pl.pallas_call(
        functools.partial(merge_kernel, parts=parts, ranks=ranks),
        grid=(rows // tile,),
        in_specs=[row, pl.BlockSpec(bias.shape, lambda i: (0, 0))]
        + [ANYWHERE] * (1 + len(after)),
        out_specs=[row] * 3,
        out_shape=[struct(tok.shape)] * 3,
        scratch_shapes=[pltpu.VMEM((width, 3 * width), LOW), pltpu.SemaphoreType.DMA],
        compiler_params=params(60),
        cost_estimate=cost(6 * rows * width * width, 14 * rows * width),
        name="merge",
    )(tok, bias, held, *after)


def attend_forward_kernel(q_ref, k_ref, v_ref, o_ref):
    shape = o_ref.shape
    query, keys, values = [ref[...].reshape(-1, 2 * HEAD) for ref in (q_ref, k_ref, v_ref)]
    first = lax.broadcasted_iota(jnp.int32, query.shape, 1) < HEAD
    zero = jnp.zeros_like(query)
    outs = []
    for one in (jnp.where(first, query, zero), jnp.where(first, zero, query)):
        scores = dot(one, keys, NT)
        peak = jnp.max(scores, axis=1, keepdims=True)
        raised = jnp.exp((scores - peak) * (1.0 / math.sqrt(HEAD)))
        total = jnp.sum(raised, axis=1, keepdims=True)
        outs.append(dot(raised.astype(LOW), values, NN) * (1.0 / total))
    o_ref[...] = jnp.where(first, outs[0], outs[1]).astype(LOW).reshape(shape)


def head_spec(shape):
    pieces, _, length, _ = shape
    return pl.BlockSpec((pieces, 1, length, 2 * HEAD), lambda s, h: (0, s, 0, h))


def attend_forward(query, keys, values, shape):
    spec = head_spec(shape)
    rows = math.prod(shape[:3])
    area = rows * shape[0] * shape[2] * shape[3]
    return pl.pallas_call(
        attend_forward_kernel,
        grid=(shape[1], shape[3] // (2 * HEAD)),
        in_specs=[spec] * 3,
        out_specs=spec,
        out_shape=struct(shape),
        compiler_params=params(60),
        cost_estimate=cost(16 * area, 8 * rows * shape[3]),
        name="attend_forward",
    )(*[member.reshape(shape) for member in (query, keys, values)])


def attend_backward_kernel(q_ref, k_ref, v_ref, c_ref, *refs):
    dq_ref, dk_ref, dv_ref, qs_ref, vs_ref, mark_ref = refs[-6:]
    mark_ref[...] = jnp.zeros_like(mark_ref)
    shape = dq_ref.shape
    query, keys, values, d_context = [
        ref[...].reshape(-1, 2 * HEAD) for ref in (q_ref, k_ref, v_ref, c_ref)
    ]
    first = lax.broadcasted_iota(jnp.int32, query.shape, 1) < HEAD
    zero = jnp.zeros_like(query)
    factor = 1.0 / math.sqrt(HEAD)
    outs = []
    for head in range(2):

        def only(value):
            return jnp.where(first, value, zero) if head == 0 else jnp.where(first, zero, value)

        scores = dot(keys, only(query), NT)
        peak = jnp.max(scores, axis=0, keepdims=True)
        raised = jnp.exp((scores - peak) * factor)
        probs = raised * (1.0 / jnp.sum(raised, axis=0, keepdims=True))
        d_probs = dot(values, only(d_context), NT)
        product = probs * d_probs
        d_scores = (product - probs * jnp.sum(product, axis=0, keepdims=True)).astype(LOW)
        outs.append(
            (
                dot(d_scores, keys, TN),
                dot(d_scores, query, NN),
                dot(probs.astype(LOW), d_context, NN),
            )
        )
    d_query = (jnp.where(first, outs[0][0], outs[1][0]) * factor).astype(LOW)
    d_keys = (jnp.where(first, outs[0][1], outs[1][1]) * factor).astype(LOW)
    d_values = jnp.where(first, outs[0][2], outs[1][2]).astype(LOW)
    dq_ref[...] = d_query.reshape(shape)
    dk_ref[...] = d_keys.reshape(shape)
    dv_ref[...] = d_values.reshape(shape)
    for value, out in ((d_query, qs_ref), (d_values, vs_ref)):
        total = jnp.sum(value.astype(WIDE), axis=0, keepdims=True)
        out[...] = jnp.broadcast_to(total, (8, 2 * HEAD))


def attend_backward(query, keys, values, d_context, shape, share, begun, after):
    pieces, count, length, width = shape
    pairs = width // (2 * HEAD) // 2
    sequence, first = share // 2, share % 2 * pairs
    spec = pl.BlockSpec((pieces, 1, length, 2 * HEAD), lambda h: (0, sequence, 0, first + h))
    sums = pl.BlockSpec((8, 2 * HEAD), lambda h: (sequence, first + h))
    rows = math.prod(shape[:3])
    area = rows * pieces * length * width // count // 2
    return pl.pallas_call(
        attend_backward_kernel,
        grid=(pairs,),
        in_specs=[spec] * 4 + [ANYWHERE] * (len(begun) + len(after)),
        out_specs=[spec] * 3 + [sums] * 2 + [pl.BlockSpec((8, 2 * HEAD), lambda h: (0, 0))],
        out_shape=[struct(shape)] * 3
        + [struct((8 * count, width), WIDE)] * 2
        + [struct((8, 2 * HEAD), WIDE)],
        input_output_aliases={4 + at: at for at in range(len(begun))},
        compiler_params=params(60),
        cost_estimate=cost(40 * area, 14 * rows * width // count),
        name="attend_backward",
    )(*[member.reshape(shape) for member in (query, keys, values, d_context)], *begun, *after)


def gelu_and_slope(value):
    raised = jnp.exp(value * value * -0.5)
    at = 1.0 / (1.0 + (0.3275911 * math.sqrt(0.5)) * jnp.abs(value))
    series = 0.5 * -1.453152027 + at * (0.5 * 1.061405429)
    for term in (1.421413741, -0.284496736, 0.254829592):
        series = 0.5 * term + at * series
    tail = at * series * raised
    below = jnp.where(value >= 0, 1.0 - tail, tail)
    return value * below, below + value * raised * (1.0 / math.sqrt(2.0 * math.pi))


def mean(value):
    return jnp.mean(value, axis=1, keepdims=True)


def total(value):
    return jnp.sum(value, axis=0, keepdims=True)


def norm_forward(value):
    centre = value - mean(value)
    inverse = lax.rsqrt(mean(centre * centre) + EPSILON)
    return centre * inverse, inverse


def norm_backward(upstream, normed, inverse, gain):
    scaled = upstream * gain
    return inverse * (scaled - mean(scaled) - normed * mean(scaled * normed))


def middle_kernel(
    context_ref,
    tok_ref,
    cot_ref,
    vector_ref,
    up_bias_ref,
    *refs,
    parts,
    ranks,
    chunk,
):
    held_ref, refs = refs[0], refs[-15:]
    (
    out_ref,
    hidden_ref,
    active_ref,
    d_branch_ref,
    d_inner_ref,
    d_attn_ref,
    d_context_ref,
    d_pre_ref,
    sums_ref,
    up_sums_ref,
    output_weight,
    up_weight,
    down_weight,
    slope_ref,
    sems,
    ) = refs
    width, inner_width = up_weight.shape
    start = pl.program_id(0) == 0

    @pl.when(start)
    def _():
        own = width // parts
        span, narrow = inner_width // ranks, width // ranks
        fetch(
            held_ref,
            parts,
            ranks,
            [
                (
                    span,
                    lambda part, rank: output_weight.at[
                        ds(part, own), pl.ds(rank * narrow, narrow)
                    ],
                    sems.at[0],
                ),
                (
                    0,
                    lambda part, rank: up_weight.at[ds(part, own), pl.ds(rank * span, span)],
                    sems.at[1],
                ),
                (
                    span + narrow,
                    lambda part, rank: down_weight.at[ds(part * ranks + rank, own), :],
                    sems.at[2],
                ),
            ],
        )
        sums_ref[...] = jnp.zeros_like(sums_ref)
        up_sums_ref[...] = jnp.zeros_like(up_sums_ref)
        landed(output_weight, sems.at[0])

    output_bias, norm_gain, norm_shift, down_bias, final_gain, final_shift = [
        vector_ref[at : at + 1, :].astype(WIDE) for at in range(2, 8)
    ]
    pre_one = (
        tok_ref[...].astype(WIDE) + dot(context_ref[...], output_weight[...], NN) + output_bias
    )
    normed_one, inverse_one = norm_forward(pre_one)
    hidden = normed_one * norm_gain + norm_shift
    hidden_low = hidden.astype(LOW)
    hidden_ref[...] = hidden_low

    @pl.when(start)
    def _():
        landed(up_weight, sems.at[1])
        landed(down_weight, sems.at[2])

    branch = hidden + down_bias
    for at in range(0, inner_width, chunk):
        span = slice(at, at + chunk)
        inner = dot(hidden_low, up_weight[:, span], NN) + up_bias_ref[:, span].astype(WIDE)
        active, slope = gelu_and_slope(inner)
        active = active.astype(LOW)
        active_ref[:, span] = active
        slope_ref[:, span] = slope
        branch = branch + dot(active, down_weight[span, :], NN)
    normed_two, inverse_two = norm_forward(branch)
    out_ref[...] = (normed_two * final_gain + final_shift).astype(LOW)
    upstream = cot_ref[...].astype(WIDE)
    d_pre_two = norm_backward(upstream, normed_two, inverse_two, final_gain)
    d_branch = d_pre_two.astype(LOW)
    d_branch_ref[...] = d_branch
    d_hidden = d_pre_two
    for at in range(0, inner_width, chunk):
        span = slice(at, at + chunk)
        d_inner = (dot(d_branch, down_weight[span, :], NT) * slope_ref[:, span]).astype(LOW)
        d_inner_ref[:, span] = d_inner
        up_sums_ref[:, span] += total(d_inner.astype(WIDE))
        d_hidden = d_hidden + dot(d_inner, up_weight[:, span], NT)
    d_pre_one = norm_backward(d_hidden, normed_one, inverse_one, norm_gain)
    d_attn = d_pre_one.astype(LOW)
    d_attn_ref[...] = d_attn
    d_pre_ref[...] = d_pre_one
    d_context_ref[...] = dot(d_attn, output_weight[...], NT).astype(LOW)
    sums = (
        d_pre_one,
        d_hidden * normed_one,
        d_hidden,
        d_pre_two,
        upstream * normed_two,
        upstream,
    )
    for at, value in enumerate(sums):
        sums_ref[at : at + 1, :] += total(value)


def middle(context, tok, cot, held, vectors, up_bias, parts, ranks, tile=256):
    rows, width = tok.shape
    inner_width = up_bias.shape[1]
    row = pl.BlockSpec((tile, width), lambda i: (i, 0))
    broad = pl.BlockSpec((tile, inner_width), lambda i: (i, 0))

    def whole(shape):
        return pl.BlockSpec(shape, lambda i: (0, 0))

    low, deep = struct((rows, width)), struct((rows, inner_width))
    return pl.pallas_call(
        functools.partial(middle_kernel, parts=parts, ranks=ranks, chunk=1024),
        grid=(rows // tile,),
        in_specs=[row] * 3 + [whole(vectors.shape), whole(up_bias.shape), ANYWHERE],
        out_specs=[row, row, broad, row, broad, row, row, row]
        + [whole((8, width)), whole((1, inner_width))],
        scratch_shapes=[
            pltpu.VMEM((width, width), LOW),
            pltpu.VMEM((width, inner_width), LOW),
            pltpu.VMEM((inner_width, width), LOW),
            pltpu.VMEM((tile, inner_width), WIDE),
            pltpu.SemaphoreType.DMA((3,)),
        ],
        out_shape=[low, low, deep, low, deep, low, low, struct((rows, width), WIDE)]
        + [struct((8, width), WIDE), struct((1, inner_width), WIDE)],
        compiler_params=params(60),
        cost_estimate=cost(
            4 * rows * width * (2 * inner_width + width), 18 * width * inner_width * rows // 1024
        ),
        name="middle",
    )(context, tok, cot, vectors, up_bias, held)


def down_grad_kernel(half_ref, near_ref, far_ref, active_ref, *refs):
    out_near, out_far, turned = refs[-3:]
    columns = near_ref.shape[1]

    @pl.when(pl.program_id(0) == 0)
    def _():
        turned[:columns] = near_ref[...].T
        turned[columns:] = far_ref[...].T

    group, _, _, deep = out_near.shape
    result = dot(turned[...], active_ref[...], NN).astype(LOW)
    for part in range(group):
        at = placed(part, range(bits_of(group)))
        span = slice(part * deep, (part + 1) * deep)
        out_near[at, 0] = result[:columns, span]
        out_far[at, 0] = result[columns:, span]


def down_grad(half, active, d_branch, parts, order, after):
    rows, inner_width = active.shape
    columns = d_branch.shape[1] // 2
    deep = inner_width // parts
    group = max(1, 1024 // deep)
    steps = parts // group
    low = bits_of(group)
    order = tuple(range(low)) + tuple(bit for bit in order if bit >= low)
    high = [bit - low for bit in order[low:]]
    out = pl.BlockSpec((group, 1, columns, deep), lambda i, half: (0, placed(i, high), 0, 0))
    near, far = pl.pallas_call(
        down_grad_kernel,
        grid_spec=pltpu.PrefetchScalarGridSpec(
            num_scalar_prefetch=1,
            grid=(steps,),
            in_specs=[
                pl.BlockSpec((rows, columns), lambda i, half: (0, half[0])),
                pl.BlockSpec((rows, columns), lambda i, half: (0, 1 - half[0])),
                pl.BlockSpec((rows, group * deep), lambda i, half: (0, i)),
            ]
            + [ANYWHERE] * len(after),
            out_specs=[out, out],
            scratch_shapes=[pltpu.VMEM((2 * columns, rows), LOW)],
        ),
        out_shape=[struct((group, steps, columns, deep))] * 2,
        compiler_params=params(60),
        cost_estimate=cost(4 * rows * inner_width * columns, 4 * rows * inner_width),
        name="down_grad",
    )(half, d_branch, d_branch, active, *after)
    return near.reshape(parts, columns, deep), far.reshape(parts, columns, deep), order


def spread(result, out_ref, order):
    rows = result.shape[0] // 2 ** len(order)
    for part in range(2 ** len(order)):
        out_ref[placed(part, order)] = result[part * rows : (part + 1) * rows]


def output_grad_kernel(half_ref, context_ref, *refs, order, chips):
    grads, (far_ref, near_ref, turned) = refs[:2], refs[-3:]
    at = pl.program_id(0)

    @pl.when(at == 0)
    def _():
        turned[...] = context_ref[...].T
        spread(dot(turned[...], grads[0][...], NN).astype(LOW), far_ref.at[0], order)

    for chip in range(chips):
        for side, out_ref in ((0, far_ref), (1, near_ref)):
            if chip + side > 0:

                @pl.when(at == side * chips + chip)
                def _():
                    spread(dot(turned[...], grads[side][...], NN).astype(LOW), out_ref.at[0], order)


def output_grad(half, context, d_attn, near, far, parts, ranks, order, after):
    rows, width = context.shape
    chips, narrow, own = ranks // 2, width // ranks, width // parts
    shape = (chips, parts, own, near.shape[2])
    last = shape[3] // narrow - 1
    block = (1, parts, own, narrow)

    def far_at(i):
        return jnp.minimum(i, chips - 1)

    def near_at(i):
        return jnp.maximum(i - chips, 0)

    far, near = pl.pallas_call(
        functools.partial(output_grad_kernel, order=order, chips=chips),
        grid_spec=pltpu.PrefetchScalarGridSpec(
            num_scalar_prefetch=1,
            grid=(ranks,),
            in_specs=[
                pl.BlockSpec((rows, width), lambda i, half: (0, 0)),
                pl.BlockSpec((rows, narrow), lambda i, half: (0, 2 * far_at(i) + 1 - half[0])),
                pl.BlockSpec((rows, narrow), lambda i, half: (0, 2 * near_at(i) + half[0])),
            ]
            + [ANYWHERE] * (2 + len(after)),
            out_specs=[
                pl.BlockSpec(block, lambda i, half: (far_at(i), 0, 0, last)),
                pl.BlockSpec(block, lambda i, half: (near_at(i), 0, 0, last)),
            ],
            scratch_shapes=[pltpu.VMEM((width, rows), LOW)],
        ),
        out_shape=[struct(shape)] * 2,
        input_output_aliases={4: 0, 5: 1},
        compiler_params=params(40),
        cost_estimate=cost(2 * rows * width * width, 6 * rows * width),
        name="output_grad",
    )(half, context, d_attn, d_attn, far.reshape(shape), near.reshape(shape), *after)
    return [member.reshape(-1, own, shape[3]) for member in (near, far)]


def up_grad_kernel(half_ref, hidden_ref, grad_ref, *refs, order, chips):
    far_ref, near_ref, turned = refs[-3:]
    at = pl.program_id(0)

    @pl.when(at == 0)
    def _():
        turned[...] = hidden_ref[...].T

    for first, out_ref in ((0, far_ref), (chips, near_ref)):

        @pl.when((at >= first) & (at < first + chips))
        def _():
            spread(dot(turned[...], grad_ref[...], NN).astype(LOW), out_ref.at[0], order)


def up_grad(half, hidden_low, d_inner, parts, ranks, order, extra, after):
    rows, width = hidden_low.shape
    columns = d_inner.shape[1] // ranks
    chips = ranks // 2

    def column(i, half):
        far = i < chips
        return 0, jnp.where(far, 2 * i + 1 - half[0], 2 * (i - chips) + half[0])

    block = (1, parts, width // parts, columns)
    far, near = pl.pallas_call(
        functools.partial(up_grad_kernel, order=order, chips=chips),
        grid_spec=pltpu.PrefetchScalarGridSpec(
            num_scalar_prefetch=1,
            grid=(ranks,),
            in_specs=[
                pl.BlockSpec((rows, width), lambda i, half: (0, 0)),
                pl.BlockSpec((rows, columns), column),
            ]
            + [ANYWHERE] * len(after),
            out_specs=[
                pl.BlockSpec(block, lambda i, half: (jnp.minimum(i, chips - 1), 0, 0, 0)),
                pl.BlockSpec(block, lambda i, half: (jnp.maximum(i - chips, 0), 0, 0, 0)),
            ],
            scratch_shapes=[pltpu.VMEM((width, rows), LOW)],
        ),
        out_shape=[struct((chips,) + block[1:3] + (columns + extra,))] * 2,
        compiler_params=params(60),
        cost_estimate=cost(2 * rows * width * columns * ranks, 4 * rows * columns * ranks),
        name="up_grad",
    )(half, hidden_low, d_inner, *after)
    return [member.reshape(-1, width // parts, columns + extra) for member in (near, far)]


def input_grad_kernel(half_ref, tok_ref, *refs, order, chips):
    grads, outs, turned = refs[:6], refs[-5:-1], refs[-1]
    at = pl.program_id(0)

    @pl.when(at == 0)
    def _():
        turned[...] = tok_ref[...].T

    for side in range(2):
        for step in range(2 + chips):

            @pl.when(at == side * (2 + chips) + step)
            def _():
                grad_ref = grads[3 * side + min(step, 2)]
                out_ref = outs[2 * side] if step < 2 else outs[2 * side + 1].at[0]
                spread(dot(turned[...], grad_ref[...], NN).astype(LOW), out_ref, order)


def input_grad(half, tok, d_query, d_values, d_keys, parts, ranks, order, after):
    rows, width = tok.shape
    columns, narrow = width // 2, width // ranks
    own = width // parts
    chips = ranks // 2
    steps = 2 + chips

    def key_at(i, side):
        return jnp.clip(i - side * steps - 2, 0, chips - 1)

    ins, out_specs, outs = [], [], []
    for side in range(2):

        def core(half, side=side):
            return half[0] if side else 1 - half[0]

        ins += [pl.BlockSpec((rows, columns), lambda i, half, core=core: (0, core(half)))] * 2
        ins += [
            pl.BlockSpec(
                (rows, narrow),
                lambda i, half, core=core, side=side: (0, 2 * key_at(i, side) + core(half)),
            )
        ]
        out_specs += [
            pl.BlockSpec(
                (parts, own, columns),
                lambda i, half, side=side: (0, jnp.clip(i - side * steps, 0, 1), 0),
            ),
            pl.BlockSpec(
                (1, parts, own, narrow), lambda i, half, side=side: (key_at(i, side), 0, 0, 0)
            ),
        ]
        outs += [struct((parts, 2 * own + PAD, columns)), struct((chips, parts, own, narrow))]
    far, far_keys, near, near_keys = pl.pallas_call(
        functools.partial(input_grad_kernel, order=order, chips=chips),
        grid_spec=pltpu.PrefetchScalarGridSpec(
            num_scalar_prefetch=1,
            grid=(2 * steps,),
            in_specs=[pl.BlockSpec((rows, width), lambda i, half: (0, 0))]
            + ins
            + [ANYWHERE] * len(after),
            out_specs=out_specs,
            scratch_shapes=[pltpu.VMEM((width, rows), LOW)],
        ),
        out_shape=outs,
        compiler_params=params(40),
        cost_estimate=cost(6 * rows * width * width, 10 * rows * width),
        name="input_grad",
    )(half, tok, *[d_query, d_values, d_keys] * 2, *after)
    shape = (-1, own, narrow)
    return near, far, near_keys.reshape(shape), far_keys.reshape(shape)


def tokens_grad_kernel(d_pre_ref, dq_ref, dk_ref, dv_ref, held_ref, *refs, parts, ranks):
    out_ref, weight, sem = refs[-3:]
    width = d_pre_ref.shape[1]

    @pl.when(pl.program_id(0) == 0)
    def _():
        fetch_input(held_ref, weight, sem, parts, ranks)

    value = d_pre_ref[...]
    for at, ref in enumerate((dq_ref, dk_ref, dv_ref)):
        value = value + dot(ref[...], weight[:, at * width : (at + 1) * width], NT)
    out_ref[...] = value.astype(LOW)


def tokens_grad_of(d_pre_one, grads, held, parts, ranks, after, tile=256):
    rows, width = d_pre_one.shape
    row = pl.BlockSpec((tile, width), lambda i: (i, 0))
    return pl.pallas_call(
        functools.partial(tokens_grad_kernel, parts=parts, ranks=ranks),
        grid=(rows // tile,),
        in_specs=[row] * 4 + [ANYWHERE] * (1 + len(after)),
        out_specs=row,
        out_shape=struct((rows, width)),
        scratch_shapes=[pltpu.VMEM((width, 3 * width), LOW), pltpu.SemaphoreType.DMA],
        compiler_params=params(40),
        cost_estimate=cost(6 * rows * width * width, 18 * rows * width),
        name="tokens_grad",
    )(d_pre_one, *grads, held, *after)


def swap(value, axis, bit):
    count = lax.axis_size(axis)
    return lax.ppermute(value, axis, [(at, at ^ (1 << bit)) for at in range(count)])


def bit_of(axis, bit):
    return (lax.axis_index(axis) // (1 << bit)) % 2


def pick_kernel(pick_ref, spot_ref, *refs, count):
    out_ref = refs[-1]
    for piece in range(count):

        @pl.when(pl.program_id(0) == piece)
        def _():
            out_ref[...] = refs[piece][...]


def pick(arrays, picks, spots, after):
    count = len(arrays)
    block = (1,) + arrays[0].shape[1:]
    rest = (0,) * (len(block) - 1)
    return pl.pallas_call(
        functools.partial(pick_kernel, count=count),
        grid_spec=pltpu.PrefetchScalarGridSpec(
            num_scalar_prefetch=2,
            grid=(count,),
            in_specs=[
                pl.BlockSpec(block, lambda i, picks, spots, at=at: (picks[at],) + rest)
                for at in range(count)
            ]
            + [ANYWHERE] * len(after),
            out_specs=pl.BlockSpec(block, lambda i, picks, spots: (spots[i],) + rest),
        ),
        out_shape=struct((count,) + block[1:]),
        compiler_params=params(40),
        cost_estimate=cost(0, 4 * count * math.prod(block)),
        name="pick",
    )(jnp.stack([jnp.int32(at) for at in picks]), spots, *arrays, *after)


def settle_kernel(side_ref, keep_ref, keep_far, came_ref, came_far, *refs):
    out_ref, send_ref = refs[-2:]
    send_ref[...] = (keep_far[...].astype(WIDE) + came_far[...].astype(WIDE)).astype(LOW)
    out_ref[...] = (keep_ref[...].astype(WIDE) + came_ref[...].astype(WIDE)).astype(LOW)


def settle(keep, came, side, after):
    half = keep.shape[0] // 2
    block = (1,) + keep.shape[1:]
    near = pl.BlockSpec(block, lambda i, side: (side[0] * half + i, 0, 0))
    far = pl.BlockSpec(block, lambda i, side: ((1 - side[0]) * half + i, 0, 0))
    out = pl.BlockSpec(block, lambda i, side: (i, 0, 0))
    return pl.pallas_call(
        settle_kernel,
        grid_spec=pltpu.PrefetchScalarGridSpec(
            num_scalar_prefetch=1,
            grid=(half,),
            in_specs=[near, far, near, far] + [ANYWHERE] * len(after),
            out_specs=[out, out],
        ),
        out_shape=[struct((half,) + keep.shape[1:])] * 2,
        compiler_params=params(40),
        cost_estimate=cost(0, 6 * math.prod(keep.shape)),
        name="settle",
    )(side, keep, keep, came, came, *after)


def plus_kernel(left_ref, right_ref, *refs):
    refs[-1][...] = (left_ref[...].astype(WIDE) + right_ref[...].astype(WIDE)).astype(LOW)


def plus(left, right, after):
    spec = pl.BlockSpec(left.shape, lambda i: (0, 0, 0))
    return pl.pallas_call(
        plus_kernel,
        grid=(1,),
        in_specs=[spec, spec] + [ANYWHERE] * len(after),
        out_specs=spec,
        out_shape=struct(left.shape),
        compiler_params=params(40),
        cost_estimate=cost(0, 6 * math.prod(left.shape)),
        name="plus",
    )(left, right, *after)


class Order:
    def __init__(self):
        self.after = ()

    def __call__(self, kernel, *args):
        out = kernel(*args, self.after)
        self.after = (out[-1] if isinstance(out, (tuple, list)) else out,)
        return out


class Reduce:
    def __init__(self, order, route, keep, send):
        self.order, self.route = order, list(route)
        self.keep = keep
        self.came = swap(send, "ctx", 0)

    def step(self):
        axis, bit = self.route.pop(0)
        if self.keep.shape[0] == 1:
            self.keep = self.order(plus, self.keep, self.came)
            self.came = swap(self.keep, axis, bit)
            return
        side = bit_of(axis, bit).reshape(1)
        self.keep, send = self.order(settle, self.keep, self.came, side)
        self.came = swap(send, axis, bit)

    def last(self):
        self.keep = self.order(plus, self.keep, self.came)
        return self.keep[0]


def both(value, axis, bit):
    other = swap(value, axis, bit)
    upper = bit_of(axis, bit) == 1
    return jnp.where(upper, other, value), jnp.where(upper, value, other)


class Sequences:
    def __init__(self, order, value):
        self.order, self.core, self.chip = order, bit_of("ctx", 0), bit_of("ctx", 1)
        self.blocks = value.reshape((4, value.shape[0] // 4) + value.shape[1:])
        send = lax.dynamic_slice_in_dim(self.blocks, 2 * (1 - self.chip), 2, 0)
        self.came = swap(send, "ctx", 1)

    def step(self):
        picks = (2 * self.chip + 1 - self.core, 1 - self.core)
        spots = jnp.arange(2, dtype=jnp.int32)
        self.late = swap(self.order(pick, (self.blocks, self.came), picks, spots), "ctx", 0)

    def last(self):
        arrays = (self.blocks, self.late, self.came, self.late)
        picks = (2 * self.chip + self.core, 0, self.core, 1)
        return self.order(pick, arrays, picks, jnp.arange(4, dtype=jnp.int32))


class Positions:
    def __init__(self, order, value):
        self.order, self.value = order, value
        spots = jnp.arange(2, dtype=jnp.int32)
        self.came = swap(order(pick, (value, value), (2, 3), spots), "ctx", 1)

    def step(self):
        spots = jnp.arange(2, dtype=jnp.int32)
        self.late = swap(self.order(pick, (self.value, self.came), (1, 1), spots), "ctx", 0)

    def last(self):
        arrays = (self.value, self.late, self.came, self.late)
        around = lax.axis_index("ctx") ^ jnp.arange(4, dtype=jnp.int32)
        return self.order(pick, arrays, (0, 0, 0, 1), around)


def packed(values, parts, order, columns):
    joined = jnp.concatenate(values, axis=1)
    length = joined.shape[1]
    bits = bits_of(parts)
    joined = joined.reshape((2,) * bits + (length,))
    joined = joined.transpose(tuple(bits - 1 - bit for bit in order) + (bits,))
    joined = jnp.pad(joined.reshape(parts, length), ((0, 0), (0, 2 * PAD * columns - length)))
    return joined.astype(LOW).reshape(parts, 2, PAD, columns)


def local(
    tokens,
    cotangent,
    input_weight,
    output_weight,
    up_weight,
    down_weight,
    query_bias,
    value_bias,
    output_bias,
    norm_gain,
    norm_shift,
    up_bias,
    down_bias,
    final_gain,
    final_shift,
):
    ranks, parts = lax.axis_size("ctx"), lax.axis_size("fsdp")
    rank = lax.axis_index("ctx")
    core = bit_of("ctx", 0)
    width = tokens.shape[2]

    bits = bits_of(parts)
    upward = tuple(range(bits))
    own, deep = input_weight.shape[0], down_weight.shape[0]
    half = width // 2

    order = Order()

    def columns_of(shard, index, count):
        count = shard.shape[1] // count
        return lax.dynamic_slice_in_dim(shard, index * count, count, 1)

    small = jnp.stack(
        [
            query_bias,
            value_bias,
            value_bias,
            output_bias,
            norm_gain,
            norm_shift,
            down_bias,
            final_gain,
            final_shift,
        ]
    )
    small = jnp.concatenate([small.reshape(-1), up_bias])[None]
    stages = []
    for bit in upward:
        small = jnp.concatenate(both(small, "fsdp", bit), axis=0)
        stages.append(small)
    vectors = small[:, : 9 * own].reshape(parts, 9, own).transpose(1, 0, 2).reshape(9, width)
    wide_up_bias = small[:, 9 * own :].reshape(1, -1)

    everyone = ("fsdp", "ctx")
    attn = lax.all_gather(columns_of(input_weight, rank, ranks), everyone, axis=0, tiled=False)
    held = lax.all_gather(
        jnp.concatenate(
            [
                columns_of(up_weight, rank, ranks),
                columns_of(output_weight, rank, ranks),
                lax.dynamic_slice_in_dim(down_weight, rank * (deep // ranks), deep // ranks, 0),
            ],
            axis=1,
        ),
        everyone,
        axis=0,
        tiled=False,
    )
    tok = Sequences(order, tokens)
    order.after = (stages[-1],)
    tok.step()
    tok = tok.last()
    cot = Sequences(order, cotangent)
    cot.step()
    cot = cot.last()
    shape = (ranks, tok.shape[1]) + tok.shape[2:]
    rows = math.prod(shape[:3])
    tok_rows, cot_rows = tok.reshape(rows, width), cot.reshape(rows, width)

    query, keys, values = order(merge, tok_rows, attn, vectors[0:3], parts, ranks)
    context = attend_forward(query, keys, values, shape).reshape(rows, width)
    (
        layer_out,
        hidden_low,
        active,
        d_branch,
        d_inner,
        d_attn,
        d_context,
        d_pre_one,
        sums,
        up_sums,
    ) = middle(context, tok_rows, cot_rows, held, vectors[1:9], wide_up_bias, parts, ranks)

    mine, other = core.reshape(1), (1 - core).reshape(1)
    row_vectors = sums[:6].reshape(6, parts, own).transpose(1, 0, 2).reshape(parts, 6 * own)
    order = Order()
    shards = [("fsdp", bit) for bit in upward]
    chip = [("ctx", 1)]
    turned = upward[1:2] + upward[:1] + upward[2:]

    down_mine, down_other, down_turn = down_grad(mine, active, d_branch, parts, turned, ())
    order.after = (down_other,)
    down_sum = Reduce(order, [("fsdp", bit) for bit in down_turn] + chip, down_mine, down_other)
    layer_out = Positions(order, layer_out.reshape(shape))
    up_mine, up_other = order(
        up_grad, mine, hidden_low, d_inner, parts, ranks, turned, width // ranks
    )
    down_sum.step()
    layer_out.step()
    up_mine, up_other = order(
        output_grad, mine, context, d_attn, up_mine, up_other, parts, ranks, turned
    )
    up_sum = Reduce(order, chip + [("fsdp", bit) for bit in turned], up_mine, up_other)
    up_sum.step()

    begun = ()
    for share in range(2 * shape[1]):
        begun = order(attend_backward, query, keys, values, d_context, shape, share, begun)[:5]
        if share == 0:
            layer_out = layer_out.last()
        if share == shape[1] - 1:
            down_sum.step()
    d_query, d_keys, d_values = [member.reshape(rows, width) for member in begun[:3]]
    down_sum.step()
    small_in = packed(
        [
            member.reshape(-1, 8, width)[:, 0].sum(axis=0).reshape(parts, own)
            for member in begun[3:]
        ]
        + [row_vectors, up_sums.reshape(parts, deep)],
        parts,
        upward,
        half,
    )

    near, far, near_keys, far_keys = order(
        input_grad, mine, tok_rows, d_query, d_values, d_keys, parts, ranks, upward
    )
    near, far = [
        lax.dynamic_update_slice(
            held,
            lax.dynamic_index_in_dim(small_in, side[0], 1, keepdims=False),
            (0, 2 * own, 0),
        )
        for held, side in ((near, mine), (far, other))
    ]
    input_sum = Reduce(order, shards + chip, near, far)
    keys_sum = Reduce(order, chip + shards, near_keys, far_keys)
    up_sum.step()
    input_sum.step()
    keys_sum.step()
    tokens_grad = order(
        tokens_grad_of, d_pre_one, (d_query, d_keys, d_values), attn, parts, ranks
    )
    tokens_grad = Positions(order, tokens_grad.reshape(shape))
    turns = [input_sum, keys_sum, up_sum, input_sum, down_sum, keys_sum, tokens_grad, up_sum]
    turns += [input_sum, keys_sum, down_sum, input_sum]
    for chain in turns:
        if not isinstance(chain, Reduce) or chain.route:
            chain.step()
    chains = [up_sum, down_sum, input_sum, keys_sum]
    while any(chain.route for chain in chains):
        for chain in chains:
            if chain.route:
                chain.step()
    up_done = up_sum.last()
    keys_done = keys_sum.last()
    down_done = down_sum.last()
    input_done = input_sum.last()
    tokens_grad = tokens_grad.last()
    layer_out, tokens_grad = [member.reshape(tokens.shape) for member in (layer_out, tokens_grad)]

    def across(value):
        lower, upper = both(jnp.stack(both(value, "ctx", 1)), "ctx", 0)
        return [lower[0], upper[0], lower[1], upper[1]]

    def joined(members):
        return jnp.concatenate(members, axis=1).astype(WIDE)

    lower, upper = both(down_done, "ctx", 0)
    down_result = jnp.concatenate([lower, upper], axis=0).astype(WIDE).T

    blocks = across(up_done)
    span = up_weight.shape[1] // ranks
    up_result = joined([member[:, :span] for member in blocks])
    output_result = joined([member[:, span:] for member in blocks])

    sides = both(input_done, "ctx", 0)
    query_result, value_result = [
        joined([side[at * own : (at + 1) * own] for side in sides]) for at in range(2)
    ]
    input_result = jnp.concatenate([query_result, joined(across(keys_done)), value_result], axis=1)
    flat = jnp.concatenate([side[2 * own :].reshape(-1) for side in sides]).astype(WIDE)
    eight = [flat[at * own : (at + 1) * own] for at in range(8)]
    up_bias_grad = flat[8 * own : 8 * own + deep]

    return (
        layer_out,
        tokens_grad,
        input_result,
        output_result,
        up_result,
        down_result,
        *eight[:5],
        up_bias_grad,
        *eight[5:],
    )


def solution(mesh):
    rows = P("fsdp", "ctx", None)
    matrix = P("fsdp", None)
    vector = P("fsdp")
    return jax.shard_map(
        local,
        mesh=mesh,
        in_specs=(rows,) * 2 + (matrix,) * 4 + (vector,) * 9,
        out_specs=(rows,) * 2 + (matrix,) * 4 + (vector,) * 9,
        check_vma=False,
    )
```

time: 994 us -> 602 us (0.61)
  matrix products: 286 us -> 0 us
  Pallas kernels: 0 us -> 245 us
  waiting for transfers between devices: 384 us -> 250 us
  blocking collectives: 120 us -> 0 us
  local copies, waits for them, and re-layouts: 102 us -> 36.9 us
  other arithmetic: 64.5 us -> 14.3 us
  starting transfers between devices: 12.4 us -> 35.7 us
    dot_general x26 -> x0, matrix products: 286 us -> none  [the longest x1 51.7 us: local(): jnp.dot(hidden_low, wide_up, preferred_element_type=jnp.float32)]
    reduce_scatter x4 -> x0, waiting for transfers between devices: 255 us -> none  [reduced(): lax.psum_scatter(grad.astype(jnp.bfloat16), ('fsdp', 'ctx'), scatter_dime...]
    pallas_call x0 -> x42, Pallas kernels: none -> 245 us  [the longest x1 67.4 us: middle(): pl.pallas_call(functools.partial(middle_kernel, parts=parts, ranks=ranks,...]
    ppermute x0 -> x37, waiting for transfers between devices: none -> 156 us  [swap(): lax.ppermute(value, axis, [(at, at ^ 1 << bit) for at in range(count)])]
    all_gather x3 -> x0, blocking collectives: 47.9 us -> none  [the longest x1 33 us: local(): lax.all_gather(jnp.concatenate(small), 'fsdp', axis=0, tiled=False)]
    psum x1 -> x0, blocking collectives: 39 us -> none  [local(): summed = lax.psum(joined, ('fsdp', 'ctx'))]
    all_to_all x3 -> x0, waiting for transfers between devices: 37.6 us -> none  [the longest x2 37.6 us: local(): lax.all_to_all(member, 'ctx', split_axis=1, concat_axis=0, tiled=True)]
    ppermute x0 -> x37, starting transfers between devices: none -> 35.6 us  [swap(): lax.ppermute(value, axis, [(at, at ^ 1 << bit) for at in range(count)])]
  transfers between devices with their start and end apart: 13 -> 39, of which waited for: 9 -> 20; matrix products, arithmetic and copies ran while one was open for 38% -> 3% of each run, Pallas kernels for 0% -> 26%
where the time goes in v2:
time: 602 us; the launch traced here: 597 us
  waiting for transfers between devices  250 us (42%)
  Pallas kernels  245 us (41%)
  local copies, waits for them, and re-layouts  36.9 us (6%)
  starting transfers between devices  35.7 us (6%)
  between operations  15.5 us (3%)
  other arithmetic  14.3 us (2%)
    ppermute x37, waiting for transfers between devices, swap(): lax.ppermute(value, axis, [(at, at ^ 1 << bit) for at in range(count)])  156 us
    all_gather x1, waiting for transfers between devices, local(): lax.all_gather(jnp.concatenate([columns_of(up_weight, rank, ranks), colum...  93.9 us
    pallas_call x1, Pallas kernels, middle(): pl.pallas_call(functools.partial(middle_kernel, parts=parts, ranks=ranks,...  67.4 us
    pallas_call x4, Pallas kernels, attend_backward(): pl.pallas_call(attend_backward_kernel, grid=(pairs,), in_specs=[spec] * 4...  47.6 us
    ppermute x37, starting transfers between devices, swap(): lax.ppermute(value, axis, [(at, at ^ 1 << bit) for at in range(count)])  35.6 us
    unnamed x134, local copies, waits for them, and re-layouts  29.8 us
    pallas_call x14, Pallas kernels, settle(): pl.pallas_call(settle_kernel, grid_spec=pltpu.PrefetchScalarGridSpec(num_...  21.3 us
    pallas_call x10, Pallas kernels, pick(): pl.pallas_call(functools.partial(pick_kernel, count=count), grid_spec=plt...  20.2 us
  transfers between devices with their start and end apart: 39, of which 20 were waited for; matrix products, arithmetic and copies ran while one was open for 3% of the time, Pallas kernels for 26%

profile of v2, /device:TPU:0, one launch (start us, length us, event | category | flops | bytes accessed | tf_op | source)
XLA Modules:
  0.0 597.0 jit_solution(4441976742467609116)
XLA Ops:
  12.1 3.0 collective-permute-start.1
  15.1 1.6 collective-permute-done.1
  16.8 2.1 collective-permute-start.2
  19.9 1.5 collective-permute-start
  21.5 2.7 collective-permute-start.3
  24.2 2.0 collective-permute-done.3
  26.3 23.2 %collective-permute-done.refs_1_.refs_2_ = bf16[2,2,128,1024]{3,2,1,0:T(8,128)(2,1)} collective-permute-done((bf16[2,2,128,1024]{3,2,1,0:T(8,128)(2,1)}, bf16[2,2,128,1024]{3,2,1,0:T(8,128)(2,1)}, u32[]{:S(2)}, u32[]{:S(2)}) %collective-permute-start) | collective-permute-done | bytes 1048608 | tf_op jit(solution)/shard_map/ppermute | solution.py:666
  49.5 2.7 pick.10.refs_4_
  53.3 2.5 collective-permute-start.5
  55.8 1.6 copy-done.16
  57.4 1.9 pick.11.refs_2_
  59.4 31.7 %collective-permute-done.5.refs_1_.refs_2_ = bf16[2,2,128,1024]{3,2,1,0:T(8,128)(2,1)} collective-permute-done((bf16[2,2,128,1024]{3,2,1,0:T(8,128)(2,1)}, bf16[2,2,128,1024]{3,2,1,0:T(8,128)(2,1)}, u32[]{:S(2)}, u32[]{:S(2)}) %collective-permute-start.5) | collective-permute-done | bytes 1048608 | tf_op jit(solution)/shard_map/ppermute | solution.py:666
  91.1 1.7 pick.12.refs_4_
  95.6 1.9 pick.13.refs_0_
  98.8 11.9 %merge.1 = (bf16[1024,1024]{1,0:T(8,128)(2,1)}, bf16[1024,1024]{1,0:T(8,128)(2,1)}, bf16[1024,1024]{1,0:T(8,128)(2,1)}) custom-call(bf16[1024,1024]{1,0:T(8,128)(2,1)} %bitcast.137, bf16[3,1024]{1,0:T(4,128)(2,1)} %slice_bitcast_fusion.11.bias_ref, bf16[32,128,768]{2,1,0:T(8,128)(2,1)} %bitcast.189, bf16[4,2,128,1024]{3,2,1,0:T(8,128)(2,1)} %copy-done.13), custom_call_target="tpu_custom_call" | custom-call | flops 402653184 | bytes 917504 | tf_op jit(solution)/shard_map/merge/pallas_call | solution.py:105
  110.7 19.9 %attend_forward.1 = bf16[4,2,128,1024]{3,2,1,0:T(8,128)(2,1)} custom-call(bf16[4,2,128,1024]{3,2,1,0:T(8,128)(2,1)} %bitcast.170, bf16[4,2,128,1024]{3,2,1,0:T(8,128)(2,1)} %bitcast.175, bf16[4,2,128,1024]{3,2,1,0:T(8,128)(2,1)} %bitcast.180), custom_call_target="tpu_custom_call" | custom-call | flops 536870912 | bytes 524288 | tf_op jit(solution)/shard_map/attend_forward/pallas_call | solution.py:143
  130.6 93.9 %all-gather.7.cloned.1.call-done = bf16[4096,2304]{1,0:T(8,128)(2,1)} async-done(((bf16[128,2304]{1,0:T(8,128)(2,1)}), bf16[4096,2304]{1,0:T(8,128)(2,1)}) %all-gather.7.cloned.1.call-update) | async-done | bytes 18874384 | tf_op jit(solution)/shard_map/all_gather | solution.py:887
  224.5 67.4 %middle.1 = (bf16[1024,1024]{1,0:T(8,128)(2,1)}, bf16[1024,1024]{1,0:T(8,128)(2,1)}, bf16[1024,4096]{1,0:T(8,128)(2,1)}, bf16[1024,1024]{1,0:T(8,128)(2,1)}, bf1...) custom-call(bf16[1024,1024]{1,0:T(8,128)(2,1)} %bitcast.149, ...), custom_call_target="tpu_custom_call" | custom-call | flops 2415919104 | bytes 4718592 | tf_op jit(solution)/shard_map/middle/pallas_call | solution.py:378
  291.9 13.9 %down_grad.1 = (bf16[2,4,512,512]{3,2,1,0:T(8,128)(2,1)}, bf16[2,4,512,512]{3,2,1,0:T(8,128)(2,1)}) custom-call(s32[1]{0:T(128)} %bitcast.1.half_ref, bf16[1024,1024]{1,0:T(8,128)(2,1)} %get-tuple-element.94.near_ref.far_ref, bf16[1024,1024]{1,0:T(8,128)(2,1)} %get-tuple-element.94.near_ref.far_ref, bf16[1024,4096]{1,0:T(8,128)(2,1)} %get-tuple-element.95.active_ref), custom_call_target="tpu_custom_call" | custom-call | flops 536870912 | bytes 1048576 | tf_op jit(solution)/shard_map/down_grad/pallas_call | solution.py:429
  306.0 2.2 copy-done.27
  308.9 1.5 collective-permute-start.7
  310.4 14.4 %up_grad.1 = (bf16[2,8,128,1280]{3,2,1,0:T(8,128)(2,1)}, bf16[2,8,128,1280]{3,2,1,0:T(8,128)(2,1)}) custom-call(s32[1]{0:T(128)} %bitcast.1.half_ref, bf16[1024,1024]{1,0:T(8,128)(2,1)} %get-tuple-element.98.hidden_ref, bf16[1024,4096]{1,0:T(8,128)(2,1)} %get-tuple-element.99.grad_ref, bf16[2,2,128,1024]{3,2,1,0:T(8,128)(2,1)} %copy-done.26), custom_call_target="tpu_custom_call" | custom-call | flops 536870912 | bytes 1048576 | tf_op jit(solution)/shard_map/up_grad/pallas_call | solution.py:539
  324.8 2.2 copy-done.14
  327.0 4.7 settle.14
  331.7 2.7 collective-permute-done.7.refs_1_.refs_2_
  334.4 2.9 pick.15.refs_4_
  337.3 4.4 output_grad.1
  341.7 1.5 collective-permute-start.11
  343.4 6.9 %collective-permute-done.10.came_ref.came_far = bf16[16,128,1280]{2,1,0:T(8,128)(2,1)S(1)} collective-permute-done((bf16[16,128,1280]{2,1,0:T(8,128)(2,1)S(1)}, bf16[16,128,1280]{2,1,0:T(8,128)(2,1)S(1)}, u32[]{:S(2)}, u32[]{:S(2)}) %collective-permute-start.10) | collective-permute-done | bytes 5242912 | tf_op jit(solution)/shard_map/ppermute | solution.py:666
  350.3 2.3 copy-done.43
  352.6 2.5 copy-done.10
  355.1 5.3 settle.15
  361.9 1.5 copy-done.31
  363.4 11.7 %attend_backward.4 = (bf16[4,2,128,1024]{3,2,1,0:T(8,128)(2,1)}, bf16[4,2,128,1024]{3,2,1,0:T(8,128)(2,1)}, bf16[4,2,128,1024]{3,2,1,0:T(8,128)(2,1)}, f32[16,10...) custom-call(bf16[4,2,128,1024]{3,2,1,0:T(8,128)(2,1)} %bitcast.171, bf16[4,2,128,1024]{3,2,1,0:T(8,128)(2,1)} %bitcast.176, ...), custom_call_target="tpu_custom_call" | custom-call | flops 335544320 | bytes 458752 | tf_op jit(solution)/shard_map/attend_backward/pallas_call | solution.py:204
  375.9 3.5 pick.16.refs_5_
  379.3 12.1 %attend_backward.5 = (bf16[4,2,128,1024]{3,2,1,0:T(8,128)(2,1)}, bf16[4,2,128,1024]{3,2,1,0:T(8,128)(2,1)}, bf16[4,2,128,1024]{3,2,1,0:T(8,128)(2,1)}, f32[16,10...) custom-call(bf16[4,2,128,1024]{3,2,1,0:T(8,128)(2,1)} %bitcast.172, ...), custom_call_target="tpu_custom_call", output_to_operand_aliasing={{0}: (4, {}), {1}: (5, {}), {2}: (6, {}), {3}: (7, {}), {4}... | custom-call | flops 335544320 | bytes 458752 | tf_op jit(solution)/shard_map/attend_backward/pallas_call | solution.py:204
  392.2 2.5 settle.16
  394.9 2.9 collective-permute-start.15
  397.8 11.8 %attend_backward.6 = (bf16[4,2,128,1024]{3,2,1,0:T(8,128)(2,1)}, bf16[4,2,128,1024]{3,2,1,0:T(8,128)(2,1)}, bf16[4,2,128,1024]{3,2,1,0:T(8,128)(2,1)}, f32[16,10...) custom-call(bf16[4,2,128,1024]{3,2,1,0:T(8,128)(2,1)} %bitcast.173, ...), custom_call_target="tpu_custom_call", output_to_operand_aliasing={{0}: (4, {}), {1}: (5, {}), {2}: (6, {}), {3}: (7, {}), {4}... | custom-call | flops 335544320 | bytes 458752 | tf_op jit(solution)/shard_map/attend_backward/pallas_call | solution.py:204
  409.6 11.9 %attend_backward.7 = (bf16[4,2,128,1024]{3,2,1,0:T(8,128)(2,1)}, bf16[4,2,128,1024]{3,2,1,0:T(8,128)(2,1)}, bf16[4,2,128,1024]{3,2,1,0:T(8,128)(2,1)}, f32[16,10...) custom-call(bf16[4,2,128,1024]{3,2,1,0:T(8,128)(2,1)} %bitcast.174, ...), custom_call_target="tpu_custom_call", output_to_operand_aliasing={{0}: (4, {}), {1}: (5, {}), {2}: (6, {}), {3}: (7, {}), {4}... | custom-call | flops 335544320 | bytes 458752 | tf_op jit(solution)/shard_map/attend_backward/pallas_call | solution.py:204
  424.1 1.6 settle.17
  426.6 1.6 copy-done.4
  428.3 11.1 %input_grad.1 = (bf16[8,272,512]{2,1,0:T(8,128)(2,1)}, bf16[2,8,128,256]{3,2,1,0:T(8,128)(2,1)S(1)}, bf16[8,272,512]{2,1,0:T(8,128)(2,1)}, bf16[2,8,128,256]{3,2,1,0:T(8,128)(2,1)S(1)}) custom-call(s32[1]{0:T(128)} %bitcast.1.half_ref, bf16[1024,1024]{1,0:T(8,128)(2,1)S(1)} %bitcast.139, bf16[1024,1024]{1,0:T(8,128)(2,1)S(1)} %bitcast.128, ...), custom_call_target="tpu_custom_call" | custom-call | flops 402653184 | bytes 655360 | tf_op jit(solution)/shard_map/input_grad/pallas_call | solution.py:614
  440.6 14.6 %collective-permute-done.15.came_ref.came_far = bf16[8,128,1280]{2,1,0:T(8,128)(2,1)} collective-permute-done((bf16[8,128,1280]{2,1,0:T(8,128)(2,1)}, bf16[8,128,1280]{2,1,0:T(8,128)(2,1)}, u32[]{:S(2)}, u32[]{:S(2)}) %collective-permute-start.15) | collective-permute-done | bytes 2621472 | tf_op jit(solution)/shard_map/ppermute | solution.py:666
  455.3 4.0 settle.18
  459.2 1.7 collective-permute-start.22
  461.0 1.7 settle.19
  462.6 1.8 collective-permute-start.18
  466.0 2.2 copy-done.25
  468.2 10.4 %tokens_grad.1.refs_2_ = bf16[1024,1024]{1,0:T(8,128)(2,1)S(1)} custom-call(f32[1024,1024]{1,0:T(8,128)S(1)} %copy-done.25, bf16[1024,1024]{1,0:T(8,128)(2,1)S(1)} %bitcast.130, bf16[1024,1024]{1,0:T(8,128)(2,1)S(1)} %bitcast.133, bf16[1024,1024]{1,0:T(8,128)(2,1)S(1)} %bitcast.136, bf16[32,128,768]{2,1,0:T(8,128)(2,1)} %bitcast.190, ...), custom_call_target="tpu_custom_call" | custom-call | flops 402653184 | bytes 1179648 | tf_op jit(solution)/shard_map/tokens_grad/pallas_call | solution.py:651
  480.2 8.1 %collective-permute-done.18.came_ref.came_far = bf16[4,272,512]{2,1,0:T(8,128)(2,1)S(1)} collective-permute-done((bf16[4,272,512]{2,1,0:T(8,128)(2,1)}, bf16[4,272,512]{2,1,0:T(8,128)(2,1)S(1)}, u32[]{:S(2)}, u32[]{:S(2)}) %collective-permute-start.18) | collective-permute-done | bytes 1114144 | tf_op jit(solution)/shard_map/ppermute | solution.py:666
  491.5 1.6 collective-permute-start.21
  493.0 1.5 collective-permute-start.20
  494.9 19.8 %collective-permute-done.21.came_ref.came_far = bf16[2,272,512]{2,1,0:T(8,128)(2,1)S(1)} collective-permute-done((bf16[2,272,512]{2,1,0:T(8,128)(2,1)S(1)}, bf16[2,272,512]{2,1,0:T(8,128)(2,1)S(1)}, u32[]{:S(2)}, u32[]{:S(2)}) %collective-permute-start.21) | collective-permute-done | bytes 557088 | tf_op jit(solution)/shard_map/ppermute | solution.py:666
  520.8 15.7 %collective-permute-done.24.right_ref = bf16[1,272,512]{2,1,0:T(8,128)(2,1)S(1)} collective-permute-done((bf16[1,272,512]{2,1,0:T(8,128)(2,1)S(1)}, bf16[1,272,512]{2,1,0:T(8,128)(2,1)S(1)}, u32[]{:S(2)}, u32[]{:S(2)}) %collective-permute-start.24) | collective-permute-done | bytes 278560 | tf_op jit(solution)/shard_map/ppermute | solution.py:666
  536.8 7.9 %collective-permute-done.30.right_ref = bf16[1,128,1280]{2,1,0:T(8,128)(2,1)S(1)} collective-permute-done((bf16[1,128,1280]{2,1,0:T(8,128)(2,1)S(1)}, bf16[1,128,1280]{2,1,0:T(8,128)(2,1)S(1)}, u32[]{:S(2)}, u32[]{:S(2)}) %collective-permute-start.30) | collective-permute-done | bytes 327712 | tf_op jit(solution)/shard_map/ppermute | solution.py:666
  548.4 2.1 collective-permute-done.32
  552.2 9.5 %collective-permute-done.27.right_ref = bf16[1,512,512]{2,1,0:T(8,128)(2,1)} collective-permute-done((bf16[1,512,512]{2,1,0:T(8,128)(2,1)S(1)}, bf16[1,512,512]{2,1,0:T(8,128)(2,1)}, u32[]{:S(2)}, u32[]{:S(2)}) %collective-permute-start.27) | collective-permute-done | bytes 524320 | tf_op jit(solution)/shard_map/ppermute | solution.py:666
  563.1 4.7 collective-permute-done.26.right_ref
  570.8 2.1 collective-permute-done.34
  577.6 1.6 convert_bitcast_fusion
  579.3 3.0 copy.52
  582.2 3.6 pick.19
  587.3 1.5 maximum_convert_fusion
  (260 shorter events, 49.8 us)
Async XLA Ops:
  7.2 4.7 copy-start.57
  7.2 4.7 copy-start.58
  7.2 4.7 copy-start.59
  7.2 4.7 copy-start.53
  7.2 4.7 copy-start.51
  7.2 4.7 copy-start.54
  7.3 4.8 copy-start.52
  7.3 11.6 %copy-start.15 = (bf16[8,128,1024]{2,1,0:T(8,128)(2,1)S(1)}, bf16[8,128,1024]{2,1,0:T(8,128)(2,1)}, u32[]{:S(2)}) copy-start(bf16[8,128,1024]{2,1,0:T(8,128)(2,1)} %param.15) | copy-start | bytes 6291460
  7.3 91.5 %all-gather.5.cloned.1.call-start = ((), (), s32[]{:S(2)}) async-start(), calls=%async_computation | async-start | bytes 6488064 | tf_op jit(solution)/shard_map/all_gather | solution.py:886
  9.0 215.4 %all-gather.7.cloned.1.call-start = ((), (), s32[]{:S(2)}) async-start(), calls=%async_computation.1 | async-start | bytes 19464192 | tf_op jit(solution)/shard_map/all_gather | solution.py:887
  12.1 4.6 collective-permute-start.1
  16.8 4.7 collective-permute-start.2
  19.9 29.6 %collective-permute-start = (bf16[2,2,128,1024]{3,2,1,0:T(8,128)(2,1)}, bf16[2,2,128,1024]{3,2,1,0:T(8,128)(2,1)}, u32[]{:S(2)}, u32[]{:S(2)}) collective-permute-start(bf16[2,2,128,1024]{3,2,1,0:T(8,128)(2,1)} %constant_dynamic-slice_fusion.5), channel_id=1, source_target_pairs={{0,16},{8,24},{16,0},{24,8},{1,17},{9,25},{17,1},{25,9},{2,18},{10... | collective-permute-start | bytes 3145736 | tf_op jit(solution)/shard_map/ppermute | solution.py:666
  21.5 4.8 collective-permute-start.3
  52.2 3.6 collective-permute-start.4
  53.3 37.9 %collective-permute-start.5 = (bf16[2,2,128,1024]{3,2,1,0:T(8,128)(2,1)}, bf16[2,2,128,1024]{3,2,1,0:T(8,128)(2,1)}, u32[]{:S(2)}, u32[]{:S(2)}) collective-permute-start(bf16[2,2,128,1024]{3,2,1,0:T(8,128)(2,1)} %constant_dynamic-slice_fusion.3), channel_id=1, source_target_pairs={{0,16},{8,24},{16,0},{24,8},{1,17},{9,25},{17,1},{25,9},{2,18},{10... | collective-permute-start | bytes 3145736 | tf_op jit(solution)/shard_map/ppermute | solution.py:666
  57.4 33.7 %copy-start.18 = (bf16[8,128,1024]{2,1,0:T(8,128)(2,1)S(1)}, bf16[8,128,1024]{2,1,0:T(8,128)(2,1)}, u32[]{:S(2)}) copy-start(bf16[8,128,1024]{2,1,0:T(8,128)(2,1)} %param.16) | copy-start | bytes 6291460
  59.4 33.5 %copy-start.6 = (bf16[4,2,128,1024]{3,2,1,0:T(8,128)(2,1)}, bf16[4,2,128,1024]{3,2,1,0:T(8,128)(2,1)S(1)}, u32[]{:S(2)}) copy-start(bf16[4,2,128,1024]{3,2,1,0:T(8,128)(2,1)S(1)} %pick.11.refs_2_) | copy-start | bytes 6291460
  92.8 2.8 collective-permute-start.6
  291.8 14.2 %copy-start.11 = (bf16[1024,1024]{1,0:T(8,128)(2,1)S(1)}, bf16[1024,1024]{1,0:T(8,128)(2,1)}, u32[]{:S(2)}) copy-start(bf16[1024,1024]{1,0:T(8,128)(2,1)} %get-tuple-element.93) | copy-start | bytes 6291460
  291.9 14.2 %copy-start.42 = (s32[2]{0:T(128)S(1)}, s32[2]{0:T(128)}, u32[]{:S(2)}) copy-start(s32[2]{0:T(128)} %constant.207.clone.1.pick_ref) | copy-start | bytes 28
  305.8 19.0 %collective-permute-start.8 = (bf16[8,512,512]{2,1,0:T(8,128)(2,1)}, bf16[8,512,512]{2,1,0:T(8,128)(2,1)}, u32[]{:S(2)}, u32[]{:S(2)}) collective-permute-start(bf16[8,512,512]{2,1,0:T(8,128)(2,1)} %bitcast.161), channel_id=1, source_target_pairs={{0,8},{8,0},{16,24},{24,16},{1,9},{9,1},{17,25},{25,17},{2,10},{10... | collective-permute-start | bytes 12582920 | tf_op jit(solution)/shard_map/ppermute | solution.py:666
  308.9 25.5 %collective-permute-start.7 = (bf16[2,2,128,1024]{3,2,1,0:T(8,128)(2,1)S(1)}, bf16[2,2,128,1024]{3,2,1,0:T(8,128)(2,1)}, u32[]{:S(2)}, u32[]{:S(2)}) collective-permute-start(bf16[2,2,128,1024]{3,2,1,0:T(8,128)(2,1)S(1)} %pick.14.refs_0_), channel_id=1, source_target_pairs={{0,16},{8,24},{16,0},{24,8},{1,17},{9,25},{17,1},{25,9},{2,18},{10... | collective-permute-start | bytes 3145736 | tf_op jit(solution)/shard_map/ppermute | solution.py:666
  327.0 10.3 %copy-start.12 = (bf16[4,2,128,1024]{3,2,1,0:T(8,128)(2,1)S(1)}, bf16[4,2,128,1024]{3,2,1,0:T(8,128)(2,1)}, u32[]{:S(2)}) copy-start(bf16[4,2,128,1024]{3,2,1,0:T(8,128)(2,1)} %attend_forward.1) | copy-start | bytes 6291460
  327.0 10.3 %copy-start.22 = (bf16[1024,1024]{1,0:T(8,128)(2,1)S(1)}, bf16[1024,1024]{1,0:T(8,128)(2,1)}, u32[]{:S(2)}) copy-start(bf16[1024,1024]{1,0:T(8,128)(2,1)} %get-tuple-element.103.refs_0_.refs_1_) | copy-start | bytes 6291460
  331.7 5.6 copy-start.23
  341.7 10.9 %copy-start.9 = (bf16[2,8,128,1280]{3,2,1,0:T(8,128)(2,1)}, bf16[2,8,128,1280]{3,2,1,0:T(8,128)(2,1)S(1)}, u32[]{:S(2)}) copy-start(bf16[2,8,128,1280]{3,2,1,0:T(8,128)(2,1)S(1)} %get-tuple-element.106) | copy-start | bytes 15728644
  341.7 8.7 %collective-permute-start.10 = (bf16[16,128,1280]{2,1,0:T(8,128)(2,1)S(1)}, bf16[16,128,1280]{2,1,0:T(8,128)(2,1)S(1)}, u32[]{:S(2)}, u32[]{:S(2)}) collective-permute-start(bf16[16,128,1280]{2,1,0:T(8,128)(2,1)S(1)} %bitcast.141), channel_id=1, source_target_pairs={{0,8},{8,0},{16,24},{24,16},{1,9},{9,1},{17,25},{25,17},{2,10},{10... | collective-permute-start | bytes 15728648 | tf_op jit(solution)/shard_map/ppermute | solution.py:666
  341.7 49.8 %collective-permute-start.11 = (bf16[4,512,512]{2,1,0:T(8,128)(2,1)}, bf16[4,512,512]{2,1,0:T(8,128)(2,1)}, u32[]{:S(2)}, u32[]{:S(2)}) collective-permute-start(bf16[4,512,512]{2,1,0:T(8,128)(2,1)} %get-tuple-element.101.refs_2_), channel_id=1, source_target_pairs={{0,1},{1,0},{2,3},{3,2},{4,5},{5,4},{6,7},{7,6},{8,9},{9,8},{10,11... | collective-permute-start | bytes 6291464 | tf_op jit(solution)/shard_map/ppermute | solution.py:666
  343.2 32.0 %collective-permute-start.9 = (bf16[2,2,128,1024]{3,2,1,0:T(8,128)(2,1)}, bf16[2,2,128,1024]{3,2,1,0:T(8,128)(2,1)S(1)}, u32[]{:S(2)}, u32[]{:S(2)}) collective-permute-start(bf16[2,2,128,1024]{3,2,1,0:T(8,128)(2,1)} %pick.15.refs_4_), channel_id=1, source_target_pairs={{0,8},{8,0},{16,24},{24,16},{1,9},{9,1},{17,25},{25,17},{2,10},{10... | collective-permute-start | bytes 3145736 | tf_op jit(solution)/shard_map/ppermute | solution.py:666
  363.4 11.8 %copy-start.41 = (s32[4]{0:T(128)S(1)}, s32[4]{0:T(128)}, u32[]{:S(2)}) copy-start(s32[4]{0:T(128)} %constant.189.clone.1.pick_ref) | copy-start | bytes 52
  379.3 12.1 %copy-start.24 = (bf16[4,512,512]{2,1,0:T(8,128)(2,1)S(1)}, bf16[4,512,512]{2,1,0:T(8,128)(2,1)}, u32[]{:S(2)}) copy-start(bf16[4,512,512]{2,1,0:T(8,128)(2,1)} %copy-done.23) | copy-start | bytes 6291460
  394.6 28.8 %collective-permute-start.12 = (bf16[2,512,512]{2,1,0:T(8,128)(2,1)}, bf16[2,512,512]{2,1,0:T(8,128)(2,1)}, u32[]{:S(2)}, u32[]{:S(2)}) collective-permute-start(bf16[2,512,512]{2,1,0:T(8,128)(2,1)} %get-tuple-element.122.refs_5_), channel_id=1, source_target_pairs={{0,2},{1,3},{2,0},{3,1},{4,6},{5,7},{6,4},{7,5},{8,10},{9,11},{10,... | collective-permute-start | bytes 3145736 | tf_op jit(solution)/shard_map/ppermute | solution.py:666
  394.9 60.4 %collective-permute-start.15 = (bf16[8,128,1280]{2,1,0:T(8,128)(2,1)}, bf16[8,128,1280]{2,1,0:T(8,128)(2,1)}, u32[]{:S(2)}, u32[]{:S(2)}) collective-permute-start(bf16[8,128,1280]{2,1,0:T(8,128)(2,1)} %copy-done.31), channel_id=1, source_target_pairs={{0,16},{8,24},{16,0},{24,8},{1,17},{9,25},{17,1},{25,9},{2,18},{10... | collective-permute-start | bytes 7864328 | tf_op jit(solution)/shard_map/ppermute | solution.py:666
  409.6 16.9 %copy-start.7 = (bf16[4,2,128,1024]{3,2,1,0:T(8,128)(2,1)S(1)}, bf16[4,2,128,1024]{3,2,1,0:T(8,128)(2,1)}, u32[]{:S(2)}) copy-start(bf16[4,2,128,1024]{3,2,1,0:T(8,128)(2,1)} %copy-done.6) | copy-start | bytes 6291460
  426.5 12.9 %copy-start.36 = (bf16[1,512,512]{2,1,0:T(8,128)(2,1)}, bf16[1,512,512]{2,1,0:T(8,128)(2,1)S(1)}, u32[]{:S(2)}) copy-start(bf16[1,512,512]{2,1,0:T(8,128)(2,1)S(1)} %get-tuple-element.134.refs_6_) | copy-start | bytes 1572868
  428.3 27.0 %copy-start.20 = (bf16[8,128,1280]{2,1,0:T(8,128)(2,1)S(1)}, bf16[8,128,1280]{2,1,0:T(8,128)(2,1)}, u32[]{:S(2)}) copy-start(bf16[8,128,1280]{2,1,0:T(8,128)(2,1)} %copy-done.19) | copy-start | bytes 7864324
  440.1 20.8 %collective-permute-start.14 = (bf16[8,272,512]{2,1,0:T(8,128)(2,1)}, bf16[8,272,512]{2,1,0:T(8,128)(2,1)S(1)}, u32[]{:S(2)}, u32[]{:S(2)}) collective-permute-start(bf16[8,272,512]{2,1,0:T(8,128)(2,1)} %get-tuple-element.209), channel_id=1, source_target_pairs={{0,8},{8,0},{16,24},{24,16},{1,9},{9,1},{17,25},{25,17},{2,10},{10... | collective-permute-start | bytes 6684680 | tf_op jit(solution)/shard_map/ppermute | solution.py:666
  440.1 24.3 %collective-permute-start.13 = (bf16[16,128,256]{2,1,0:T(8,128)(2,1)S(1)}, bf16[16,128,256]{2,1,0:T(8,128)(2,1)S(1)}, u32[]{:S(2)}, u32[]{:S(2)}) collective-permute-start(bf16[16,128,256]{2,1,0:T(8,128)(2,1)S(1)} %bitcast.167), channel_id=1, source_target_pairs={{0,8},{8,0},{16,24},{24,16},{1,9},{9,1},{17,25},{25,17},{2,10},{10... | collective-permute-start | bytes 3145736 | tf_op jit(solution)/shard_map/ppermute | solution.py:666
  455.3 5.7 copy-start.21
  459.2 30.5 %collective-permute-start.22 = (bf16[4,128,1280]{2,1,0:T(8,128)(2,1)}, bf16[4,128,1280]{2,1,0:T(8,128)(2,1)S(1)}, u32[]{:S(2)}, u32[]{:S(2)}) collective-permute-start(bf16[4,128,1280]{2,1,0:T(8,128)(2,1)} %get-tuple-element.144.refs_0_), channel_id=1, source_target_pairs={{0,2},{1,3},{2,0},{3,1},{4,6},{5,7},{6,4},{7,5},{8,10},{9,11},{10,... | collective-permute-start | bytes 3932168 | tf_op jit(solution)/shard_map/ppermute | solution.py:666
  462.6 25.7 %collective-permute-start.18 = (bf16[4,272,512]{2,1,0:T(8,128)(2,1)}, bf16[4,272,512]{2,1,0:T(8,128)(2,1)S(1)}, u32[]{:S(2)}, u32[]{:S(2)}) collective-permute-start(bf16[4,272,512]{2,1,0:T(8,128)(2,1)} %get-tuple-element.145.refs_0_), channel_id=1, source_target_pairs={{0,1},{1,0},{2,3},{3,2},{4,5},{5,4},{6,7},{7,6},{8,9},{9,8},{10,11... | collective-permute-start | bytes 3342344 | tf_op jit(solution)/shard_map/ppermute | solution.py:666
  464.8 23.8 %collective-permute-start.17 = (bf16[8,128,256]{2,1,0:T(8,128)(2,1)S(1)}, bf16[8,128,256]{2,1,0:T(8,128)(2,1)S(1)}, u32[]{:S(2)}, u32[]{:S(2)}) collective-permute-start(bf16[8,128,256]{2,1,0:T(8,128)(2,1)S(1)} %get-tuple-element.146.refs_0_), channel_id=1, source_target_pairs={{0,16},{8,24},{16,0},{24,8},{1,17},{9,25},{17,1},{25,9},{2,18},{10... | collective-permute-start | bytes 1572872 | tf_op jit(solution)/shard_map/ppermute | solution.py:666
  479.3 37.7 %collective-permute-start.16 = (bf16[2,2,128,1024]{3,2,1,0:T(8,128)(2,1)S(1)}, bf16[2,2,128,1024]{3,2,1,0:T(8,128)(2,1)S(1)}, u32[]{:S(2)}, u32[]{:S(2)}) collective-permute-start(bf16[2,2,128,1024]{3,2,1,0:T(8,128)(2,1)S(1)} %pick.17.refs_0_), channel_id=1, source_target_pairs={{0,16},{8,24},{16,0},{24,8},{1,17},{9,25},{17,1},{25,9},{2,18},{10... | collective-permute-start | bytes 3145736 | tf_op jit(solution)/shard_map/ppermute | solution.py:666
  490.1 26.7 %copy-start.35 = (bf16[1,512,512]{2,1,0:T(8,128)(2,1)S(1)}, bf16[1,512,512]{2,1,0:T(8,128)(2,1)}, u32[]{:S(2)}) copy-start(bf16[1,512,512]{2,1,0:T(8,128)(2,1)} %copy-done.34) | copy-start | bytes 1572868
  490.1 27.9 %collective-permute-start.25 = (bf16[2,128,1280]{2,1,0:T(8,128)(2,1)S(1)}, bf16[2,128,1280]{2,1,0:T(8,128)(2,1)S(1)}, u32[]{:S(2)}, u32[]{:S(2)}) collective-permute-start(bf16[2,128,1280]{2,1,0:T(8,128)(2,1)S(1)} %get-tuple-element.155.refs_0_), channel_id=1, source_target_pairs={{0,1},{1,0},{2,3},{3,2},{4,5},{5,4},{6,7},{7,6},{8,9},{9,8},{10,11... | collective-permute-start | bytes 1966088 | tf_op jit(solution)/shard_map/ppermute | solution.py:666
  491.5 23.2 %collective-permute-start.21 = (bf16[2,272,512]{2,1,0:T(8,128)(2,1)S(1)}, bf16[2,272,512]{2,1,0:T(8,128)(2,1)S(1)}, u32[]{:S(2)}, u32[]{:S(2)}) collective-permute-start(bf16[2,272,512]{2,1,0:T(8,128)(2,1)S(1)} %get-tuple-element.149.refs_0_), channel_id=1, source_target_pairs={{0,2},{1,3},{2,0},{3,1},{4,6},{5,7},{6,4},{7,5},{8,10},{9,11},{10,... | collective-permute-start | bytes 1671176 | tf_op jit(solution)/shard_map/ppermute | solution.py:666
  493.0 23.7 %collective-permute-start.20 = (bf16[1,512,512]{2,1,0:T(8,128)(2,1)S(1)}, bf16[1,512,512]{2,1,0:T(8,128)(2,1)S(1)}, u32[]{:S(2)}, u32[]{:S(2)}) collective-permute-start(bf16[1,512,512]{2,1,0:T(8,128)(2,1)S(1)} %copy-done.37), channel_id=1, source_target_pairs={{0,4},{1,5},{2,6},{3,7},{4,0},{5,1},{6,2},{7,3},{8,12},{9,13},{10,... | collective-permute-start | bytes 1572872 | tf_op jit(solution)/shard_map/ppermute | solution.py:666
  494.5 22.3 %collective-permute-start.19 = (bf16[4,128,256]{2,1,0:T(8,128)(2,1)S(1)}, bf16[4,128,256]{2,1,0:T(8,128)(2,1)S(1)}, u32[]{:S(2)}, u32[]{:S(2)}) collective-permute-start(bf16[4,128,256]{2,1,0:T(8,128)(2,1)S(1)} %get-tuple-element.151.refs_0_), channel_id=1, source_target_pairs={{0,1},{1,0},{2,3},{3,2},{4,5},{5,4},{6,7},{7,6},{8,9},{9,8},{10,11... | collective-permute-start | bytes 786440 | tf_op jit(solution)/shard_map/ppermute | solution.py:666
  514.8 21.7 %collective-permute-start.24 = (bf16[1,272,512]{2,1,0:T(8,128)(2,1)S(1)}, bf16[1,272,512]{2,1,0:T(8,128)(2,1)S(1)}, u32[]{:S(2)}, u32[]{:S(2)}) collective-permute-start(bf16[1,272,512]{2,1,0:T(8,128)(2,1)S(1)} %get-tuple-element.156.refs_0_), channel_id=1, source_target_pairs={{0,4},{1,5},{2,6},{3,7},{4,0},{5,1},{6,2},{7,3},{8,12},{9,13},{10,... | collective-permute-start | bytes 835592 | tf_op jit(solution)/shard_map/ppermute | solution.py:666
  519.1 25.5 %collective-permute-start.30 = (bf16[1,128,1280]{2,1,0:T(8,128)(2,1)S(1)}, bf16[1,128,1280]{2,1,0:T(8,128)(2,1)S(1)}, u32[]{:S(2)}, u32[]{:S(2)}) collective-permute-start(bf16[1,128,1280]{2,1,0:T(8,128)(2,1)S(1)} %get-tuple-element.160.refs_0_), channel_id=1, source_target_pairs={{0,4},{1,5},{2,6},{3,7},{4,0},{5,1},{6,2},{7,3},{8,12},{9,13},{10,... | collective-permute-start | bytes 983048 | tf_op jit(solution)/shard_map/ppermute | solution.py:666
  520.3 16.3 %collective-permute-start.28 = (bf16[2,128,256]{2,1,0:T(8,128)(2,1)S(1)}, bf16[2,128,256]{2,1,0:T(8,128)(2,1)S(1)}, u32[]{:S(2)}, u32[]{:S(2)}) collective-permute-start(bf16[2,128,256]{2,1,0:T(8,128)(2,1)S(1)} %get-tuple-element.157.refs_2_), channel_id=1, source_target_pairs={{0,2},{1,3},{2,0},{3,1},{4,6},{5,7},{6,4},{7,5},{8,10},{9,11},{10,... | collective-permute-start | bytes 393224 | tf_op jit(solution)/shard_map/ppermute | solution.py:666
  536.6 26.4 %copy-start.32 = (bf16[1,272,512]{2,1,0:T(8,128)(2,1)}, bf16[1,272,512]{2,1,0:T(8,128)(2,1)S(1)}, u32[]{:S(2)}) copy-start(bf16[1,272,512]{2,1,0:T(8,128)(2,1)S(1)} %plus.7.refs_0_.left_ref) | copy-start | bytes 835588
  536.7 8.7 %collective-permute-start.29 = (bf16[1,128,256]{2,1,0:T(8,128)(2,1)S(1)}, bf16[1,128,256]{2,1,0:T(8,128)(2,1)S(1)}, u32[]{:S(2)}, u32[]{:S(2)}) collective-permute-start(bf16[1,128,256]{2,1,0:T(8,128)(2,1)S(1)} %get-tuple-element.163.refs_0_), channel_id=1, source_target_pairs={{0,4},{1,5},{2,6},{3,7},{4,0},{5,1},{6,2},{7,3},{8,12},{9,13},{10,... | collective-permute-start | bytes 196616 | tf_op jit(solution)/shard_map/ppermute | solution.py:666
  545.4 5.1 collective-permute-start.32
  546.3 15.4 %collective-permute-start.27 = (bf16[1,512,512]{2,1,0:T(8,128)(2,1)S(1)}, bf16[1,512,512]{2,1,0:T(8,128)(2,1)}, u32[]{:S(2)}, u32[]{:S(2)}) collective-permute-start(bf16[1,512,512]{2,1,0:T(8,128)(2,1)S(1)} %plus.6.refs_0_.left_ref), channel_id=1, source_target_pairs={{0,16},{8,24},{16,0},{24,8},{1,17},{9,25},{17,1},{25,9},{2,18},{10... | collective-permute-start | bytes 1572872 | tf_op jit(solution)/shard_map/ppermute | solution.py:666
  547.5 20.3 %collective-permute-start.26 = (bf16[1,272,512]{2,1,0:T(8,128)(2,1)S(1)}, bf16[1,272,512]{2,1,0:T(8,128)(2,1)}, u32[]{:S(2)}, u32[]{:S(2)}) collective-permute-start(bf16[1,272,512]{2,1,0:T(8,128)(2,1)S(1)} %plus.7.refs_0_.left_ref), channel_id=1, source_target_pairs={{0,16},{8,24},{16,0},{24,8},{1,17},{9,25},{17,1},{25,9},{2,18},{10... | collective-permute-start | bytes 835592 | tf_op jit(solution)/shard_map/ppermute | solution.py:666
  550.5 12.6 %copy-start.48 = (bf16[1,128,256]{2,1,0:T(8,128)(2,1)}, bf16[1,128,256]{2,1,0:T(8,128)(2,1)S(1)}, u32[]{:S(2)}) copy-start(bf16[1,128,256]{2,1,0:T(8,128)(2,1)S(1)} %get-tuple-element.212) | copy-start | bytes 196612
  551.2 18.7 %collective-permute-start.33 = (bf16[2,128,256]{2,1,0:T(8,128)(2,1)}, bf16[2,128,256]{2,1,0:T(8,128)(2,1)}, u32[]{:S(2)}, u32[]{:S(2)}) collective-permute-start(bf16[2,128,256]{2,1,0:T(8,128)(2,1)} %pad_maximum_fusion.2), channel_id=1, source_target_pairs={{0,8},{8,0},{16,24},{24,16},{1,9},{9,1},{17,25},{25,17},{2,10},{10... | collective-permute-start | bytes 393224 | tf_op jit(solution)/shard_map/ppermute | solution.py:666
  551.2 21.7 %collective-permute-start.34 = (bf16[128,1280]{1,0:T(8,128)(2,1)S(1)}, bf16[128,1280]{1,0:T(8,128)(2,1)}, u32[]{:S(2)}, u32[]{:S(2)}) collective-permute-start(bf16[128,1280]{1,0:T(8,128)(2,1)S(1)} %bitcast.165), channel_id=1, source_target_pairs={{0,16},{8,24},{16,0},{24,8},{1,17},{9,25},{17,1},{25,9},{2,18},{10... | collective-permute-start | bytes 983048 | tf_op jit(solution)/shard_map/ppermute | solution.py:666
  552.0 30.2 %collective-permute-start.23 = (bf16[2,2,128,1024]{3,2,1,0:T(8,128)(2,1)}, bf16[2,2,128,1024]{3,2,1,0:T(8,128)(2,1)}, u32[]{:S(2)}, u32[]{:S(2)}) collective-permute-start(bf16[2,2,128,1024]{3,2,1,0:T(8,128)(2,1)} %copy-done.30), channel_id=1, source_target_pairs={{0,8},{8,0},{16,24},{24,16},{1,9},{9,1},{17,25},{25,17},{2,10},{10... | collective-permute-start | bytes 3145736 | tf_op jit(solution)/shard_map/ppermute | solution.py:666
  563.0 14.6 %collective-permute-start.36 = (bf16[512,512]{1,0:T(8,128)(2,1)S(1)}, bf16[512,512]{1,0:T(8,128)(2,1)S(1)}, u32[]{:S(2)}, u32[]{:S(2)}) collective-permute-start(bf16[512,512]{1,0:T(8,128)(2,1)S(1)} %bitcast.160), channel_id=1, source_target_pairs={{0,8},{8,0},{16,24},{24,16},{1,9},{9,1},{17,25},{25,17},{2,10},{10... | collective-permute-start | bytes 1572872 | tf_op jit(solution)/shard_map/ppermute | solution.py:666
  569.7 5.2 collective-permute-start.31
  574.9 11.0 %collective-permute-start.35 = (bf16[2,128,1280]{2,1,0:T(8,128)(2,1)}, bf16[2,128,1280]{2,1,0:T(8,128)(2,1)}, u32[]{:S(2)}, u32[]{:S(2)}) collective-permute-start(bf16[2,128,1280]{2,1,0:T(8,128)(2,1)} %pad_maximum_fusion), channel_id=1, source_target_pairs={{0,8},{8,0},{16,24},{24,16},{1,9},{9,1},{17,25},{25,17},{2,10},{10... | collective-permute-start | bytes 1966088 | tf_op jit(solution)/shard_map/ppermute | solution.py:666
  (35 other events, 75.3 us)
Sparse Core Ops, SparseCore 0:
  11.6 86.3 all-gather.4
  100.9 123.5 all-gather.6

commit v3 on v2

--- a/solution.py
+++ b/solution.py
@@ -399,7 +399,7 @@
 
 
 def down_grad_kernel(half_ref, near_ref, far_ref, active_ref, *refs):
-    out_near, out_far, turned = refs[-3:]
+    out_near, *out_far, turned = refs[-4:]
     columns = near_ref.shape[1]
 
     @pl.when(pl.program_id(0) == 0)
@@ -413,20 +413,23 @@
         at = placed(part, range(bits_of(group)))
         span = slice(part * deep, (part + 1) * deep)
         out_near[at, 0] = result[:columns, span]
-        out_far[at, 0] = result[columns:, span]
+        out_far[at // (group // 2)][at % (group // 2), 0] = result[columns:, span]
 
 
 def down_grad(half, active, d_branch, parts, order, after):
     rows, inner_width = active.shape
     columns = d_branch.shape[1] // 2
     deep = inner_width // parts
-    group = max(1, 1024 // deep)
+    group = max(2, 1024 // deep)
     steps = parts // group
     low = bits_of(group)
     order = tuple(range(low)) + tuple(bit for bit in order if bit >= low)
     high = [bit - low for bit in order[low:]]
-    out = pl.BlockSpec((group, 1, columns, deep), lambda i, half: (0, placed(i, high), 0, 0))
-    near, far = pl.pallas_call(
+
+    def spec(count):
+        return pl.BlockSpec((count, 1, columns, deep), lambda i, half: (0, placed(i, high), 0, 0))
+
+    near, *far = pl.pallas_call(
         down_grad_kernel,
         grid_spec=pltpu.PrefetchScalarGridSpec(
             num_scalar_prefetch=1,
@@ -437,45 +440,48 @@
                 pl.BlockSpec((rows, group * deep), lambda i, half: (0, i)),
             ]
             + [ANYWHERE] * len(after),
-            out_specs=[out, out],
+            out_specs=[spec(group), spec(group // 2), spec(group // 2)],
             scratch_shapes=[pltpu.VMEM((2 * columns, rows), LOW)],
         ),
-        out_shape=[struct((group, steps, columns, deep))] * 2,
+        out_shape=[struct((group, steps, columns, deep))]
+        + [struct((group // 2, steps, columns, deep))] * 2,
         compiler_params=params(60),
         cost_estimate=cost(4 * rows * inner_width * columns, 4 * rows * inner_width),
         name="down_grad",
     )(half, d_branch, d_branch, active, *after)
-    return near.reshape(parts, columns, deep), far.reshape(parts, columns, deep), order
-
-
-def spread(result, out_ref, order):
-    rows = result.shape[0] // 2 ** len(order)
-    for part in range(2 ** len(order)):
-        out_ref[placed(part, order)] = result[part * rows : (part + 1) * rows]
+    return near.reshape(parts, columns, deep), [
+        member.reshape(parts // 2, columns, deep) for member in far
+    ], order
+
+
+def spread(result, outs, order):
+    parts = 2 ** len(order)
+    rows, each = result.shape[0] // parts, parts // len(outs)
+    for part in range(parts):
+        at = placed(part, order)
+        outs[at // each][at % each] = result[part * rows : (part + 1) * rows]
 
 
 def output_grad_kernel(half_ref, context_ref, *refs, order, chips):
-    grads, (far_ref, near_ref, turned) = refs[:2], refs[-3:]
+    grads, outs, turned = refs[:2], refs[-chips - 2 : -1], refs[-1]
     at = pl.program_id(0)
 
     @pl.when(at == 0)
     def _():
         turned[...] = context_ref[...].T
-        spread(dot(turned[...], grads[0][...], NN).astype(LOW), far_ref.at[0], order)
-
-    for chip in range(chips):
-        for side, out_ref in ((0, far_ref), (1, near_ref)):
-            if chip + side > 0:
-
-                @pl.when(at == side * chips + chip)
-                def _():
-                    spread(dot(turned[...], grads[side][...], NN).astype(LOW), out_ref.at[0], order)
+
+    for step in range(2 * chips):
+
+        @pl.when(at == step)
+        def _():
+            result = dot(turned[...], grads[step // chips][...], NN).astype(LOW)
+            spread(result, [outs[min(step, chips)].at[0]], order)
 
 
 def output_grad(half, context, d_attn, near, far, parts, ranks, order, after):
     rows, width = context.shape
     chips, narrow, own = ranks // 2, width // ranks, width // parts
-    shape = (chips, parts, own, near.shape[2])
+    shape = (1, parts, own, near.shape[2])
     last = shape[3] // narrow - 1
     block = (1, parts, own, narrow)
 
@@ -485,7 +491,8 @@
     def near_at(i):
         return jnp.maximum(i - chips, 0)
 
-    far, near = pl.pallas_call(
+    near_shape = (chips,) + shape[1:]
+    *far, near = pl.pallas_call(
         functools.partial(output_grad_kernel, order=order, chips=chips),
         grid_spec=pltpu.PrefetchScalarGridSpec(
             num_scalar_prefetch=1,
@@ -495,35 +502,42 @@
                 pl.BlockSpec((rows, narrow), lambda i, half: (0, 2 * far_at(i) + 1 - half[0])),
                 pl.BlockSpec((rows, narrow), lambda i, half: (0, 2 * near_at(i) + half[0])),
             ]
-            + [ANYWHERE] * (2 + len(after)),
-            out_specs=[
-                pl.BlockSpec(block, lambda i, half: (far_at(i), 0, 0, last)),
-                pl.BlockSpec(block, lambda i, half: (near_at(i), 0, 0, last)),
-            ],
+            + [ANYWHERE] * (1 + chips + len(after)),
+            out_specs=[pl.BlockSpec(block, lambda i, half: (0, 0, 0, last))] * chips
+            + [pl.BlockSpec(block, lambda i, half: (near_at(i), 0, 0, last))],
             scratch_shapes=[pltpu.VMEM((width, rows), LOW)],
         ),
-        out_shape=[struct(shape)] * 2,
-        input_output_aliases={4: 0, 5: 1},
-        compiler_params=params(40),
+        out_shape=[struct(shape)] * chips + [struct(near_shape)],
+        input_output_aliases={4 + at: at for at in range(chips + 1)},
+        compiler_params=params(60),
         cost_estimate=cost(2 * rows * width * width, 6 * rows * width),
         name="output_grad",
-    )(half, context, d_attn, d_attn, far.reshape(shape), near.reshape(shape), *after)
-    return [member.reshape(-1, own, shape[3]) for member in (near, far)]
+    )(
+        half,
+        context,
+        d_attn,
+        d_attn,
+        *[member.reshape(shape) for member in far],
+        near.reshape(near_shape),
+        *after,
+    )
+    return near.reshape(-1, own, shape[3]), [member[0] for member in far]
 
 
 def up_grad_kernel(half_ref, hidden_ref, grad_ref, *refs, order, chips):
-    far_ref, near_ref, turned = refs[-3:]
+    outs, turned = refs[-chips - 2 : -1], refs[-1]
     at = pl.program_id(0)
 
     @pl.when(at == 0)
     def _():
         turned[...] = hidden_ref[...].T
 
-    for first, out_ref in ((0, far_ref), (chips, near_ref)):
-
-        @pl.when((at >= first) & (at < first + chips))
+    for step in range(2 * chips):
+
+        @pl.when(at == step)
         def _():
-            spread(dot(turned[...], grad_ref[...], NN).astype(LOW), out_ref.at[0], order)
+            result = dot(turned[...], grad_ref[...], NN).astype(LOW)
+            spread(result, [outs[min(step, chips)].at[0]], order)
 
 
 def up_grad(half, hidden_low, d_inner, parts, ranks, order, extra, after):
@@ -536,7 +550,8 @@
         return 0, jnp.where(far, 2 * i + 1 - half[0], 2 * (i - chips) + half[0])
 
     block = (1, parts, width // parts, columns)
-    far, near = pl.pallas_call(
+    shape = block[1:3] + (columns + extra,)
+    *far, near = pl.pallas_call(
         functools.partial(up_grad_kernel, order=order, chips=chips),
         grid_spec=pltpu.PrefetchScalarGridSpec(
             num_scalar_prefetch=1,
@@ -546,89 +561,78 @@
                 pl.BlockSpec((rows, columns), column),
             ]
             + [ANYWHERE] * len(after),
-            out_specs=[
-                pl.BlockSpec(block, lambda i, half: (jnp.minimum(i, chips - 1), 0, 0, 0)),
-                pl.BlockSpec(block, lambda i, half: (jnp.maximum(i - chips, 0), 0, 0, 0)),
-            ],
+            out_specs=[pl.BlockSpec(block, lambda i, half: (0, 0, 0, 0))] * chips
+            + [pl.BlockSpec(block, lambda i, half: (jnp.maximum(i - chips, 0), 0, 0, 0))],
             scratch_shapes=[pltpu.VMEM((width, rows), LOW)],
         ),
-        out_shape=[struct((chips,) + block[1:3] + (columns + extra,))] * 2,
+        out_shape=[struct((1,) + shape)] * chips + [struct((chips,) + shape)],
         compiler_params=params(60),
         cost_estimate=cost(2 * rows * width * columns * ranks, 4 * rows * columns * ranks),
         name="up_grad",
     )(half, hidden_low, d_inner, *after)
-    return [member.reshape(-1, width // parts, columns + extra) for member in (near, far)]
-
-
-def input_grad_kernel(half_ref, tok_ref, *refs, order, chips):
-    grads, outs, turned = refs[:6], refs[-5:-1], refs[-1]
+    return near.reshape((-1,) + shape[1:]), [member[0] for member in far]
+
+
+def input_grad_kernel(half_ref, tok_ref, *refs, orders):
+    grads, turned = refs[:6], refs[-1]
+    far_low, far_high, far_keys, near, near_keys = refs[-6:-1]
+    outs = [far_low, far_high], [far_keys], [near], [near_keys]
     at = pl.program_id(0)
 
     @pl.when(at == 0)
     def _():
         turned[...] = tok_ref[...].T
 
+    for step in range(6):
+
+        @pl.when(at == step)
+        def _():
+            result = dot(turned[...], grads[step][...], NN).astype(LOW)
+            keys = step % 3 == 2
+            spread(result, outs[step // 3 * 2 + keys], orders[keys])
+
+
+def input_grad(half, tok, d_query, d_values, d_keys, parts, orders, after):
+    rows, width = tok.shape
+    columns, own = width // 2, width // parts
+    deep = 2 * own + PAD
+    ins = []
     for side in range(2):
-        for step in range(2 + chips):
-
-            @pl.when(at == side * (2 + chips) + step)
-            def _():
-                grad_ref = grads[3 * side + min(step, 2)]
-                out_ref = outs[2 * side] if step < 2 else outs[2 * side + 1].at[0]
-                spread(dot(turned[...], grad_ref[...], NN).astype(LOW), out_ref, order)
-
-
-def input_grad(half, tok, d_query, d_values, d_keys, parts, ranks, order, after):
-    rows, width = tok.shape
-    columns, narrow = width // 2, width // ranks
-    own = width // parts
-    chips = ranks // 2
-    steps = 2 + chips
-
-    def key_at(i, side):
-        return jnp.clip(i - side * steps - 2, 0, chips - 1)
-
-    ins, out_specs, outs = [], [], []
-    for side in range(2):
-
-        def core(half, side=side):
-            return half[0] if side else 1 - half[0]
-
-        ins += [pl.BlockSpec((rows, columns), lambda i, half, core=core: (0, core(half)))] * 2
-        ins += [
-            pl.BlockSpec(
-                (rows, narrow),
-                lambda i, half, core=core, side=side: (0, 2 * key_at(i, side) + core(half)),
-            )
-        ]
-        out_specs += [
-            pl.BlockSpec(
-                (parts, own, columns),
-                lambda i, half, side=side: (0, jnp.clip(i - side * steps, 0, 1), 0),
-            ),
-            pl.BlockSpec(
-                (1, parts, own, narrow), lambda i, half, side=side: (key_at(i, side), 0, 0, 0)
-            ),
-        ]
-        outs += [struct((parts, 2 * own + PAD, columns)), struct((chips, parts, own, narrow))]
-    far, far_keys, near, near_keys = pl.pallas_call(
-        functools.partial(input_grad_kernel, order=order, chips=chips),
+
+        def column(i, half, side=side):
+            return 0, half[0] if side else 1 - half[0]
+
+        ins += [pl.BlockSpec((rows, columns), column)] * 3
+
+    def spec(count, side):
+        return pl.BlockSpec(
+            (count, own, columns), lambda i, half: (0, jnp.clip(i - 3 * side, 0, 1), 0)
+        )
+
+    keys = pl.BlockSpec((parts, own, columns), lambda i, half: (0, 0, 0))
+    far_low, far_high, far_keys, near, near_keys = pl.pallas_call(
+        functools.partial(input_grad_kernel, orders=orders),
         grid_spec=pltpu.PrefetchScalarGridSpec(
             num_scalar_prefetch=1,
-            grid=(2 * steps,),
+            grid=(6,),
             in_specs=[pl.BlockSpec((rows, width), lambda i, half: (0, 0))]
             + ins
             + [ANYWHERE] * len(after),
-            out_specs=out_specs,
+            out_specs=[spec(parts // 2, 0), spec(parts // 2, 0), keys, spec(parts, 1), keys],
             scratch_shapes=[pltpu.VMEM((width, rows), LOW)],
         ),
-        out_shape=outs,
-        compiler_params=params(40),
+        out_shape=[
+            struct((parts // 2, deep, columns)),
+            struct((parts // 2, deep, columns)),
+            struct((parts, own, columns)),
+            struct((parts, deep, columns)),
+            struct((parts, own, columns)),
+        ],
+        compiler_params=params(60),
         cost_estimate=cost(6 * rows * width * width, 10 * rows * width),
         name="input_grad",
     )(half, tok, *[d_query, d_values, d_keys] * 2, *after)
-    shape = (-1, own, narrow)
-    return near, far, near_keys.reshape(shape), far_keys.reshape(shape)
+    return near, [far_low, far_high], near_keys, far_keys
 
 
 def tokens_grad_kernel(d_pre_ref, dq_ref, dk_ref, dv_ref, held_ref, *refs, parts, ranks):
@@ -655,7 +659,7 @@
         out_specs=row,
         out_shape=struct((rows, width)),
         scratch_shapes=[pltpu.VMEM((width, 3 * width), LOW), pltpu.SemaphoreType.DMA],
-        compiler_params=params(40),
+        compiler_params=params(60),
         cost_estimate=cost(6 * rows * width * width, 18 * rows * width),
         name="tokens_grad",
     )(d_pre_one, *grads, held, *after)
@@ -702,10 +706,24 @@
     )(jnp.stack([jnp.int32(at) for at in picks]), spots, *arrays, *after)
 
 
-def settle_kernel(side_ref, keep_ref, keep_far, came_ref, came_far, *refs):
+def settle_kernel(side_ref, keep_ref, keep_far, low_ref, high_ref, *refs, swapped):
     out_ref, send_ref = refs[-2:]
-    send_ref[...] = (keep_far[...].astype(WIDE) + came_far[...].astype(WIDE)).astype(LOW)
-    out_ref[...] = (keep_ref[...].astype(WIDE) + came_ref[...].astype(WIDE)).astype(LOW)
+
+    def add(near, far):
+        send_ref[...] = (keep_far[...].astype(WIDE) + far[...].astype(WIDE)).astype(LOW)
+        out_ref[...] = (keep_ref[...].astype(WIDE) + near[...].astype(WIDE)).astype(LOW)
+
+    if not swapped:
+        add(low_ref, high_ref)
+        return
+
+    @pl.when(side_ref[0] == 0)
+    def _():
+        add(low_ref, high_ref)
+
+    @pl.when(side_ref[0] == 1)
+    def _():
+        add(high_ref, low_ref)
 
 
 def settle(keep, came, side, after):
@@ -714,19 +732,20 @@
     near = pl.BlockSpec(block, lambda i, side: (side[0] * half + i, 0, 0))
     far = pl.BlockSpec(block, lambda i, side: ((1 - side[0]) * half + i, 0, 0))
     out = pl.BlockSpec(block, lambda i, side: (i, 0, 0))
+    whole = len(came) == 1
     return pl.pallas_call(
-        settle_kernel,
+        functools.partial(settle_kernel, swapped=not whole),
         grid_spec=pltpu.PrefetchScalarGridSpec(
             num_scalar_prefetch=1,
             grid=(half,),
-            in_specs=[near, far, near, far] + [ANYWHERE] * len(after),
+            in_specs=[near, far] + ([near, far] if whole else [out, out]) + [ANYWHERE] * len(after),
             out_specs=[out, out],
         ),
         out_shape=[struct((half,) + keep.shape[1:])] * 2,
-        compiler_params=params(40),
+        compiler_params=params(60 if 2 * math.prod(keep.shape) > 3 << 20 else 40),
         cost_estimate=cost(0, 6 * math.prod(keep.shape)),
         name="settle",
-    )(side, keep, keep, came, came, *after)
+    )(side, keep, keep, *(came * 2 if whole else came), *after)
 
 
 def plus_kernel(left_ref, right_ref, *refs):
@@ -758,24 +777,22 @@
 
 
 class Reduce:
-    def __init__(self, order, route, keep, send):
+    def __init__(self, order, route, keep, *send):
         self.order, self.route = order, list(route)
         self.keep = keep
-        self.came = swap(send, "ctx", 0)
+        self.came = [swap(member, "ctx", 0) for member in send]
 
     def step(self):
         axis, bit = self.route.pop(0)
         if self.keep.shape[0] == 1:
-            self.keep = self.order(plus, self.keep, self.came)
-            self.came = swap(self.keep, axis, bit)
-            return
-        side = bit_of(axis, bit).reshape(1)
-        self.keep, send = self.order(settle, self.keep, self.came, side)
-        self.came = swap(send, axis, bit)
+            self.keep = send = self.order(plus, self.keep, self.came[0])
+        else:
+            side = bit_of(axis, bit).reshape(1)
+            self.keep, send = self.order(settle, self.keep, self.came, side)
+        self.came = [swap(send, axis, bit)]
 
     def last(self):
-        self.keep = self.order(plus, self.keep, self.came)
-        return self.keep[0]
+        return self.order(plus, self.keep, self.came[0])[0]
 
 
 def both(value, axis, bit):
@@ -805,16 +822,17 @@
 class Positions:
     def __init__(self, order, value):
         self.order, self.value = order, value
-        spots = jnp.arange(2, dtype=jnp.int32)
-        self.came = swap(order(pick, (value, value), (2, 3), spots), "ctx", 1)
+        send = order(pick, (value, value), (1, 3), jnp.arange(2, dtype=jnp.int32))
+        self.came = swap(send, "ctx", 0)
 
     def step(self):
         spots = jnp.arange(2, dtype=jnp.int32)
-        self.late = swap(self.order(pick, (self.value, self.came), (1, 1), spots), "ctx", 0)
+        send = self.order(pick, (self.value, self.came), (2, 1), spots)
+        self.late = swap(send, "ctx", 1)
 
     def last(self):
-        arrays = (self.value, self.late, self.came, self.late)
         around = lax.axis_index("ctx") ^ jnp.arange(4, dtype=jnp.int32)
+        arrays = (self.value, self.came, self.late, self.late)
         return self.order(pick, arrays, (0, 0, 0, 1), around)
 
 
@@ -930,30 +948,33 @@
     chip = [("ctx", 1)]
     turned = upward[1:2] + upward[:1] + upward[2:]
 
-    down_mine, down_other, down_turn = down_grad(mine, active, d_branch, parts, turned, ())
-    order.after = (down_other,)
-    down_sum = Reduce(order, [("fsdp", bit) for bit in down_turn] + chip, down_mine, down_other)
+    up_mine, up_other = up_grad(
+        mine, hidden_low, d_inner, parts, ranks, upward, width // ranks, ()
+    )
+    up_mine, up_other = output_grad(
+        mine, context, d_attn, up_mine, up_other, parts, ranks, upward, ()
+    )
+    order.after = (up_mine,)
+    up_sum = Reduce(order, chip + shards, up_mine, *up_other)
+    down_mine, down_other, down_turn = order(down_grad, mine, active, d_branch, parts, upward)
+    order.after = (down_mine,)
+    down_sum = Reduce(
+        order, [("fsdp", bit) for bit in down_turn] + chip, down_mine, *down_other
+    )
+    up_sum.step()
+    down_sum.step()
+
     layer_out = Positions(order, layer_out.reshape(shape))
-    up_mine, up_other = order(
-        up_grad, mine, hidden_low, d_inner, parts, ranks, turned, width // ranks
-    )
-    down_sum.step()
-    layer_out.step()
-    up_mine, up_other = order(
-        output_grad, mine, context, d_attn, up_mine, up_other, parts, ranks, turned
-    )
-    up_sum = Reduce(order, chip + [("fsdp", bit) for bit in turned], up_mine, up_other)
-    up_sum.step()
-
     begun = ()
     for share in range(2 * shape[1]):
         begun = order(attend_backward, query, keys, values, d_context, shape, share, begun)[:5]
-        if share == 0:
-            layer_out = layer_out.last()
-        if share == shape[1] - 1:
-            down_sum.step()
     d_query, d_keys, d_values = [member.reshape(rows, width) for member in begun[:3]]
+    up_sum.step()
     down_sum.step()
+    tokens_grad = order(
+        tokens_grad_of, d_pre_one, (d_query, d_keys, d_values), attn, parts, ranks
+    )
+    tokens_grad = Positions(order, tokens_grad.reshape(shape))
     small_in = packed(
         [
             member.reshape(-1, 8, width)[:, 0].sum(axis=0).reshape(parts, own)
@@ -965,42 +986,46 @@
         half,
     )
 
+    orders = upward, turned
     near, far, near_keys, far_keys = order(
-        input_grad, mine, tok_rows, d_query, d_values, d_keys, parts, ranks, upward
-    )
-    near, far = [
-        lax.dynamic_update_slice(
-            held,
-            lax.dynamic_index_in_dim(small_in, side[0], 1, keepdims=False),
-            (0, 2 * own, 0),
-        )
-        for held, side in ((near, mine), (far, other))
-    ]
-    input_sum = Reduce(order, shards + chip, near, far)
-    keys_sum = Reduce(order, chip + shards, near_keys, far_keys)
+        input_grad, mine, tok_rows, d_query, d_values, d_keys, parts, orders
+    )
+    def with_vectors(held, side, first):
+        extra = lax.dynamic_index_in_dim(small_in, side[0], 1, keepdims=False)
+        extra = extra[first : first + held.shape[0]]
+        return lax.dynamic_update_slice(held, extra, (0, 2 * own, 0))
+
+    near = with_vectors(near, mine, 0)
+    far = [with_vectors(member, other, at * parts // 2) for at, member in enumerate(far)]
+    input_sum = Reduce(order, shards + chip, near, *far)
+    keys_sum = Reduce(order, [("fsdp", bit) for bit in turned] + chip, near_keys, far_keys)
     up_sum.step()
+    down_sum.step()
+    tokens_grad.step()
     input_sum.step()
     keys_sum.step()
-    tokens_grad = order(
-        tokens_grad_of, d_pre_one, (d_query, d_keys, d_values), attn, parts, ranks
-    )
-    tokens_grad = Positions(order, tokens_grad.reshape(shape))
-    turns = [input_sum, keys_sum, up_sum, input_sum, down_sum, keys_sum, tokens_grad, up_sum]
-    turns += [input_sum, keys_sum, down_sum, input_sum]
-    for chain in turns:
-        if not isinstance(chain, Reduce) or chain.route:
-            chain.step()
-    chains = [up_sum, down_sum, input_sum, keys_sum]
-    while any(chain.route for chain in chains):
-        for chain in chains:
+    up_sum.step()
+    down_sum.step()
+    layer_out.step()
+    input_sum.step()
+    keys_sum.step()
+    tokens_grad = tokens_grad.last()
+    late = layer_out
+    chains = {"up": up_sum, "down": down_sum, "input": input_sum, "keys": keys_sum}
+    done = {}
+    while chains:
+        for name, chain in list(chains.items()):
             if chain.route:
                 chain.step()
-    up_done = up_sum.last()
-    keys_done = keys_sum.last()
-    down_done = down_sum.last()
-    input_done = input_sum.last()
-    tokens_grad = tokens_grad.last()
+            else:
+                done[name] = chain.last()
+                del chains[name]
+        if late is not None:
+            layer_out, late = late.last(), None
     layer_out, tokens_grad = [member.reshape(tokens.shape) for member in (layer_out, tokens_grad)]
+    up_done, down_done, input_done, keys_done = [
+        done[name] for name in ("up", "down", "input", "keys")
+    ]
 
     def across(value):
         lower, upper = both(jnp.stack(both(value, "ctx", 1)), "ctx", 0)
@@ -1017,11 +1042,9 @@
     up_result = joined([member[:, :span] for member in blocks])
     output_result = joined([member[:, span:] for member in blocks])
 
-    sides = both(input_done, "ctx", 0)
-    query_result, value_result = [
-        joined([side[at * own : (at + 1) * own] for side in sides]) for at in range(2)
-    ]
-    input_result = jnp.concatenate([query_result, joined(across(keys_done)), value_result], axis=1)
+    sides, keys_sides = both(input_done, "ctx", 0), both(keys_done, "ctx", 0)
+    query_result, value_result = [[side[at * own : (at + 1) * own] for side in sides] for at in range(2)]
+    input_result = joined([*query_result, *keys_sides, *value_result])
     flat = jnp.concatenate([side[2 * own :].reshape(-1) for side in sides]).astype(WIDE)
     eight = [flat[at * own : (at + 1) * own] for at in range(8)]
     up_bias_grad = flat[8 * own : 8 * own + deep]

time: 602 us -> 565 us (0.939)
  waiting for transfers between devices: 250 us -> 202 us
  Pallas kernels: 245 us -> 263 us
    ppermute x37 -> x39, waiting for transfers between devices: 156 us -> 108 us  [swap(): lax.ppermute(value, axis, [(at, at ^ 1 << bit) for at in range(count)])]
    pallas_call x15 -> x14, Pallas kernels: 32.4 us -> 46 us  [the longest x13 32.2 us: settle(): pl.pallas_call(functools.partial(settle_kernel, swapped=not whole), grid_...]
    unnamed x134 -> x118, local copies, waits for them, and re-layouts: 29.8 us -> 25.7 us
    ppermute x37 -> x39, starting transfers between devices: 35.6 us -> 32.4 us  [swap(): lax.ppermute(value, axis, [(at, at ^ 1 << bit) for at in range(count)])]
  transfers between devices with their start and end apart: 39 -> 41, of which waited for: 20 -> 16; matrix products, arithmetic and copies ran while one was open for 3% -> 4% of each run, Pallas kernels for 26% -> 31%
where the time goes in v3:
time: 565 us; the launch traced here: 559 us
  Pallas kernels  263 us (47%)
  waiting for transfers between devices  202 us (36%)
  local copies, waits for them, and re-layouts  32.6 us (6%)
  starting transfers between devices  32.4 us (6%)
  between operations  15.3 us (3%)
  other arithmetic  13.7 us (2%)
    ppermute x39, waiting for transfers between devices, swap(): lax.ppermute(value, axis, [(at, at ^ 1 << bit) for at in range(count)])  108 us
    all_gather x1, waiting for transfers between devices, local(): lax.all_gather(jnp.concatenate([columns_of(up_weight, rank, ranks), colum...  93.9 us
    pallas_call x1, Pallas kernels, middle(): pl.pallas_call(functools.partial(middle_kernel, parts=parts, ranks=ranks,...  67.3 us
    pallas_call x4, Pallas kernels, attend_backward(): pl.pallas_call(attend_backward_kernel, grid=(pairs,), in_specs=[spec] * 4...  47.3 us
    ppermute x39, starting transfers between devices, swap(): lax.ppermute(value, axis, [(at, at ^ 1 << bit) for at in range(count)])  32.4 us
    pallas_call x13, Pallas kernels, settle(): pl.pallas_call(functools.partial(settle_kernel, swapped=not whole), grid_...  32.2 us
    unnamed x118, local copies, waits for them, and re-layouts  25.7 us
    pallas_call x10, Pallas kernels, pick(): pl.pallas_call(functools.partial(pick_kernel, count=count), grid_spec=plt...  21.1 us
  transfers between devices with their start and end apart: 41, of which 16 were waited for; matrix products, arithmetic and copies ran while one was open for 4% of the time, Pallas kernels for 31%

profile of v3, /device:TPU:0, one launch (start us, length us, event | category | flops | bytes accessed | tf_op | source)
XLA Modules:
  0.0 558.6 jit_solution(9552198618897811623)
XLA Ops:
  12.1 3.0 collective-permute-start.1
  15.1 1.6 collective-permute-done.1
  16.7 2.1 collective-permute-start.2
  19.9 1.5 collective-permute-start
  21.5 2.7 collective-permute-start.3
  24.2 2.0 collective-permute-done.3
  26.2 23.3 %collective-permute-done.refs_1_.refs_2_ = bf16[2,2,128,1024]{3,2,1,0:T(8,128)(2,1)} collective-permute-done((bf16[2,2,128,1024]{3,2,1,0:T(8,128)(2,1)}, bf16[2,2,128,1024]{3,2,1,0:T(8,128)(2,1)}, u32[]{:S(2)}, u32[]{:S(2)}) %collective-permute-start) | collective-permute-done | bytes 1048608 | tf_op jit(solution)/shard_map/ppermute | solution.py:670
  49.5 2.7 pick.10.refs_4_
  53.2 2.5 collective-permute-start.5
  55.8 1.6 copy-done.8
  57.4 1.9 pick.11.refs_2_
  59.3 31.7 %collective-permute-done.5.refs_1_.refs_2_ = bf16[2,2,128,1024]{3,2,1,0:T(8,128)(2,1)} collective-permute-done((bf16[2,2,128,1024]{3,2,1,0:T(8,128)(2,1)}, bf16[2,2,128,1024]{3,2,1,0:T(8,128)(2,1)}, u32[]{:S(2)}, u32[]{:S(2)}) %collective-permute-start.5) | collective-permute-done | bytes 1048608 | tf_op jit(solution)/shard_map/ppermute | solution.py:670
  91.1 1.7 pick.12.refs_4_
  95.6 1.9 pick.13.refs_0_
  98.8 11.9 %merge.1 = (bf16[1024,1024]{1,0:T(8,128)(2,1)}, bf16[1024,1024]{1,0:T(8,128)(2,1)}, bf16[1024,1024]{1,0:T(8,128)(2,1)}) custom-call(bf16[1024,1024]{1,0:T(8,128)(2,1)} %bitcast.118, bf16[3,1024]{1,0:T(4,128)(2,1)} %slice_bitcast_fusion.7.bias_ref, bf16[32,128,768]{2,1,0:T(8,128)(2,1)} %bitcast.172, bf16[4,2,128,1024]{3,2,1,0:T(8,128)(2,1)} %copy-done.6), custom_call_target="tpu_custom_call" | custom-call | flops 402653184 | bytes 917504 | tf_op jit(solution)/shard_map/merge/pallas_call | solution.py:105
  110.7 19.9 %attend_forward.1 = bf16[4,2,128,1024]{3,2,1,0:T(8,128)(2,1)} custom-call(bf16[4,2,128,1024]{3,2,1,0:T(8,128)(2,1)} %bitcast.150, bf16[4,2,128,1024]{3,2,1,0:T(8,128)(2,1)} %bitcast.155, bf16[4,2,128,1024]{3,2,1,0:T(8,128)(2,1)} %bitcast.160), custom_call_target="tpu_custom_call" | custom-call | flops 536870912 | bytes 524288 | tf_op jit(solution)/shard_map/attend_forward/pallas_call | solution.py:143
  130.6 93.9 %all-gather.7.cloned.1.call-done = bf16[4096,2304]{1,0:T(8,128)(2,1)} async-done(((bf16[128,2304]{1,0:T(8,128)(2,1)}), bf16[4096,2304]{1,0:T(8,128)(2,1)}) %all-gather.7.cloned.1.call-update) | async-done | bytes 18874384 | tf_op jit(solution)/shard_map/all_gather | solution.py:905
  224.4 67.3 %middle.1 = (bf16[1024,1024]{1,0:T(8,128)(2,1)}, bf16[1024,1024]{1,0:T(8,128)(2,1)}, bf16[1024,4096]{1,0:T(8,128)(2,1)}, bf16[1024,1024]{1,0:T(8,128)(2,1)}, bf1...) custom-call(bf16[1024,1024]{1,0:T(8,128)(2,1)} %bitcast.174, ...), custom_call_target="tpu_custom_call" | custom-call | flops 2415919104 | bytes 4718592 | tf_op jit(solution)/shard_map/middle/pallas_call | solution.py:378
  291.8 14.5 %up_grad.1 = (bf16[1,8,128,1280]{3,2,1,0:T(8,128)(2,1)}, bf16[1,8,128,1280]{3,2,1,0:T(8,128)(2,1)}, bf16[2,8,128,1280]{3,2,1,0:T(8,128)(2,1)}) custom-call(s32[1]{0:T(128)} %bitcast.1.half_ref, bf16[1024,1024]{1,0:T(8,128)(2,1)} %get-tuple-element.99.hidden_ref, bf16[1024,4096]{1,0:T(8,128)(2,1)} %get-tuple-element.100.grad_ref), custom_call_target="tpu_custom_call" | custom-call | flops 536870912 | bytes 1048576 | tf_op jit(solution)/shard_map/up_grad/pallas_call | solution.py:554
  306.3 6.6 %output_grad.1 = (bf16[1,8,128,1280]{3,2,1,0:T(8,128)(2,1)}, bf16[1,8,128,1280]{3,2,1,0:T(8,128)(2,1)}, bf16[2,8,128,1280]{3,2,1,0:T(8,128)(2,1)}) custom-call(s32[1]{0:T(128)} %bitcast.1.half_ref, bf16[1024,1024]{1,0:T(8,128)(2,1)} %bitcast.175, ...), custom_call_target="tpu_custom_call", output_to_operand_aliasing={{0}: (4, {}), {1}: (5, {}), {2}: (6, {})} | custom-call | flops 134217728 | bytes 393216 | tf_op jit(solution)/shard_map/output_grad/pallas_call | solution.py:495
  313.4 13.7 %down_grad.1 = (bf16[2,4,512,512]{3,2,1,0:T(8,128)(2,1)}, bf16[1,4,512,512]{3,2,1,0:T(8,128)(2,1)}, bf16[1,4,512,512]{3,2,1,0:T(8,128)(2,1)}) custom-call(s32[1]{0:T(128)} %bitcast.1.half_ref, bf16[1024,1024]{1,0:T(8,128)(2,1)} %get-tuple-element.96.near_ref.far_ref, bf16[1024,1024]{1,0:T(8,128)(2,1)} %get-tuple-element.96.near_ref.far_ref, ...), custom_call_target="tpu_custom_call" | custom-call | flops 536870912 | bytes 1048576 | tf_op jit(solution)/shard_map/down_grad/pallas_call | solution.py:432
  327.6 1.5 copy-done.40
  329.0 8.6 %settle.13 = (bf16[8,128,1280]{2,1,0:T(8,128)(2,1)}, bf16[8,128,1280]{2,1,0:T(8,128)(2,1)}) custom-call(s32[1]{0:T(128)} %bitcast.33.side_ref, bf16[16,128,1280]{2,1,0:T(8,128)(2,1)} %bitcast.139, bf16[16,128,1280]{2,1,0:T(8,128)(2,1)} %bitcast.140, bf16[8,128,1280]{2,1,0:T(8,128)(2,1)} %collective-permute-done.9.low_ref, bf16[8,128,1280]{2,1,0:T(8,128)(2,1)} %copy-done.40, ...), custom_call_target="tpu_custom_call" | custom-call | bytes 983040 | tf_op jit(solution)/shard_map/settle/pallas_call | solution.py:736
  337.6 1.4 collective-permute-start.13
  339.1 6.1 %settle.14 = (bf16[4,512,512]{2,1,0:T(8,128)(2,1)}, bf16[4,512,512]{2,1,0:T(8,128)(2,1)}) custom-call(s32[1]{0:T(128)} %bitcast.28.side_ref, bf16[8,512,512]{2,1,0:T(8,128)(2,1)} %bitcast.166, bf16[8,512,512]{2,1,0:T(8,128)(2,1)} %bitcast.167, bf16[4,512,512]{2,1,0:T(8,128)(2,1)} %collective-permute-done.7.low_ref, ...), custom_call_target="tpu_custom_call" | custom-call | bytes 786432 | tf_op jit(solution)/shard_map/settle/pallas_call | solution.py:736
  345.9 1.6 copy-done.23
  349.1 11.9 %attend_backward.4 = (bf16[4,2,128,1024]{3,2,1,0:T(8,128)(2,1)}, bf16[4,2,128,1024]{3,2,1,0:T(8,128)(2,1)}, bf16[4,2,128,1024]{3,2,1,0:T(8,128)(2,1)}, f32[16,10...) custom-call(bf16[4,2,128,1024]{3,2,1,0:T(8,128)(2,1)} %bitcast.151, bf16[4,2,128,1024]{3,2,1,0:T(8,128)(2,1)} %bitcast.156, ...), custom_call_target="tpu_custom_call" | custom-call | flops 335544320 | bytes 458752 | tf_op jit(solution)/shard_map/attend_backward/pallas_call | solution.py:204
  361.0 11.8 %attend_backward.5 = (bf16[4,2,128,1024]{3,2,1,0:T(8,128)(2,1)}, bf16[4,2,128,1024]{3,2,1,0:T(8,128)(2,1)}, bf16[4,2,128,1024]{3,2,1,0:T(8,128)(2,1)}, f32[16,10...) custom-call(bf16[4,2,128,1024]{3,2,1,0:T(8,128)(2,1)} %bitcast.152, ...), custom_call_target="tpu_custom_call", output_to_operand_aliasing={{0}: (4, {}), {1}: (5, {}), {2}: (6, {}), {3}: (7, {}), {4}... | custom-call | flops 335544320 | bytes 458752 | tf_op jit(solution)/shard_map/attend_backward/pallas_call | solution.py:204
  372.9 11.8 %attend_backward.6 = (bf16[4,2,128,1024]{3,2,1,0:T(8,128)(2,1)}, bf16[4,2,128,1024]{3,2,1,0:T(8,128)(2,1)}, bf16[4,2,128,1024]{3,2,1,0:T(8,128)(2,1)}, f32[16,10...) custom-call(bf16[4,2,128,1024]{3,2,1,0:T(8,128)(2,1)} %bitcast.153, ...), custom_call_target="tpu_custom_call", output_to_operand_aliasing={{0}: (4, {}), {1}: (5, {}), {2}: (6, {}), {3}: (7, {}), {4}... | custom-call | flops 335544320 | bytes 458752 | tf_op jit(solution)/shard_map/attend_backward/pallas_call | solution.py:204
  384.7 11.8 %attend_backward.7 = (bf16[4,2,128,1024]{3,2,1,0:T(8,128)(2,1)}, bf16[4,2,128,1024]{3,2,1,0:T(8,128)(2,1)}, bf16[4,2,128,1024]{3,2,1,0:T(8,128)(2,1)}, f32[16,10...) custom-call(bf16[4,2,128,1024]{3,2,1,0:T(8,128)(2,1)} %bitcast.154, ...), custom_call_target="tpu_custom_call", output_to_operand_aliasing={{0}: (4, {}), {1}: (5, {}), {2}: (6, {}), {3}: (7, {}), {4}... | custom-call | flops 335544320 | bytes 458752 | tf_op jit(solution)/shard_map/attend_backward/pallas_call | solution.py:204
  397.0 1.7 copy-done.11
  399.4 2.9 settle.15
  402.3 3.0 settle.16
  408.2 1.5 collective-permute-start.15
  410.0 12.8 %tokens_grad.1.refs_2_ = bf16[1024,1024]{1,0:T(8,128)(2,1)} custom-call(f32[1024,1024]{1,0:T(8,128)} %get-tuple-element.141.d_pre_ref, bf16[1024,1024]{1,0:T(8,128)(2,1)} %bitcast.141, bf16[1024,1024]{1,0:T(8,128)(2,1)} %bitcast.144, bf16[1024,1024]{1,0:T(8,128)(2,1)} %bitcast.147, bf16[32,128,768]{2,1,0:T(8,128)(2,1)} %bitcast.173, ...), custom_call_target="tpu_custom_call" | custom-call | flops 402653184 | bytes 1179648 | tf_op jit(solution)/shard_map/tokens_grad/pallas_call | solution.py:655
  422.8 1.6 copy-done.2
  424.4 1.6 pick.15.refs_6_
  426.0 13.8 %input_grad.1 = (bf16[4,272,512]{2,1,0:T(8,128)(2,1)}, bf16[4,272,512]{2,1,0:T(8,128)(2,1)}, bf16[8,128,512]{2,1,0:T(8,128)(2,1)}, bf16[8,272,512]{2,1,0:T(8,128)(2,1)}, bf16[8,128,512]{2,1,0:T(8,128)(2,1)}) custom-call(s32[1]{0:T(128)} %bitcast.1.half_ref, bf16[1024,1024]{1,0:T(8,128)(2,1)} %bitcast.120, bf16[1024,1024]{1,0:T(8,128)(2,1)} %bitcast.142, ...), custom_call_target="tpu_custom_call" | custom-call | flops 402653184 | bytes 655360 | tf_op jit(solution)/shard_map/input_grad/pallas_call | solution.py:613
  442.8 1.6 settle.17
  444.4 1.9 collective-permute-start.17
  446.4 1.6 settle.18
  448.3 1.7 pick.16.refs_0_
  450.1 2.7 settle.19
  454.8 1.5 collective-permute-start.16
  456.3 2.2 settle.20
  458.5 8.3 %collective-permute-done.17.low_ref.high_ref = bf16[2,128,1280]{2,1,0:T(8,128)(2,1)S(1)} collective-permute-done((bf16[2,128,1280]{2,1,0:T(8,128)(2,1)S(1)}, bf16[2,128,1280]{2,1,0:T(8,128)(2,1)S(1)}, u32[]{:S(2)}, u32[]{:S(2)}) %collective-permute-start.17) | collective-permute-done | bytes 655392 | tf_op jit(solution)/shard_map/ppermute | solution.py:670
  466.9 13.6 %collective-permute-done.16.right_ref = bf16[1,512,512]{2,1,0:T(8,128)(2,1)S(1)} collective-permute-done((bf16[1,512,512]{2,1,0:T(8,128)(2,1)S(1)}, bf16[1,512,512]{2,1,0:T(8,128)(2,1)S(1)}, u32[]{:S(2)}, u32[]{:S(2)}) %collective-permute-start.16) | collective-permute-done | bytes 524320 | tf_op jit(solution)/shard_map/ppermute | solution.py:670
  481.3 1.7 pick.17.refs_0_
  484.0 5.3 collective-permute-done.23.low_ref.high_ref
  489.5 3.5 pick.18.refs_0_
  493.0 3.7 collective-permute-done.28.right_ref
  496.7 1.6 copy-done.14
  499.1 1.4 collective-permute-start.22
  503.2 6.1 %collective-permute-done.36 = bf16[128,1280]{1,0:T(8,128)(2,1)} collective-permute-done((bf16[128,1280]{1,0:T(8,128)(2,1)S(1)}, bf16[128,1280]{1,0:T(8,128)(2,1)}, u32[]{:S(2)}, u32[]{:S(2)}) %collective-permute-start.36) | collective-permute-done | bytes 327712 | tf_op jit(solution)/shard_map/ppermute | solution.py:670
  513.7 1.8 settle.24
  517.8 1.7 collective-permute-start.32
  520.6 1.6 convert_bitcast_fusion
  522.2 2.9 copy.54
  525.1 3.4 collective-permute-done.22.refs_2_.refs_3_
  528.5 3.8 pick.19.refs_0_
  533.5 1.6 copy-done.15
  536.8 1.5 collective-permute-start.34
  539.7 6.0 %collective-permute-done.31.right_ref = bf16[1,272,512]{2,1,0:T(8,128)(2,1)S(1)} collective-permute-done((bf16[1,272,512]{2,1,0:T(8,128)(2,1)S(1)}, bf16[1,272,512]{2,1,0:T(8,128)(2,1)S(1)}, u32[]{:S(2)}, u32[]{:S(2)}) %collective-permute-start.31) | collective-permute-done | bytes 278560 | tf_op jit(solution)/shard_map/ppermute | solution.py:670
  545.8 1.5 maximum_convert_fusion
  (247 shorter events, 45.9 us)
Async XLA Ops:
  7.2 4.7 copy-start.51
  7.2 4.7 copy-start.52
  7.2 4.7 copy-start.53
  7.2 4.7 copy-start.47
  7.2 4.7 copy-start.45
  7.2 4.7 copy-start.48
  7.3 4.7 copy-start.49
  7.3 4.7 copy-start.50
  7.3 4.7 copy-start.46
  7.3 11.6 %copy-start.7 = (bf16[8,128,1024]{2,1,0:T(8,128)(2,1)S(1)}, bf16[8,128,1024]{2,1,0:T(8,128)(2,1)}, u32[]{:S(2)}) copy-start(bf16[8,128,1024]{2,1,0:T(8,128)(2,1)} %param.15) | copy-start | bytes 6291460
  7.3 91.5 %all-gather.5.cloned.1.call-start = ((), (), s32[]{:S(2)}) async-start(), calls=%async_computation | async-start | bytes 6488064 | tf_op jit(solution)/shard_map/all_gather | solution.py:904
  9.0 215.4 %all-gather.7.cloned.1.call-start = ((), (), s32[]{:S(2)}) async-start(), calls=%async_computation.1 | async-start | bytes 19464192 | tf_op jit(solution)/shard_map/all_gather | solution.py:905
  12.1 4.6 collective-permute-start.1
  16.7 4.7 collective-permute-start.2
  19.9 29.5 %collective-permute-start = (bf16[2,2,128,1024]{3,2,1,0:T(8,128)(2,1)}, bf16[2,2,128,1024]{3,2,1,0:T(8,128)(2,1)}, u32[]{:S(2)}, u32[]{:S(2)}) collective-permute-start(bf16[2,2,128,1024]{3,2,1,0:T(8,128)(2,1)} %constant_dynamic-slice_fusion.5), channel_id=1, source_target_pairs={{0,16},{8,24},{16,0},{24,8},{1,17},{9,25},{17,1},{25,9},{2,18},{10... | collective-permute-start | bytes 3145736 | tf_op jit(solution)/shard_map/ppermute | solution.py:670
  21.5 4.7 collective-permute-start.3
  52.2 3.6 collective-permute-start.4
  53.2 37.9 %collective-permute-start.5 = (bf16[2,2,128,1024]{3,2,1,0:T(8,128)(2,1)}, bf16[2,2,128,1024]{3,2,1,0:T(8,128)(2,1)}, u32[]{:S(2)}, u32[]{:S(2)}) collective-permute-start(bf16[2,2,128,1024]{3,2,1,0:T(8,128)(2,1)} %constant_dynamic-slice_fusion.3), channel_id=1, source_target_pairs={{0,16},{8,24},{16,0},{24,8},{1,17},{9,25},{17,1},{25,9},{2,18},{10... | collective-permute-start | bytes 3145736 | tf_op jit(solution)/shard_map/ppermute | solution.py:670
  57.4 33.7 %copy-start.10 = (bf16[8,128,1024]{2,1,0:T(8,128)(2,1)S(1)}, bf16[8,128,1024]{2,1,0:T(8,128)(2,1)}, u32[]{:S(2)}) copy-start(bf16[8,128,1024]{2,1,0:T(8,128)(2,1)} %param.16) | copy-start | bytes 6291460
  59.3 33.5 %copy-start.4 = (bf16[4,2,128,1024]{3,2,1,0:T(8,128)(2,1)}, bf16[4,2,128,1024]{3,2,1,0:T(8,128)(2,1)S(1)}, u32[]{:S(2)}) copy-start(bf16[4,2,128,1024]{3,2,1,0:T(8,128)(2,1)S(1)} %pick.11.refs_2_) | copy-start | bytes 6291460
  92.8 2.8 collective-permute-start.6
  312.9 14.7 %collective-permute-start.10 = (bf16[8,128,1280]{2,1,0:T(8,128)(2,1)}, bf16[8,128,1280]{2,1,0:T(8,128)(2,1)S(1)}, u32[]{:S(2)}, u32[]{:S(2)}) collective-permute-start(bf16[8,128,1280]{2,1,0:T(8,128)(2,1)} %bitcast.178), channel_id=1, source_target_pairs={{0,8},{8,0},{16,24},{24,16},{1,9},{9,1},{17,25},{25,17},{2,10},{10... | collective-permute-start | bytes 7864328 | tf_op jit(solution)/shard_map/ppermute | solution.py:670
  313.1 14.4 %collective-permute-start.9 = (bf16[8,128,1280]{2,1,0:T(8,128)(2,1)}, bf16[8,128,1280]{2,1,0:T(8,128)(2,1)}, u32[]{:S(2)}, u32[]{:S(2)}) collective-permute-start(bf16[8,128,1280]{2,1,0:T(8,128)(2,1)} %bitcast.177), channel_id=1, source_target_pairs={{0,8},{8,0},{16,24},{24,16},{1,9},{9,1},{17,25},{25,17},{2,10},{10... | collective-permute-start | bytes 7864328 | tf_op jit(solution)/shard_map/ppermute | solution.py:670
  327.0 12.0 %collective-permute-start.7 = (bf16[4,512,512]{2,1,0:T(8,128)(2,1)}, bf16[4,512,512]{2,1,0:T(8,128)(2,1)}, u32[]{:S(2)}, u32[]{:S(2)}) collective-permute-start(bf16[4,512,512]{2,1,0:T(8,128)(2,1)} %bitcast.204), channel_id=1, source_target_pairs={{0,8},{8,0},{16,24},{24,16},{1,9},{9,1},{17,25},{25,17},{2,10},{10... | collective-permute-start | bytes 6291464 | tf_op jit(solution)/shard_map/ppermute | solution.py:670
  327.3 11.7 %collective-permute-start.8 = (bf16[4,512,512]{2,1,0:T(8,128)(2,1)}, bf16[4,512,512]{2,1,0:T(8,128)(2,1)}, u32[]{:S(2)}, u32[]{:S(2)}) collective-permute-start(bf16[4,512,512]{2,1,0:T(8,128)(2,1)} %bitcast.203), channel_id=1, source_target_pairs={{0,8},{8,0},{16,24},{24,16},{1,9},{9,1},{17,25},{25,17},{2,10},{10... | collective-permute-start | bytes 6291464 | tf_op jit(solution)/shard_map/ppermute | solution.py:670
  337.6 59.4 %collective-permute-start.13 = (bf16[8,128,1280]{2,1,0:T(8,128)(2,1)}, bf16[8,128,1280]{2,1,0:T(8,128)(2,1)}, u32[]{:S(2)}, u32[]{:S(2)}) collective-permute-start(bf16[8,128,1280]{2,1,0:T(8,128)(2,1)} %get-tuple-element.110.refs_0_), channel_id=1, source_target_pairs={{0,16},{8,24},{16,0},{24,8},{1,17},{9,25},{17,1},{25,9},{2,18},{10... | collective-permute-start | bytes 7864328 | tf_op jit(solution)/shard_map/ppermute | solution.py:670
  339.0 6.8 %copy-start.44 = (f32[8,1024]{1,0:T(8,128)S(1)}, f32[8,1024]{1,0:T(8,128)}, u32[]{:S(2)}) copy-start(f32[8,1024]{1,0:T(8,128)} %get-tuple-element.151) | copy-start | bytes 98308
  339.0 6.8 %copy-start.5 = (bf16[1024,1024]{1,0:T(8,128)(2,1)S(1)}, bf16[1024,1024]{1,0:T(8,128)(2,1)}, u32[]{:S(2)}) copy-start(bf16[1024,1024]{1,0:T(8,128)(2,1)} %get-tuple-element.95) | copy-start | bytes 6291460
  339.1 6.8 %copy-start.35 = (s32[2]{0:T(128)S(1)}, s32[2]{0:T(128)}, u32[]{:S(2)}) copy-start(s32[2]{0:T(128)} %constant.201.clone.1.pick_ref) | copy-start | bytes 28
  345.2 57.1 %collective-permute-start.12 = (bf16[4,512,512]{2,1,0:T(8,128)(2,1)}, bf16[4,512,512]{2,1,0:T(8,128)(2,1)}, u32[]{:S(2)}, u32[]{:S(2)}) collective-permute-start(bf16[4,512,512]{2,1,0:T(8,128)(2,1)} %get-tuple-element.111.refs_2_), channel_id=1, source_target_pairs={{0,1},{1,0},{2,3},{3,2},{4,5},{5,4},{6,7},{7,6},{8,9},{9,8},{10,11... | collective-permute-start | bytes 6291464 | tf_op jit(solution)/shard_map/ppermute | solution.py:670
  406.3 34.7 %collective-permute-start.14 = (bf16[2,512,512]{2,1,0:T(8,128)(2,1)}, bf16[2,512,512]{2,1,0:T(8,128)(2,1)}, u32[]{:S(2)}, u32[]{:S(2)}) collective-permute-start(bf16[2,512,512]{2,1,0:T(8,128)(2,1)} %get-tuple-element.136.refs_0_), channel_id=1, source_target_pairs={{0,2},{1,3},{2,0},{3,1},{4,6},{5,7},{6,4},{7,5},{8,10},{9,11},{10,... | collective-permute-start | bytes 3145736 | tf_op jit(solution)/shard_map/ppermute | solution.py:670
  408.2 33.3 %collective-permute-start.15 = (bf16[4,128,1280]{2,1,0:T(8,128)(2,1)}, bf16[4,128,1280]{2,1,0:T(8,128)(2,1)}, u32[]{:S(2)}, u32[]{:S(2)}) collective-permute-start(bf16[4,128,1280]{2,1,0:T(8,128)(2,1)} %copy-done.24), channel_id=1, source_target_pairs={{0,1},{1,0},{2,3},{3,2},{4,5},{5,4},{6,7},{7,6},{8,9},{9,8},{10,11... | collective-permute-start | bytes 3932168 | tf_op jit(solution)/shard_map/ppermute | solution.py:670
  410.0 29.9 %copy-start.41 = (bf16[1,8,32,512]{3,2,1,0:T(8,128)(2,1)}, bf16[1,8,32,512]{3,2,1,0:T(8,128)(2,1)S(1)}, u32[]{:S(2)}) copy-start(bf16[1,8,32,512]{3,2,1,0:T(8,128)(2,1)S(1)} %copy.59) | copy-start | bytes 786436
  426.0 18.4 %collective-permute-start.21 = (bf16[2,2,128,1024]{3,2,1,0:T(8,128)(2,1)}, bf16[2,2,128,1024]{3,2,1,0:T(8,128)(2,1)}, u32[]{:S(2)}, u32[]{:S(2)}) collective-permute-start(bf16[2,2,128,1024]{3,2,1,0:T(8,128)(2,1)} %pick.15.refs_6_), channel_id=1, source_target_pairs={{0,8},{8,0},{16,24},{24,16},{1,9},{9,1},{17,25},{25,17},{2,10},{10... | collective-permute-start | bytes 3145736 | tf_op jit(solution)/shard_map/ppermute | solution.py:670
  440.5 9.5 %collective-permute-start.19 = (bf16[4,272,512]{2,1,0:T(8,128)(2,1)}, bf16[4,272,512]{2,1,0:T(8,128)(2,1)}, u32[]{:S(2)}, u32[]{:S(2)}) collective-permute-start(bf16[4,272,512]{2,1,0:T(8,128)(2,1)} %get-tuple-element.212), channel_id=1, source_target_pairs={{0,8},{8,0},{16,24},{24,16},{1,9},{9,1},{17,25},{25,17},{2,10},{10... | collective-permute-start | bytes 3342344 | tf_op jit(solution)/shard_map/ppermute | solution.py:670
  441.0 9.1 %collective-permute-start.20 = (bf16[4,272,512]{2,1,0:T(8,128)(2,1)}, bf16[4,272,512]{2,1,0:T(8,128)(2,1)}, u32[]{:S(2)}, u32[]{:S(2)}) collective-permute-start(bf16[4,272,512]{2,1,0:T(8,128)(2,1)} %get-tuple-element.211), channel_id=1, source_target_pairs={{0,8},{8,0},{16,24},{24,16},{1,9},{9,1},{17,25},{25,17},{2,10},{10... | collective-permute-start | bytes 3342344 | tf_op jit(solution)/shard_map/ppermute | solution.py:670
  441.0 13.7 %collective-permute-start.18 = (bf16[8,128,512]{2,1,0:T(8,128)(2,1)}, bf16[8,128,512]{2,1,0:T(8,128)(2,1)}, u32[]{:S(2)}, u32[]{:S(2)}) collective-permute-start(bf16[8,128,512]{2,1,0:T(8,128)(2,1)} %get-tuple-element.142.refs_0_), channel_id=1, source_target_pairs={{0,8},{8,0},{16,24},{24,16},{1,9},{9,1},{17,25},{25,17},{2,10},{10... | collective-permute-start | bytes 3145736 | tf_op jit(solution)/shard_map/ppermute | solution.py:670
  441.5 39.1 %collective-permute-start.11 = (bf16[2,2,128,1024]{3,2,1,0:T(8,128)(2,1)}, bf16[2,2,128,1024]{3,2,1,0:T(8,128)(2,1)}, u32[]{:S(2)}, u32[]{:S(2)}) collective-permute-start(bf16[2,2,128,1024]{3,2,1,0:T(8,128)(2,1)} %copy-done.18), channel_id=1, source_target_pairs={{0,8},{8,0},{16,24},{24,16},{1,9},{9,1},{17,25},{25,17},{2,10},{10... | collective-permute-start | bytes 3145736 | tf_op jit(solution)/shard_map/ppermute | solution.py:670
  444.4 22.3 %collective-permute-start.17 = (bf16[2,128,1280]{2,1,0:T(8,128)(2,1)S(1)}, bf16[2,128,1280]{2,1,0:T(8,128)(2,1)S(1)}, u32[]{:S(2)}, u32[]{:S(2)}) collective-permute-start(bf16[2,128,1280]{2,1,0:T(8,128)(2,1)S(1)} %get-tuple-element.143.refs_0_), channel_id=1, source_target_pairs={{0,2},{1,3},{2,0},{3,1},{4,6},{5,7},{6,4},{7,5},{8,10},{9,11},{10,... | collective-permute-start | bytes 1966088 | tf_op jit(solution)/shard_map/ppermute | solution.py:670
  450.0 6.2 %copy-start.20 = (bf16[8,128,512]{2,1,0:T(8,128)(2,1)S(1)}, bf16[8,128,512]{2,1,0:T(8,128)(2,1)}, u32[]{:S(2)}) copy-start(bf16[8,128,512]{2,1,0:T(8,128)(2,1)} %get-tuple-element.147.keep_ref.keep_far) | copy-start | bytes 3145732
  452.7 30.3 %collective-permute-start.24 = (bf16[4,272,512]{2,1,0:T(8,128)(2,1)S(1)}, bf16[4,272,512]{2,1,0:T(8,128)(2,1)S(1)}, u32[]{:S(2)}, u32[]{:S(2)}) collective-permute-start(bf16[4,272,512]{2,1,0:T(8,128)(2,1)S(1)} %get-tuple-element.155.refs_0_), channel_id=1, source_target_pairs={{0,1},{1,0},{2,3},{3,2},{4,5},{5,4},{6,7},{7,6},{8,9},{9,8},{10,11... | collective-permute-start | bytes 3342344 | tf_op jit(solution)/shard_map/ppermute | solution.py:670
  453.4 36.2 %collective-permute-start.29 = (bf16[2,2,128,1024]{3,2,1,0:T(8,128)(2,1)S(1)}, bf16[2,2,128,1024]{3,2,1,0:T(8,128)(2,1)S(1)}, u32[]{:S(2)}, u32[]{:S(2)}) collective-permute-start(bf16[2,2,128,1024]{3,2,1,0:T(8,128)(2,1)S(1)} %pick.16.refs_0_), channel_id=1, source_target_pairs={{0,16},{8,24},{16,0},{24,8},{1,17},{9,25},{17,1},{25,9},{2,18},{10... | collective-permute-start | bytes 3145736 | tf_op jit(solution)/shard_map/ppermute | solution.py:670
  454.8 25.7 %collective-permute-start.16 = (bf16[1,512,512]{2,1,0:T(8,128)(2,1)S(1)}, bf16[1,512,512]{2,1,0:T(8,128)(2,1)S(1)}, u32[]{:S(2)}, u32[]{:S(2)}) collective-permute-start(bf16[1,512,512]{2,1,0:T(8,128)(2,1)S(1)} %get-tuple-element.145.refs_2_), channel_id=1, source_target_pairs={{0,4},{1,5},{2,6},{3,7},{4,0},{5,1},{6,2},{7,3},{8,12},{9,13},{10,... | collective-permute-start | bytes 1572872 | tf_op jit(solution)/shard_map/ppermute | solution.py:670
  466.8 22.6 %collective-permute-start.23 = (bf16[4,128,512]{2,1,0:T(8,128)(2,1)S(1)}, bf16[4,128,512]{2,1,0:T(8,128)(2,1)S(1)}, u32[]{:S(2)}, u32[]{:S(2)}) collective-permute-start(bf16[4,128,512]{2,1,0:T(8,128)(2,1)S(1)} %get-tuple-element.156.refs_0_), channel_id=1, source_target_pairs={{0,2},{1,3},{2,0},{3,1},{4,6},{5,7},{6,4},{7,5},{8,10},{9,11},{10,... | collective-permute-start | bytes 1572872 | tf_op jit(solution)/shard_map/ppermute | solution.py:670
  480.5 16.3 %collective-permute-start.28 = (bf16[1,128,1280]{2,1,0:T(8,128)(2,1)S(1)}, bf16[1,128,1280]{2,1,0:T(8,128)(2,1)S(1)}, u32[]{:S(2)}, u32[]{:S(2)}) collective-permute-start(bf16[1,128,1280]{2,1,0:T(8,128)(2,1)S(1)} %get-tuple-element.157.refs_0_), channel_id=1, source_target_pairs={{0,4},{1,5},{2,6},{3,7},{4,0},{5,1},{6,2},{7,3},{8,12},{9,13},{10,... | collective-permute-start | bytes 983048 | tf_op jit(solution)/shard_map/ppermute | solution.py:670
  480.6 20.5 %collective-permute-start.27 = (bf16[1,512,512]{2,1,0:T(8,128)(2,1)S(1)}, bf16[1,512,512]{2,1,0:T(8,128)(2,1)S(1)}, u32[]{:S(2)}, u32[]{:S(2)}) collective-permute-start(bf16[1,512,512]{2,1,0:T(8,128)(2,1)S(1)} %plus.7.refs_2_.left_ref), channel_id=1, source_target_pairs={{0,16},{8,24},{16,0},{24,8},{1,17},{9,25},{17,1},{25,9},{2,18},{10... | collective-permute-start | bytes 1572872 | tf_op jit(solution)/shard_map/ppermute | solution.py:670
  484.0 9.0 %copy-start.21 = (bf16[2,272,512]{2,1,0:T(8,128)(2,1)}, bf16[2,272,512]{2,1,0:T(8,128)(2,1)S(1)}, u32[]{:S(2)}) copy-start(bf16[2,272,512]{2,1,0:T(8,128)(2,1)S(1)} %get-tuple-element.163.keep_ref.keep_far) | copy-start | bytes 1671172
  484.0 9.0 %copy-start.28 = (bf16[2,272,512]{2,1,0:T(8,128)(2,1)}, bf16[2,272,512]{2,1,0:T(8,128)(2,1)S(1)}, u32[]{:S(2)}) copy-start(bf16[2,272,512]{2,1,0:T(8,128)(2,1)S(1)} %get-tuple-element.160.refs_0_) | copy-start | bytes 1671172
  484.0 5.5 copy-start.33
  498.4 10.8 %collective-permute-start.36 = (bf16[128,1280]{1,0:T(8,128)(2,1)S(1)}, bf16[128,1280]{1,0:T(8,128)(2,1)}, u32[]{:S(2)}, u32[]{:S(2)}) collective-permute-start(bf16[128,1280]{1,0:T(8,128)(2,1)S(1)} %bitcast.135), channel_id=1, source_target_pairs={{0,16},{8,24},{16,0},{24,8},{1,17},{9,25},{17,1},{25,9},{2,18},{10... | collective-permute-start | bytes 983048 | tf_op jit(solution)/shard_map/ppermute | solution.py:670
  499.1 29.4 %collective-permute-start.22 = (bf16[2,2,128,1024]{3,2,1,0:T(8,128)(2,1)}, bf16[2,2,128,1024]{3,2,1,0:T(8,128)(2,1)}, u32[]{:S(2)}, u32[]{:S(2)}) collective-permute-start(bf16[2,2,128,1024]{3,2,1,0:T(8,128)(2,1)} %copy-done.19), channel_id=1, source_target_pairs={{0,16},{8,24},{16,0},{24,8},{1,17},{9,25},{17,1},{25,9},{2,18},{10... | collective-permute-start | bytes 3145736 | tf_op jit(solution)/shard_map/ppermute | solution.py:670
  500.5 12.1 %collective-permute-start.26 = (bf16[2,272,512]{2,1,0:T(8,128)(2,1)}, bf16[2,272,512]{2,1,0:T(8,128)(2,1)}, u32[]{:S(2)}, u32[]{:S(2)}) collective-permute-start(bf16[2,272,512]{2,1,0:T(8,128)(2,1)} %copy-done.28), channel_id=1, source_target_pairs={{0,2},{1,3},{2,0},{3,1},{4,6},{5,7},{6,4},{7,5},{8,10},{9,11},{10,... | collective-permute-start | bytes 1671176 | tf_op jit(solution)/shard_map/ppermute | solution.py:670
  500.5 16.3 %collective-permute-start.25 = (bf16[2,128,512]{2,1,0:T(8,128)(2,1)}, bf16[2,128,512]{2,1,0:T(8,128)(2,1)}, u32[]{:S(2)}, u32[]{:S(2)}) collective-permute-start(bf16[2,128,512]{2,1,0:T(8,128)(2,1)} %copy-done.31), channel_id=1, source_target_pairs={{0,1},{1,0},{2,3},{3,2},{4,5},{5,4},{6,7},{7,6},{8,9},{9,8},{10,11... | collective-permute-start | bytes 786440 | tf_op jit(solution)/shard_map/ppermute | solution.py:670
  503.1 16.4 %collective-permute-start.38 = (bf16[512,512]{1,0:T(8,128)(2,1)S(1)}, bf16[512,512]{1,0:T(8,128)(2,1)}, u32[]{:S(2)}, u32[]{:S(2)}) collective-permute-start(bf16[512,512]{1,0:T(8,128)(2,1)S(1)} %bitcast.134), channel_id=1, source_target_pairs={{0,8},{8,0},{16,24},{24,16},{1,9},{9,1},{17,25},{25,17},{2,10},{10... | collective-permute-start | bytes 1572872 | tf_op jit(solution)/shard_map/ppermute | solution.py:670
  510.3 6.5 %copy-start.27 = (bf16[2,128,512]{2,1,0:T(8,128)(2,1)S(1)}, bf16[2,128,512]{2,1,0:T(8,128)(2,1)}, u32[]{:S(2)}) copy-start(bf16[2,128,512]{2,1,0:T(8,128)(2,1)} %copy-done.26) | copy-start | bytes 786436
  511.9 26.4 %collective-permute-start.37 = (bf16[2,128,1280]{2,1,0:T(8,128)(2,1)}, bf16[2,128,1280]{2,1,0:T(8,128)(2,1)}, u32[]{:S(2)}, u32[]{:S(2)}) collective-permute-start(bf16[2,128,1280]{2,1,0:T(8,128)(2,1)} %pad_maximum_fusion), channel_id=1, source_target_pairs={{0,8},{8,0},{16,24},{24,16},{1,9},{9,1},{17,25},{25,17},{2,10},{10... | collective-permute-start | bytes 1966088 | tf_op jit(solution)/shard_map/ppermute | solution.py:670
  515.5 18.0 %collective-permute-start.30 = (bf16[1,272,512]{2,1,0:T(8,128)(2,1)}, bf16[1,272,512]{2,1,0:T(8,128)(2,1)}, u32[]{:S(2)}, u32[]{:S(2)}) collective-permute-start(bf16[1,272,512]{2,1,0:T(8,128)(2,1)} %get-tuple-element.165.refs_0_), channel_id=1, source_target_pairs={{0,4},{1,5},{2,6},{3,7},{4,0},{5,1},{6,2},{7,3},{8,12},{9,13},{10,... | collective-permute-start | bytes 835592 | tf_op jit(solution)/shard_map/ppermute | solution.py:670
  517.8 18.9 %collective-permute-start.32 = (bf16[1,128,512]{2,1,0:T(8,128)(2,1)S(1)}, bf16[1,128,512]{2,1,0:T(8,128)(2,1)S(1)}, u32[]{:S(2)}, u32[]{:S(2)}) collective-permute-start(bf16[1,128,512]{2,1,0:T(8,128)(2,1)S(1)} %get-tuple-element.166.refs_4_), channel_id=1, source_target_pairs={{0,4},{1,5},{2,6},{3,7},{4,0},{5,1},{6,2},{7,3},{8,12},{9,13},{10,... | collective-permute-start | bytes 393224 | tf_op jit(solution)/shard_map/ppermute | solution.py:670
  528.5 9.8 %copy-start.37 = (bf16[1,128,1280]{2,1,0:T(8,128)(2,1)S(1)}, bf16[1,128,1280]{2,1,0:T(8,128)(2,1)}, u32[]{:S(2)}) copy-start(bf16[1,128,1280]{2,1,0:T(8,128)(2,1)} %copy-done.36) | copy-start | bytes 983044
  528.5 9.8 %copy-start.39 = (bf16[1,128,1280]{2,1,0:T(8,128)(2,1)S(1)}, bf16[1,128,1280]{2,1,0:T(8,128)(2,1)}, u32[]{:S(2)}) copy-start(bf16[1,128,1280]{2,1,0:T(8,128)(2,1)} %copy-done.38) | copy-start | bytes 983044
  536.1 9.6 %collective-permute-start.31 = (bf16[1,272,512]{2,1,0:T(8,128)(2,1)S(1)}, bf16[1,272,512]{2,1,0:T(8,128)(2,1)S(1)}, u32[]{:S(2)}, u32[]{:S(2)}) collective-permute-start(bf16[1,272,512]{2,1,0:T(8,128)(2,1)S(1)} %plus.10.refs_0_.left_ref), channel_id=1, source_target_pairs={{0,16},{8,24},{16,0},{24,8},{1,17},{9,25},{17,1},{25,9},{2,18},{10... | collective-permute-start | bytes 835592 | tf_op jit(solution)/shard_map/ppermute | solution.py:670
  536.8 11.5 %collective-permute-start.34 = (bf16[1,128,512]{2,1,0:T(8,128)(2,1)S(1)}, bf16[1,128,512]{2,1,0:T(8,128)(2,1)S(1)}, u32[]{:S(2)}, u32[]{:S(2)}) collective-permute-start(bf16[1,128,512]{2,1,0:T(8,128)(2,1)S(1)} %plus.11.refs_0_.left_ref), channel_id=1, source_target_pairs={{0,16},{8,24},{16,0},{24,8},{1,17},{9,25},{17,1},{25,9},{2,18},{10... | collective-permute-start | bytes 393224 | tf_op jit(solution)/shard_map/ppermute | solution.py:670
  545.8 3.1 collective-permute-start.33
  548.3 1.8 collective-permute-start.35
  (31 other events, 60.7 us)
Sparse Core Ops, SparseCore 0:
  11.6 86.3 all-gather.4
  100.8 123.5 all-gather.6
